TPU v7x, 32 devices: a whole 2x2x4 slice. The times are simulated.
32 devices in a mesh: pole: 2 (over y), prow: 4 (over z), pcol: 4 (over x, core).
Axes of the slice: x: 2, y: 2, z: 4, core: 2. Of those that a mesh axis runs over, the one named last changes fastest.
Arguments:
- inverse_block: bfloat16 [2, 4096, 2048], P(None, ('pole', 'prow'), 'pcol'), parts along dimension 1, may hold values from -6 to 6
- factor_column: bfloat16 [4096, 2, 1024], P(('pole', 'prow')), parts along dimension 0, may hold values from -0.125 to 0.125
- block_pattern: int32 [4, 16], P('pole', 'prow'), parts along dimension 0, may hold values 0 or 1
- pivot_inverse: float32 [4, 2, 512, 512], P('pole'), parts along dimension 0, may hold values from -6 to 6
Outputs:
- selected_column: float32 [4096, 2, 1024], P(('pole', 'prow', 'pcol')), parts along dimension 0
- selected_pivot: float32 [4, 2, 512, 512], P('pole'), parts along dimension 0
There are 2 independent parts, one for each index of `pole`. A program takes and returns all parts, laid end to end along the dimension named above; each array names one. Nothing has to cross between parts.
All inputs are finite; a program needn't handle non-finite values. No bound on the sum of `block_pattern` on one device may be relied on, other than what follows from the above.
Results may differ from a plain program's by a relative error of at most 0.0025.
Values may be sent and summed in bfloat16 or wider, within the bound.
No kernel may reach another device: no remote copies, remote signals or barrier semaphores. Data moves between devices by JAX's collectives and lax.ppermute only.
A program may use at most 64 MiB of HBM per device.

v0:
```python
import jax
import jax.numpy as jnp
from jax import lax
from jax.sharding import PartitionSpec as P

S = 512
BLK = 128


def from_root(block, axis, holder):
    block = jnp.where(lax.axis_index(axis) == holder, block, jnp.zeros_like(block))
    return lax.psum(block, axis)


def expand_pattern(block_pattern):
    blocks = block_pattern.shape[1]
    keep_rows = block_pattern.T.astype(jnp.bfloat16)
    keep_rows = jnp.broadcast_to(keep_rows[:, None, :, None], (blocks, BLK, 2, S))
    return keep_rows.reshape(blocks * BLK, 1, 2 * S)


def complex_column(inverse_real, inverse_imag, factor):
    row_total = inverse_real.shape[0]
    flat = factor.reshape(factor.shape[0], 4 * S)
    real_part = jnp.dot(inverse_real, flat, preferred_element_type=jnp.float32).reshape(
        row_total, 2, 2 * S
    )
    imag_part = jnp.dot(inverse_imag, flat, preferred_element_type=jnp.float32).reshape(
        row_total, 2, 2 * S
    )
    real_out = real_part[:, 0] - imag_part[:, 1]
    imag_out = real_part[:, 1] + imag_part[:, 0]
    return -jnp.stack([real_out, imag_out], axis=1)


def pivot_terms(masked_rows, chosen_rows):
    row_total = masked_rows.shape[0]
    parts = masked_rows.reshape(row_total, 2, 2, S)
    m_real = parts[:, 0]
    m_imag = parts[:, 1]
    left = jnp.stack(
        [jnp.stack([m_real, m_imag], axis=1), jnp.stack([-m_imag, m_real], axis=1)], axis=1
    )
    right = chosen_rows.reshape(row_total, 2, 2, S)
    return jnp.einsum("rqojs,rqjt->jost", left, right, preferred_element_type=jnp.float32)


def per_device(inverse_block, factor_column, block_pattern, pivot_inverse):
    masked = factor_column * expand_pattern(block_pattern)
    rows_here = masked.shape[0]
    share_rows = rows_here // lax.axis_size("pcol")
    column_index = lax.axis_index("pcol")
    factor_per = lax.axis_size("prow") // lax.axis_size("pcol")
    pieces = []
    for step_index in range(factor_per):
        pieces.append(from_root(masked, "prow", column_index * factor_per + step_index))
    column_factor = jnp.concatenate(pieces, axis=0)
    partial_value = complex_column(inverse_block[0], inverse_block[1], column_factor)
    totals = lax.psum(partial_value, "pcol")
    local_pivot = lax.psum(pivot_terms(masked, totals.astype(jnp.bfloat16)), "prow")
    own_rows = lax.dynamic_slice_in_dim(totals, column_index * share_rows, share_rows, 0)
    return (own_rows, pivot_inverse - local_pivot)


def solution(mesh):
    in_specs = (
        P(None, ("pole", "prow"), "pcol"),
        P(("pole", "prow"), None, None),
        P("pole", "prow"),
        P("pole", None, None, None),
    )
    out_specs = (P(("pole", "prow", "pcol"), None, None), P("pole", None, None, None))
    return jax.shard_map(
        per_device, mesh=mesh, in_specs=in_specs, out_specs=out_specs, check_vma=False
    )
```

profile of v0, /device:TPU:0, one launch (start us, length us, event | category | flops | bytes accessed | tf_op | source)
XLA Modules:
  0.0 375.3 jit_solution(4159504190313070753)
XLA Ops:
  7.2 0.0 all-reduce.4.cloned.1.call-start
  7.2 0.7 convert_bitcast_fusion
  7.9 0.3 broadcast_in_dim.4
  8.2 0.2 copy.30
  8.4 6.1 %copy.11 = bf16[512,2,1024]{0,2,1:T(8,128)(2,1)} copy(bf16[512,2,1024]{2,1,0:T(2,128)(2,1)} %param.5) | data formatting | bytes 4194304 | tf_op args[1]
  14.6 3.2 broadcast_select_fusion
  17.8 0.0 copy-start.2
  17.8 0.0 all-reduce.4.cloned.1.call-update
  17.8 0.0 all-reduce.6.cloned.1.call-start
  17.8 89.3 %all-reduce.4.cloned.1.call-done = bf16[512,2048]{0,1:T(8,128)(2,1)} async-done(((bf16[512,2048]{0,1:T(8,128)(2,1)}), bf16[512,2048]{0,1:T(8,128)(2,1)}) %all-reduce.4.cloned.1.call-update) | async-done | bytes 2097168 | tf_op jit(solution)/shard_map/psum | solution.py:12
  107.2 0.0 copy-done.2
  107.2 0.0 copy-start
  107.2 3.0 fusion.11
  110.2 0.0 copy-done
  110.2 1.3 fusion.9
  111.5 1.0 slice_subtract_fusion
  112.6 2.5 maximum_negate_fusion
  115.1 0.0 all-reduce.6.cloned.1.call-update
  115.1 0.0 all-reduce.8.cloned.1.call-start
  115.2 0.1 fusion.8
  115.2 0.1 slice_bitcast_fusion
  115.3 1.5 maximum_bitcast_fusion
  116.8 82.9 %all-reduce.6.cloned.1.call-done = f32[512,2,1024]{0,2,1:T(8,128)} async-done(((f32[512,2,1024]{0,2,1:T(8,128)}), f32[512,2,1024]{0,2,1:T(8,128)}) %all-reduce.6.cloned.1.call-update) | async-done | bytes 4194320 | tf_op jit(solution)/shard_map/psum | solution.py:59
  199.7 0.0 copy-start.1
  199.7 2.6 convert_element_type.11
  202.3 0.2 copy-done.1
  202.6 4.4 %fusion.4 = f32[2,2,512,512]{3,2,1,0:T(8,128)} fusion(bf16[512,1,2,2,512]{0,4,1,2,3:T(8,128)(2,1)S(1)} %copy-done.1, bf16[512,2,2,512,1]{0,3,2,1,4:T(8,128)(2,1)S(1)} %bitcast.48, bf16[512,1,2,2,512]{0,4,3,2,1:T(8,128)(2,1)S(1)} %bitcast.44), kind=kOutput, calls=%fused_computation.5 | convolution fusion | flops 2155872256 | bytes 10485760 | tf_op jit(solution)/shard_map/rqojs,rqjt->jost/dot_general | solution.py:45
  206.9 0.0 all-reduce.8.cloned.1.call-update
  207.0 1.3 constant_dynamic-slice_fusion
  208.3 1.3 copy.16
  209.6 152.7 %all-reduce.8.cloned.1.call-done = f32[2,2,512,512]{3,2,1,0:T(8,128)} async-done(((f32[2,2,512,512]{3,2,1,0:T(8,128)}), f32[2,2,512,512]{3,2,1,0:T(8,128)}) %all-reduce.8.cloned.1.call-update) | async-done | bytes 4194320 | tf_op jit(solution)/shard_map/psum | solution.py:60
  362.2 6.5 %sub.8 = f32[2,2,512,512]{3,2,1,0:T(8,128)} subtract(f32[2,2,512,512]{3,2,1,0:T(8,128)} %param.7, f32[2,2,512,512]{3,2,1,0:T(8,128)} %all-reduce.8.cloned.1.call-done) | non-fusion elementwise | flops 1048576 | bytes 12582912 | tf_op jit(solution)/shard_map/sub | solution.py:62
Async XLA Ops:
  7.2 100.0 %all-reduce.4.cloned.1.call-start = ((), (), s32[]{:S(2)}) async-start(), calls=%async_computation | async-start | bytes 4194304 | tf_op jit(solution)/shard_map/psum | solution.py:12
  17.8 89.4 %copy-start.2 = (bf16[2,512,512]{2,1,0:T(8,128)(2,1)S(1)}, bf16[2,512,512]{2,1,0:T(8,128)(2,1)}, u32[]{:S(2)}) copy-start(bf16[2,512,512]{2,1,0:T(8,128)(2,1)} %param.4) | copy-start | bytes 3145732
  17.8 181.9 %all-reduce.6.cloned.1.call-start = ((), (), s32[]{:S(2)}) async-start(), calls=%async_computation.1 | async-start | bytes 8388608 | tf_op jit(solution)/shard_map/psum | solution.py:59
  107.2 3.0 copy-start
  115.1 247.1 %all-reduce.8.cloned.1.call-start = ((), (), s32[]{:S(2)}) async-start(), calls=%async_computation.2 | async-start | bytes 8388608 | tf_op jit(solution)/shard_map/psum | solution.py:60
  199.7 2.9 copy-start.1
Sparse Core Ops, SparseCore 0:
  17.9 89.2 all-reduce.3
  115.2 84.4 all-reduce.5
  207.1 155.1 all-reduce.7
where the time goes:
time: 376 us; the launch traced here: 375 us
  waiting for transfers between devices  325 us (86%)
  other arithmetic  18.1 us (5%)
  between operations  13.8 us (4%)
  local copies, waits for them, and re-layouts  9.59 us (3%)
  matrix products  8.74 us (2%)
    psum x1, waiting for transfers between devices, per_device(): lax.psum(pivot_terms(masked, totals.astype(jnp.bfloat16)), 'prow')  153 us
    psum x1, waiting for transfers between devices, from_root(): return lax.psum(block, axis)  89.3 us
    psum x1, waiting for transfers between devices, per_device(): totals = lax.psum(partial_value, 'pcol')  82.9 us
    unnamed x10, local copies, waits for them, and re-layouts  7.95 us
  transfers between devices with their start and end apart: 3, of which 3 were waited for; matrix products, arithmetic and copies ran while one was open for 1% of the time, Pallas kernels for 0%

commit v1 on v0

v1 whole, which is shorter than its diff:
```python
import jax
import jax.numpy as jnp
from jax import lax
from jax.sharding import PartitionSpec as P

S = 512
BLK = 128


def swap(x, axis, distance):
    size = lax.axis_size(axis)
    return lax.ppermute(x, axis, [(i, i ^ distance) for i in range(size)])


def gather_z(m):
    size = lax.axis_size("prow")
    if size != 4:
        return [(m, 0)] + [(swap(m, "prow", d), d) for d in range(1, size)]
    level = lax.axis_index("prow")
    two = swap(m, "prow", 2)
    one = swap(m, "prow", 1)
    middle = lax.ppermute(m, "prow", [(1, 2), (2, 1)])
    ends = lax.ppermute(two, "prow", [(2, 3), (1, 0)])
    inner = (level == 1) | (level == 2)
    return [(m, 0), (one, 1), (two, 2), (jnp.where(inner, middle, ends), 3)]


def gather_col(a):
    size = lax.axis_size("pcol")
    across = [(a, 0)] + [(swap(a, "pcol", d), d) for d in range(2, size, 2)]
    return across + [(swap(piece, "pcol", 1), d ^ 1) for piece, d in across]


def per_device(inverse_block, factor_column, block_pattern, pivot_inverse):
    bf16 = jnp.bfloat16
    levels = lax.axis_size("prow")
    level = lax.axis_index("prow")
    columns = lax.axis_size("pcol")
    column = lax.axis_index("pcol")
    rows = factor_column.shape[0]
    width = factor_column.shape[2] // columns
    blocks = rows // BLK
    node = column * width // S

    keep = lax.dynamic_index_in_dim(block_pattern, node, 0, keepdims=False).astype(bf16)
    keep = jnp.broadcast_to(keep[:, None], (blocks, BLK)).reshape(1, rows, 1)
    own = lax.dynamic_slice_in_dim(factor_column, column * width, width, 2)
    own = jnp.transpose(own, (1, 0, 2)) * keep
    side = lax.dynamic_slice_in_dim(factor_column, node * S, S, 2)
    side = jnp.transpose(side, (1, 0, 2)) * keep

    a_pieces = gather_col(inverse_block)
    m_pieces = gather_z(own)
    depth = inverse_block.shape[2]
    a_all = jnp.zeros((2, rows, depth * columns), bf16)
    for piece, d in a_pieces:
        a_all = lax.dynamic_update_slice(a_all, piece, (0, 0, (column ^ d) * depth))
    m_all = jnp.zeros((2, rows * levels, width), bf16)
    for piece, d in m_pieces:
        m_all = lax.dynamic_update_slice(m_all, piece, (0, (level ^ d) * rows, 0))
    dot = lambda a, b: jnp.dot(a, b, preferred_element_type=jnp.float32)
    right = jnp.concatenate([m_all[0], m_all[1]], axis=1)
    turned = jnp.concatenate([-m_all[1], m_all[0]], axis=1)
    y = -(dot(a_all[0], right) + dot(a_all[1], turned))
    chosen = y.astype(bf16)
    yr, yi = chosen[:, :width], chosen[:, width:]
    dot_t = lambda a, b: lax.dot_general(a, b, (((0,), (0,)), ((), ())), preferred_element_type=jnp.float32)
    part = dot_t(side[0], chosen) + dot_t(side[1], jnp.concatenate([-yi, yr], axis=1))
    share = S // levels
    part = part.reshape(levels, share, 2 * width)

    def take(i):
        return lax.dynamic_index_in_dim(part, i, 0, keepdims=False)

    total = take(level)
    for d in range(1, levels):
        total = total + swap(take(level ^ d).astype(bf16), "prow", d).astype(jnp.float32)
    piece = total.astype(bf16)

    cut = rows // columns
    y_parts = y.reshape(columns, cut, 2 * width)
    y_all = lax.all_to_all(y_parts, "pcol", 0, 0)
    own_rows = jnp.transpose(y_all.reshape(columns, cut, 2, width), (1, 2, 0, 3)).reshape(cut, 2, columns * width)

    nodes = pivot_inverse.shape[0]
    minus = jnp.zeros((columns, levels, share, 2 * width), bf16)
    for p, d in [(piece, 0)] + [(swap(piece, "prow", d), d) for d in range(1, levels)]:
        for q, e in gather_col(p):
            minus = lax.dynamic_update_slice(minus, q[None, None], (column ^ e, level ^ d, 0, 0))
    minus = minus.reshape(nodes, columns // nodes, S, 2, width)
    minus = jnp.transpose(minus, (0, 3, 2, 1, 4)).reshape(nodes, 2, S, S)
    return own_rows, pivot_inverse - minus.astype(jnp.float32)


def solution(mesh):
    in_specs = (
        P(None, ("pole", "prow"), "pcol"),
        P(("pole", "prow"), None, None),
        P("pole", "prow"),
        P("pole", None, None, None),
    )
    out_specs = (P(("pole", "prow", "pcol"), None, None), P("pole", None, None, None))
    return jax.shard_map(
        per_device, mesh=mesh, in_specs=in_specs, out_specs=out_specs, check_vma=False
    )
```

time: 376 us -> 147 us (0.39)
  waiting for transfers between devices: 325 us -> 47.3 us
  local copies, waits for them, and re-layouts: 9.59 us -> 52.5 us
  starting transfers between devices: 0.12 us -> 29 us
  between operations: 13.8 us -> 0.82 us
  other arithmetic: 18.1 us -> 12.3 us
  matrix products: 8.74 us -> 4.45 us
    psum x3 -> x0, waiting for transfers between devices: 325 us -> none  [the longest x1 153 us: per_device(): lax.psum(pivot_terms(masked, totals.astype(jnp.bfloat16)), 'prow')]
    ppermute x0 -> x25, waiting for transfers between devices: none -> 47.3 us  [the longest x23 40.7 us: swap(): return lax.ppermute(x, axis, [(i, i ^ distance) for i in range(size)])]
    ppermute x0 -> x25, starting transfers between devices: none -> 25.3 us  [the longest x23 22.5 us: swap(): return lax.ppermute(x, axis, [(i, i ^ distance) for i in range(size)])]
    dynamic_update_slice x0 -> x21, local copies, waits for them, and re-layouts: none -> 16.8 us  [the longest x15 10 us: per_device(): lax.dynamic_update_slice(minus, q[None, None], (column ^ e, level ^ d, 0,...]
    convert_element_type x0 -> x3, local copies, waits for them, and re-layouts: none -> 13.4 us  [the longest x2 12.7 us: per_device(): return (own_rows, pivot_inverse - minus.astype(jnp.float32))]
    reshape x0 -> x3, local copies, waits for them, and re-layouts: none -> 5.39 us  [the longest x2 3.52 us: per_device(): y_all.reshape(columns, cut, 2, width)]
    dot_general x3 -> x4, matrix products: 8.74 us -> 4.45 us  [the longest x2 3.52 us: per_device(): dot = lambda a, b: jnp.dot(a, b, preferred_element_type=jnp.float32)]
    unnamed x10 -> x6, local copies, waits for them, and re-layouts: 7.95 us -> 10.5 us
  transfers between devices with their start and end apart: 3 -> 26, of which waited for: 3 -> 8; matrix products, arithmetic and copies ran while one was open for 1% -> 38% of each run, Pallas kernels for 0% -> 0%
where the time goes in v1:
time: 147 us; the launch traced here: 146 us
  local copies, waits for them, and re-layouts  52.5 us (36%)
  waiting for transfers between devices  47.3 us (32%)
  starting transfers between devices  29 us (20%)
  other arithmetic  12.3 us (8%)
  matrix products  4.45 us (3%)
    ppermute x23, waiting for transfers between devices, swap(): return lax.ppermute(x, axis, [(i, i ^ distance) for i in range(size)])  40.7 us
    ppermute x23, starting transfers between devices, swap(): return lax.ppermute(x, axis, [(i, i ^ distance) for i in range(size)])  22.5 us
    convert_element_type x2, local copies, waits for them, and re-layouts, per_device(): return (own_rows, pivot_inverse - minus.astype(jnp.float32))  12.7 us
    unnamed x6, local copies, waits for them, and re-layouts  10.5 us
    dynamic_update_slice x15, local copies, waits for them, and re-layouts, per_device(): lax.dynamic_update_slice(minus, q[None, None], (column ^ e, level ^ d, 0,...  10 us
    ppermute x1, waiting for transfers between devices, gather_z(): ends = lax.ppermute(two, 'prow', [(2, 3), (1, 0)])  6.56 us
    sub x1, other arithmetic, per_device(): return (own_rows, pivot_inverse - minus.astype(jnp.float32))  6.44 us
    dynamic_update_slice x2, local copies, waits for them, and re-layouts, per_device(): m_all = lax.dynamic_update_slice(m_all, piece, (0, (level ^ d) * rows, 0))  3.74 us
  transfers between devices with their start and end apart: 26, of which 8 were waited for; matrix products, arithmetic and copies ran while one was open for 38% of the time, Pallas kernels for 0%

profile of v1, /device:TPU:0, one launch (start us, length us, event | category | flops | bytes accessed | tf_op | source)
XLA Modules:
  0.0 146.3 jit_solution(10700706230594618296)
XLA Ops:
  0.6 3.0 %collective-permute-start = (bf16[2,512,512]{2,1,0:T(8,128)(2,1)}, bf16[2,512,512]{2,1,0:T(8,128)(2,1)}, u32[]{:S(2)}, u32[]{:S(2)}) collective-permute-start(bf16[2,512,512]{2,1,0:T(8,128)(2,1)} %param.4), channel_id=1, source_target_pairs={{0,2},{1,3},{2,0},{3,1},{4,6},{5,7},{6,4},{7,5},{8,10},{9,11},{10,... | collective-permute-start | bytes 3145736 | tf_op jit(solution)/shard_map/ppermute | solution.py:12
  3.6 0.7 fusion.27
  4.4 0.4 constant_dynamic-slice_fusion.2
  4.8 1.5 broadcast_in_dim.64
  6.2 1.1 constant_dynamic-update-slice_fusion.2
  7.4 2.6 %collective-permute-start.4 = (bf16[2,512,256]{2,1,0:T(8,128)(2,1)}, bf16[2,512,256]{2,1,0:T(8,128)(2,1)}, u32[]{:S(2)}, u32[]{:S(2)}) collective-permute-start(bf16[2,512,256]{2,1,0:T(8,128)(2,1)} %get-tuple-element.7), channel_id=1, source_target_pairs={{0,8},{4,12},{8,0},{12,4},{1,9},{5,13},{9,1},{13,5},{2,10},{6,14},... | collective-permute-start | bytes 1572872 | tf_op jit(solution)/shard_map/ppermute | solution.py:12
  10.0 1.6 %collective-permute-start.3 = (bf16[2,512,256]{2,1,0:T(8,128)(2,1)}, bf16[2,512,256]{2,1,0:T(8,128)(2,1)}, u32[]{:S(2)}, u32[]{:S(2)}) collective-permute-start(bf16[2,512,256]{2,1,0:T(8,128)(2,1)} %get-tuple-element.7), channel_id=1, source_target_pairs={{0,4},{4,0},{8,12},{12,8},{1,5},{5,1},{9,13},{13,9},{2,6},{6,2},{1... | collective-permute-start | bytes 1572872 | tf_op jit(solution)/shard_map/ppermute | solution.py:12
  11.6 1.4 collective-permute-start.5
  13.0 0.7 constant_dynamic-slice_fusion
  13.9 20.5 %collective-permute-done.4 = bf16[2,512,256]{2,1,0:T(8,128)(2,1)} collective-permute-done((bf16[2,512,256]{2,1,0:T(8,128)(2,1)}, bf16[2,512,256]{2,1,0:T(8,128)(2,1)}, u32[]{:S(2)}, u32[]{:S(2)}) %collective-permute-start.4) | collective-permute-done | bytes 524320 | tf_op jit(solution)/shard_map/ppermute | solution.py:12
  34.4 1.3 collective-permute-start.6
  35.7 0.5 broadcast_in_dim.63
  36.4 1.9 %constant_dynamic-update-slice_fusion.1 = bf16[2,2048,256]{2,1,0:T(8,128)(2,1)} fusion(bf16[2,2048,256]{2,1,0:T(8,128)(2,1)} %get-tuple-element.6, bf16[2,512,256]{2,1,0:T(8,128)(2,1)} %collective-permute-done.3, s32[]{:T(128)S(6)} %select_n.108), kind=kLoop, calls=%fused_computation.57 | loop fusion | bytes 1048580 | tf_op jit(solution)/shard_map/dynamic_update_slice | solution.py:60
  38.3 1.9 %constant_dynamic-update-slice_fusion = bf16[2,2048,256]{2,1,0:T(8,128)(2,1)} fusion(bf16[2,2048,256]{2,1,0:T(8,128)(2,1)} %constant_dynamic-update-slice_fusion.1, bf16[2,512,256]{2,1,0:T(8,128)(2,1)} %collective-permute-done.4, s32[]{:T(128)S(6)} %select_n.109), kind=kLoop, calls=%fused_computation.56 | loop fusion | bytes 1048580 | tf_op jit(solution)/shard_map/dynamic_update_slice | solution.py:60
  40.2 1.4 constant_dynamic-update-slice_fusion.5
  41.6 6.6 %collective-permute-done.6 = bf16[2,512,256]{2,1,0:T(8,128)(2,1)S(1)} collective-permute-done((bf16[2,512,256]{2,1,0:T(8,128)(2,1)}, bf16[2,512,256]{2,1,0:T(8,128)(2,1)S(1)}, u32[]{:S(2)}, u32[]{:S(2)}) %collective-permute-start.6) | collective-permute-done | bytes 524320 | tf_op jit(solution)/shard_map/ppermute | solution.py:23
  48.1 0.9 select_dynamic-update-slice_fusion
  49.1 1.4 constant_dynamic-update-slice_fusion.4
  50.5 1.3 fusion.31
  51.8 1.7 %slice_bitcast_fusion.8 = (bf16[2048,256]{1,0:T(8,128)(2,1)S(1)}, bf16[2048,256]{1,0:T(8,128)(2,1)S(1)}) fusion(bf16[2,2048,256]{2,1,0:T(8,128)(2,1)} %select_dynamic-update-slice_fusion), kind=kLoop, calls=%fused_computation.14 | loop fusion | bytes 4194304 | tf_op jit(solution)/shard_map/squeeze | solution.py:62
  53.6 1.3 fusion
  54.9 2.2 %fusion.34 = (bf16[512,512]{1,0:T(8,128)(2,1)S(1)}, f32[512,512]{1,0:T(8,128)}) fusion(f32[512,512]{1,0:T(8,128)S(1)} %fusion, bf16[2048,256]{1,0:T(8,128)(2,1)S(1)} %get-tuple-element.8, bf16[2048,256]{1,0:T(8,128)(2,1)S(1)} %get-tuple-element.9, bf16[2,512,2048]{2,1,0:T(8,128)(2,1)S(1)} %constant_dynamic-update-slice_fusion.3), kind=kOutput, calls=%fused_computation.72 | convolution fusion | flops 1078722560 | bytes 6815744 | tf_op jit(solution)/shard_map/dot_general | solution.py:61
  57.2 0.5 fusion.15
  57.7 0.5 convolution_add_fusion
  58.1 0.7 fusion.23
  58.9 4.6 %collective-permute-start.9 = (bf16[128,512]{1,0:T(8,128)(2,1)}, bf16[128,512]{1,0:T(8,128)(2,1)S(1)}, u32[]{:S(2)}, u32[]{:S(2)}) collective-permute-start(bf16[128,512]{1,0:T(8,128)(2,1)} %get-tuple-element.11), channel_id=1, source_target_pairs={{0,12},{4,8},{8,4},{12,0},{1,13},{5,9},{9,5},{13,1},{2,14},{6,10},... | collective-permute-start | bytes 393224 | tf_op jit(solution)/shard_map/ppermute | solution.py:12
  63.4 0.6 collective-permute-start.7
  64.0 4.0 %collective-permute-done.9 = bf16[128,512]{1,0:T(8,128)(2,1)S(1)} collective-permute-done((bf16[128,512]{1,0:T(8,128)(2,1)}, bf16[128,512]{1,0:T(8,128)(2,1)S(1)}, u32[]{:S(2)}, u32[]{:S(2)}) %collective-permute-start.9) | collective-permute-done | bytes 131104 | tf_op jit(solution)/shard_map/ppermute | solution.py:12
  68.0 6.0 %collective-permute-done.8 = bf16[128,512]{1,0:T(8,128)(2,1)S(1)} collective-permute-done((bf16[128,512]{1,0:T(8,128)(2,1)}, bf16[128,512]{1,0:T(8,128)(2,1)S(1)}, u32[]{:S(2)}, u32[]{:S(2)}) %collective-permute-start.8) | collective-permute-done | bytes 131104 | tf_op jit(solution)/shard_map/ppermute | solution.py:12
  74.0 1.6 %broadcast_in_dim.66 = bf16[4,4,128,512]{3,2,1,0:T(8,128)(2,1)} broadcast(bf16[]{:T(256)} %constant.41.clone.1), dimensions={} | broadcast | bytes 2097154 | tf_op jit(solution)/shard_map/broadcast_in_dim | solution.py:86
  75.6 1.6 %bitcast_dynamic-update-slice_fusion.15 = (bf16[4,4,128,512]{3,2,1,0:T(8,128)(2,1)}, bf16[128,512]{1,0:T(8,128)(2,1)S(1)}) fusion(bf16[4,4,128,512]{3,2,1,0:T(8,128)(2,1)} %broadcast_in_dim.66, s32[]{:T(128)S(6)} %select_n.118, s32[]{:T(128)S(6)} %select_n.114, bf16[128,512]{1,0:T(8,128)(2,1)S(1)} %collective-permute-done.9, ...), kind=kLoop, calls=%fused_computation.54 | loop fusion | flops 458752 | bytes 917512 | tf_op jit(solution)/shard_map/dynamic_update_slice | solution.py:89
  77.2 1.1 collective-permute-start.10
  78.3 5.2 %copy.19 = f32[2,2,512,512]{2,3,1,0:T(8,128)} copy(f32[2,2,512,512]{3,2,1,0:T(8,128)} %param.7) | data formatting | bytes 8388608 | tf_op args[3]
  83.5 3.7 %all-to-all-start = ((f32[4,128,512]{2,1,0:T(8,128)}), f32[4,128,512]{2,1,0:T(8,128)S(1)}, u32[]{:S(2)}, u32[]{:S(2)}) async-start(f32[4,128,512]{2,1,0:T(8,128)} %bitcast.95), calls=%async_computation | async-start | bytes 2097152 | tf_op jit(solution)/shard_map/all_to_all | solution.py:82
  87.5 3.2 %collective-permute-start.17 = (bf16[128,512]{1,0:T(8,128)(2,1)S(1)}, bf16[128,512]{1,0:T(8,128)(2,1)S(1)}, u32[]{:S(2)}, u32[]{:S(2)}) collective-permute-start(bf16[128,512]{1,0:T(8,128)(2,1)S(1)} %get-tuple-element.5), channel_id=1, source_target_pairs={{0,8},{4,12},{8,0},{12,4},{1,9},{5,13},{9,1},{13,5},{2,10},{6,14},... | collective-permute-start | bytes 393224 | tf_op jit(solution)/shard_map/ppermute | solution.py:12
  90.7 1.2 collective-permute-start.21
  91.9 1.7 %collective-permute-start.14 = (bf16[128,512]{1,0:T(8,128)(2,1)S(1)}, bf16[128,512]{1,0:T(8,128)(2,1)S(1)}, u32[]{:S(2)}, u32[]{:S(2)}) collective-permute-start(bf16[128,512]{1,0:T(8,128)(2,1)S(1)} %collective-permute-done.13), channel_id=1, source_target_pairs={{0,2},{1,3},{2,0},{3,1},{4,6},{5,7},{6,4},{7,5},{8,10},{9,11},{10,... | collective-permute-start | bytes 393224 | tf_op jit(solution)/shard_map/ppermute | solution.py:12
  93.6 0.7 bitcast_dynamic-update-slice_fusion.14
  94.5 6.1 %collective-permute-done.17 = bf16[128,512]{1,0:T(8,128)(2,1)S(1)} collective-permute-done((bf16[128,512]{1,0:T(8,128)(2,1)S(1)}, bf16[128,512]{1,0:T(8,128)(2,1)S(1)}, u32[]{:S(2)}, u32[]{:S(2)}) %collective-permute-start.17) | collective-permute-done | bytes 131104 | tf_op jit(solution)/shard_map/ppermute | solution.py:12
  100.6 1.8 %collective-permute-start.18 = (bf16[128,512]{1,0:T(8,128)(2,1)S(1)}, bf16[128,512]{1,0:T(8,128)(2,1)S(1)}, u32[]{:S(2)}, u32[]{:S(2)}) collective-permute-start(bf16[128,512]{1,0:T(8,128)(2,1)S(1)} %collective-permute-done.17), channel_id=1, source_target_pairs={{0,2},{1,3},{2,0},{3,1},{4,6},{5,7},{6,4},{7,5},{8,10},{9,11},{10,... | collective-permute-start | bytes 393224 | tf_op jit(solution)/shard_map/ppermute | solution.py:12
  102.3 0.7 bitcast_dynamic-update-slice_fusion.13
  103.3 0.7 bitcast_dynamic-update-slice_fusion.12
  104.0 0.7 bitcast_dynamic-update-slice_fusion.11
  104.8 0.7 bitcast_dynamic-update-slice_fusion.10
  105.5 0.4 collective-permute-start.16
  105.9 1.6 %collective-permute-done.18 = bf16[128,512]{1,0:T(8,128)(2,1)S(1)} collective-permute-done((bf16[128,512]{1,0:T(8,128)(2,1)S(1)}, bf16[128,512]{1,0:T(8,128)(2,1)S(1)}, u32[]{:S(2)}, u32[]{:S(2)}) %collective-permute-start.18) | collective-permute-done | bytes 131104 | tf_op jit(solution)/shard_map/ppermute | solution.py:12
  107.6 2.3 %collective-permute-done.22 = bf16[128,512]{1,0:T(8,128)(2,1)S(1)} collective-permute-done((bf16[128,512]{1,0:T(8,128)(2,1)S(1)}, bf16[128,512]{1,0:T(8,128)(2,1)S(1)}, u32[]{:S(2)}, u32[]{:S(2)}) %collective-permute-start.22) | collective-permute-done | bytes 131104 | tf_op jit(solution)/shard_map/ppermute | solution.py:12
  109.9 0.7 bitcast_dynamic-update-slice_fusion.9
  110.6 0.7 bitcast_dynamic-update-slice_fusion.8
  111.2 0.7 bitcast_dynamic-update-slice_fusion.7
  111.9 0.7 bitcast_dynamic-update-slice_fusion.6
  112.6 0.7 bitcast_dynamic-update-slice_fusion.5
  113.3 0.7 bitcast_dynamic-update-slice_fusion.4
  113.9 0.7 bitcast_dynamic-update-slice_fusion.3
  114.6 0.7 bitcast_dynamic-update-slice_fusion.2
  115.2 0.7 bitcast_dynamic-update-slice_fusion.1
  115.9 0.7 bitcast_dynamic-update-slice_fusion
  116.6 5.4 %reshape.38 = f32[2,2,512,2,256]{4,3,2,1,0:T(2,128)} reshape(bf16[4,4,128,512]{3,2,1,0:T(8,128)(2,1)} %bitcast_dynamic-update-slice_fusion) | data formatting | bytes 6291456 | tf_op jit(solution)/shard_map/convert_element_type | solution.py:92
  122.0 7.2 %copy.18 = f32[2,2,512,2,256]{2,4,3,1,0:T(8,128)} copy(f32[2,2,512,2,256]{4,1,2,3,0:T(2,128)} %bitcast.91) | data formatting | bytes 8388608 | tf_op jit(solution)/shard_map/convert_element_type | solution.py:92
  129.3 6.4 %bitcast_subtract_fusion = f32[2,2,512,512]{2,3,1,0:T(8,128)} fusion(f32[2,2,512,512]{2,3,1,0:T(8,128)} %copy.19, f32[2,2,512,2,256]{2,4,3,1,0:T(8,128)} %copy.18), kind=kLoop, calls=%fused_computation | loop fusion | flops 1048576 | bytes 12582912 | tf_op jit(solution)/shard_map/sub | solution.py:92
  135.7 5.2 %copy.20 = f32[2,2,512,512]{3,2,1,0:T(8,128)} copy(f32[2,2,512,512]{2,3,1,0:T(8,128)} %bitcast_subtract_fusion) | data formatting | bytes 8388608
  140.9 1.6 %reshape.34 = f32[4,128,2,256]{3,2,1,0:T(2,128)} reshape(f32[4,128,512]{2,1,0:T(8,128)S(1)} %all-to-all-done) | data formatting | bytes 2097152 | tf_op jit(solution)/shard_map/reshape | solution.py:83
  142.5 1.9 %copy.31 = f32[4,128,2,256]{3,0,2,1:T(4,128)S(1)} copy(f32[4,128,2,256]{3,2,1,0:T(2,128)} %reshape.34) | data formatting | bytes 2097152 | tf_op jit(solution)/shard_map/reshape | solution.py:83
  144.4 1.9 %reshape.35 = f32[128,2,1024]{2,1,0:T(2,128)} reshape(f32[128,2,4,256]{3,2,1,0:T(4,128)S(1)} %bitcast.92) | data formatting | bytes 2097152 | tf_op jit(solution)/shard_map/reshape | solution.py:83
  (40 shorter events, 1.6 us)
Async XLA Ops:
  0.6 3.8 %copy-start = (bf16[512,2,1024]{2,1,0:T(2,128)(2,1)S(1)}, bf16[512,2,1024]{2,1,0:T(2,128)(2,1)}, u32[]{:S(2)}) copy-start(bf16[512,2,1024]{2,1,0:T(2,128)(2,1)} %param.5) | copy-start | bytes 6291460
  0.6 39.5 %collective-permute-start = (bf16[2,512,512]{2,1,0:T(8,128)(2,1)}, bf16[2,512,512]{2,1,0:T(8,128)(2,1)}, u32[]{:S(2)}, u32[]{:S(2)}) collective-permute-start(bf16[2,512,512]{2,1,0:T(8,128)(2,1)} %param.4), channel_id=1, source_target_pairs={{0,2},{1,3},{2,0},{3,1},{4,6},{5,7},{6,4},{7,5},{8,10},{9,11},{10,... | collective-permute-start | bytes 3145736 | tf_op jit(solution)/shard_map/ppermute | solution.py:12
  4.8 5.2 %copy-start.1 = (bf16[2,512,512]{2,1,0:T(8,128)(2,1)S(1)}, bf16[2,512,512]{2,1,0:T(8,128)(2,1)}, u32[]{:S(2)}) copy-start(bf16[2,512,512]{2,1,0:T(8,128)(2,1)} %param.4) | copy-start | bytes 3145732
  7.4 27.0 %collective-permute-start.4 = (bf16[2,512,256]{2,1,0:T(8,128)(2,1)}, bf16[2,512,256]{2,1,0:T(8,128)(2,1)}, u32[]{:S(2)}, u32[]{:S(2)}) collective-permute-start(bf16[2,512,256]{2,1,0:T(8,128)(2,1)} %get-tuple-element.7), channel_id=1, source_target_pairs={{0,8},{4,12},{8,0},{12,4},{1,9},{5,13},{9,1},{13,5},{2,10},{6,14},... | collective-permute-start | bytes 1572872 | tf_op jit(solution)/shard_map/ppermute | solution.py:12
  10.0 39.1 %collective-permute-start.1 = (bf16[2,512,512]{2,1,0:T(8,128)(2,1)S(1)}, bf16[2,512,512]{2,1,0:T(8,128)(2,1)}, u32[]{:S(2)}, u32[]{:S(2)}) collective-permute-start(bf16[2,512,512]{2,1,0:T(8,128)(2,1)S(1)} %copy-done.1), channel_id=1, source_target_pairs={{0,1},{1,0},{2,3},{3,2},{4,5},{5,4},{6,7},{7,6},{8,9},{9,8},{10,11... | collective-permute-start | bytes 3145736 | tf_op jit(solution)/shard_map/ppermute | solution.py:12
  10.0 26.4 %collective-permute-start.3 = (bf16[2,512,256]{2,1,0:T(8,128)(2,1)}, bf16[2,512,256]{2,1,0:T(8,128)(2,1)}, u32[]{:S(2)}, u32[]{:S(2)}) collective-permute-start(bf16[2,512,256]{2,1,0:T(8,128)(2,1)} %get-tuple-element.7), channel_id=1, source_target_pairs={{0,4},{4,0},{8,12},{12,8},{1,5},{5,1},{9,13},{13,9},{2,6},{6,2},{1... | collective-permute-start | bytes 1572872 | tf_op jit(solution)/shard_map/ppermute | solution.py:12
  11.6 30.0 %collective-permute-start.5 = (bf16[2,512,256]{2,1,0:T(8,128)(2,1)}, bf16[2,512,256]{2,1,0:T(8,128)(2,1)}, u32[]{:S(2)}, u32[]{:S(2)}) collective-permute-start(bf16[2,512,256]{2,1,0:T(8,128)(2,1)} %get-tuple-element.7), channel_id=1, source_target_pairs={{4,8},{8,4},{5,9},{9,5},{6,10},{10,6},{7,11},{11,7},{20,24},{24,20... | collective-permute-start | bytes 1572872 | tf_op jit(solution)/shard_map/ppermute | solution.py:22
  34.4 13.7 %collective-permute-start.6 = (bf16[2,512,256]{2,1,0:T(8,128)(2,1)}, bf16[2,512,256]{2,1,0:T(8,128)(2,1)S(1)}, u32[]{:S(2)}, u32[]{:S(2)}) collective-permute-start(bf16[2,512,256]{2,1,0:T(8,128)(2,1)} %collective-permute-done.4), channel_id=1, source_target_pairs={{8,12},{4,0},{9,13},{5,1},{10,14},{6,2},{11,15},{7,3},{24,28},{20,... | collective-permute-start | bytes 1572872 | tf_op jit(solution)/shard_map/ppermute | solution.py:23
  40.2 13.3 %collective-permute-start.2 = (bf16[2,512,512]{2,1,0:T(8,128)(2,1)}, bf16[2,512,512]{2,1,0:T(8,128)(2,1)S(1)}, u32[]{:S(2)}, u32[]{:S(2)}) collective-permute-start(bf16[2,512,512]{2,1,0:T(8,128)(2,1)} %collective-permute-done), channel_id=1, source_target_pairs={{0,1},{1,0},{2,3},{3,2},{4,5},{5,4},{6,7},{7,6},{8,9},{9,8},{10,11... | collective-permute-start | bytes 3145736 | tf_op jit(solution)/shard_map/ppermute | solution.py:12
  58.9 9.1 %collective-permute-start.9 = (bf16[128,512]{1,0:T(8,128)(2,1)}, bf16[128,512]{1,0:T(8,128)(2,1)S(1)}, u32[]{:S(2)}, u32[]{:S(2)}) collective-permute-start(bf16[128,512]{1,0:T(8,128)(2,1)} %get-tuple-element.11), channel_id=1, source_target_pairs={{0,12},{4,8},{8,4},{12,0},{1,13},{5,9},{9,5},{13,1},{2,14},{6,10},... | collective-permute-start | bytes 393224 | tf_op jit(solution)/shard_map/ppermute | solution.py:12
  63.4 10.6 %collective-permute-start.8 = (bf16[128,512]{1,0:T(8,128)(2,1)}, bf16[128,512]{1,0:T(8,128)(2,1)S(1)}, u32[]{:S(2)}, u32[]{:S(2)}) collective-permute-start(bf16[128,512]{1,0:T(8,128)(2,1)} %get-tuple-element.12), channel_id=1, source_target_pairs={{0,8},{4,12},{8,0},{12,4},{1,9},{5,13},{9,1},{13,5},{2,10},{6,14},... | collective-permute-start | bytes 393224 | tf_op jit(solution)/shard_map/ppermute | solution.py:12
  63.4 10.6 %collective-permute-start.7 = (bf16[128,512]{1,0:T(8,128)(2,1)S(1)}, bf16[128,512]{1,0:T(8,128)(2,1)}, u32[]{:S(2)}, u32[]{:S(2)}) collective-permute-start(bf16[128,512]{1,0:T(8,128)(2,1)S(1)} %get-tuple-element.10), channel_id=1, source_target_pairs={{0,4},{4,0},{8,12},{12,8},{1,5},{5,1},{9,13},{13,9},{2,6},{6,2},{1... | collective-permute-start | bytes 393224 | tf_op jit(solution)/shard_map/ppermute | solution.py:12
  77.2 14.7 %collective-permute-start.10 = (bf16[128,512]{1,0:T(8,128)(2,1)S(1)}, bf16[128,512]{1,0:T(8,128)(2,1)S(1)}, u32[]{:S(2)}, u32[]{:S(2)}) collective-permute-start(bf16[128,512]{1,0:T(8,128)(2,1)S(1)} %get-tuple-element.5), channel_id=1, source_target_pairs={{0,2},{1,3},{2,0},{3,1},{4,6},{5,7},{6,4},{7,5},{8,10},{9,11},{10,... | collective-permute-start | bytes 393224 | tf_op jit(solution)/shard_map/ppermute | solution.py:12
  78.3 13.6 %collective-permute-start.13 = (bf16[128,512]{1,0:T(8,128)(2,1)S(1)}, bf16[128,512]{1,0:T(8,128)(2,1)S(1)}, u32[]{:S(2)}, u32[]{:S(2)}) collective-permute-start(bf16[128,512]{1,0:T(8,128)(2,1)S(1)} %get-tuple-element.5), channel_id=1, source_target_pairs={{0,4},{4,0},{8,12},{12,8},{1,5},{5,1},{9,13},{13,9},{2,6},{6,2},{1... | collective-permute-start | bytes 393224 | tf_op jit(solution)/shard_map/ppermute | solution.py:12
  83.5 57.4 %all-to-all-start = ((f32[4,128,512]{2,1,0:T(8,128)}), f32[4,128,512]{2,1,0:T(8,128)S(1)}, u32[]{:S(2)}, u32[]{:S(2)}) async-start(f32[4,128,512]{2,1,0:T(8,128)} %bitcast.95), calls=%async_computation | async-start | bytes 2097152 | tf_op jit(solution)/shard_map/all_to_all | solution.py:82
  87.2 7.1 %collective-permute-start.11 = (bf16[128,512]{1,0:T(8,128)(2,1)S(1)}, bf16[128,512]{1,0:T(8,128)(2,1)S(1)}, u32[]{:S(2)}, u32[]{:S(2)}) collective-permute-start(bf16[128,512]{1,0:T(8,128)(2,1)S(1)} %get-tuple-element.5), channel_id=1, source_target_pairs={{0,1},{1,0},{2,3},{3,2},{4,5},{5,4},{6,7},{7,6},{8,9},{9,8},{10,11... | collective-permute-start | bytes 393224 | tf_op jit(solution)/shard_map/ppermute | solution.py:12
  87.5 13.1 %collective-permute-start.17 = (bf16[128,512]{1,0:T(8,128)(2,1)S(1)}, bf16[128,512]{1,0:T(8,128)(2,1)S(1)}, u32[]{:S(2)}, u32[]{:S(2)}) collective-permute-start(bf16[128,512]{1,0:T(8,128)(2,1)S(1)} %get-tuple-element.5), channel_id=1, source_target_pairs={{0,8},{4,12},{8,0},{12,4},{1,9},{5,13},{9,1},{13,5},{2,10},{6,14},... | collective-permute-start | bytes 393224 | tf_op jit(solution)/shard_map/ppermute | solution.py:12
  90.7 12.3 %collective-permute-start.21 = (bf16[128,512]{1,0:T(8,128)(2,1)S(1)}, bf16[128,512]{1,0:T(8,128)(2,1)S(1)}, u32[]{:S(2)}, u32[]{:S(2)}) collective-permute-start(bf16[128,512]{1,0:T(8,128)(2,1)S(1)} %get-tuple-element.5), channel_id=1, source_target_pairs={{0,12},{4,8},{8,4},{12,0},{1,13},{5,9},{9,5},{13,1},{2,14},{6,10},... | collective-permute-start | bytes 393224 | tf_op jit(solution)/shard_map/ppermute | solution.py:12
  91.9 11.1 %collective-permute-start.12 = (bf16[128,512]{1,0:T(8,128)(2,1)S(1)}, bf16[128,512]{1,0:T(8,128)(2,1)S(1)}, u32[]{:S(2)}, u32[]{:S(2)}) collective-permute-start(bf16[128,512]{1,0:T(8,128)(2,1)S(1)} %collective-permute-done.10), channel_id=1, source_target_pairs={{0,1},{1,0},{2,3},{3,2},{4,5},{5,4},{6,7},{7,6},{8,9},{9,8},{10,11... | collective-permute-start | bytes 393224 | tf_op jit(solution)/shard_map/ppermute | solution.py:12
  91.9 12.8 %collective-permute-start.14 = (bf16[128,512]{1,0:T(8,128)(2,1)S(1)}, bf16[128,512]{1,0:T(8,128)(2,1)S(1)}, u32[]{:S(2)}, u32[]{:S(2)}) collective-permute-start(bf16[128,512]{1,0:T(8,128)(2,1)S(1)} %collective-permute-done.13), channel_id=1, source_target_pairs={{0,2},{1,3},{2,0},{3,1},{4,6},{5,7},{6,4},{7,5},{8,10},{9,11},{10,... | collective-permute-start | bytes 393224 | tf_op jit(solution)/shard_map/ppermute | solution.py:12
  94.3 11.2 %collective-permute-start.15 = (bf16[128,512]{1,0:T(8,128)(2,1)S(1)}, bf16[128,512]{1,0:T(8,128)(2,1)S(1)}, u32[]{:S(2)}, u32[]{:S(2)}) collective-permute-start(bf16[128,512]{1,0:T(8,128)(2,1)S(1)} %collective-permute-done.13), channel_id=1, source_target_pairs={{0,1},{1,0},{2,3},{3,2},{4,5},{5,4},{6,7},{7,6},{8,9},{9,8},{10,11... | collective-permute-start | bytes 393224 | tf_op jit(solution)/shard_map/ppermute | solution.py:12
  100.6 7.0 %collective-permute-start.18 = (bf16[128,512]{1,0:T(8,128)(2,1)S(1)}, bf16[128,512]{1,0:T(8,128)(2,1)S(1)}, u32[]{:S(2)}, u32[]{:S(2)}) collective-permute-start(bf16[128,512]{1,0:T(8,128)(2,1)S(1)} %collective-permute-done.17), channel_id=1, source_target_pairs={{0,2},{1,3},{2,0},{3,1},{4,6},{5,7},{6,4},{7,5},{8,10},{9,11},{10,... | collective-permute-start | bytes 393224 | tf_op jit(solution)/shard_map/ppermute | solution.py:12
  103.0 9.6 %collective-permute-start.19 = (bf16[128,512]{1,0:T(8,128)(2,1)S(1)}, bf16[128,512]{1,0:T(8,128)(2,1)S(1)}, u32[]{:S(2)}, u32[]{:S(2)}) collective-permute-start(bf16[128,512]{1,0:T(8,128)(2,1)S(1)} %collective-permute-done.17), channel_id=1, source_target_pairs={{0,1},{1,0},{2,3},{3,2},{4,5},{5,4},{6,7},{7,6},{8,9},{9,8},{10,11... | collective-permute-start | bytes 393224 | tf_op jit(solution)/shard_map/ppermute | solution.py:12
  103.0 6.9 %collective-permute-start.22 = (bf16[128,512]{1,0:T(8,128)(2,1)S(1)}, bf16[128,512]{1,0:T(8,128)(2,1)S(1)}, u32[]{:S(2)}, u32[]{:S(2)}) collective-permute-start(bf16[128,512]{1,0:T(8,128)(2,1)S(1)} %collective-permute-done.21), channel_id=1, source_target_pairs={{0,2},{1,3},{2,0},{3,1},{4,6},{5,7},{6,4},{7,5},{8,10},{9,11},{10,... | collective-permute-start | bytes 393224 | tf_op jit(solution)/shard_map/ppermute | solution.py:12
  104.7 10.5 %collective-permute-start.23 = (bf16[128,512]{1,0:T(8,128)(2,1)S(1)}, bf16[128,512]{1,0:T(8,128)(2,1)S(1)}, u32[]{:S(2)}, u32[]{:S(2)}) collective-permute-start(bf16[128,512]{1,0:T(8,128)(2,1)S(1)} %collective-permute-done.21), channel_id=1, source_target_pairs={{0,1},{1,0},{2,3},{3,2},{4,5},{5,4},{6,7},{7,6},{8,9},{9,8},{10,11... | collective-permute-start | bytes 393224 | tf_op jit(solution)/shard_map/ppermute | solution.py:12
  105.5 5.0 %collective-permute-start.16 = (bf16[128,512]{1,0:T(8,128)(2,1)S(1)}, bf16[128,512]{1,0:T(8,128)(2,1)S(1)}, u32[]{:S(2)}, u32[]{:S(2)}) collective-permute-start(bf16[128,512]{1,0:T(8,128)(2,1)S(1)} %collective-permute-done.14), channel_id=1, source_target_pairs={{0,1},{1,0},{2,3},{3,2},{4,5},{5,4},{6,7},{7,6},{8,9},{9,8},{10,11... | collective-permute-start | bytes 393224 | tf_op jit(solution)/shard_map/ppermute | solution.py:12
  107.6 5.7 %collective-permute-start.20 = (bf16[128,512]{1,0:T(8,128)(2,1)S(1)}, bf16[128,512]{1,0:T(8,128)(2,1)S(1)}, u32[]{:S(2)}, u32[]{:S(2)}) collective-permute-start(bf16[128,512]{1,0:T(8,128)(2,1)S(1)} %collective-permute-done.18), channel_id=1, source_target_pairs={{0,1},{1,0},{2,3},{3,2},{4,5},{5,4},{6,7},{7,6},{8,9},{9,8},{10,11... | collective-permute-start | bytes 393224 | tf_op jit(solution)/shard_map/ppermute | solution.py:12
  109.9 6.0 %collective-permute-start.24 = (bf16[128,512]{1,0:T(8,128)(2,1)S(1)}, bf16[128,512]{1,0:T(8,128)(2,1)S(1)}, u32[]{:S(2)}, u32[]{:S(2)}) collective-permute-start(bf16[128,512]{1,0:T(8,128)(2,1)S(1)} %collective-permute-done.22), channel_id=1, source_target_pairs={{0,1},{1,0},{2,3},{3,2},{4,5},{5,4},{6,7},{7,6},{8,9},{9,8},{10,11... | collective-permute-start | bytes 393224 | tf_op jit(solution)/shard_map/ppermute | solution.py:12

commit v2 on v1

v2 whole, which is shorter than its diff:
```python
import functools

import jax
import jax.numpy as jnp
from jax import lax
from jax.experimental import pallas as pl
from jax.experimental.pallas import tpu as pltpu
from jax.sharding import PartitionSpec as P

S = 512
BLK = 128
VMEM_LIMIT = 48 * 1024 * 1024
bf16 = jnp.bfloat16
f32 = jnp.float32


def swap(x, axis, distance):
    size = lax.axis_size(axis)
    return lax.ppermute(x, axis, [(i, i ^ distance) for i in range(size)])


def gather_z(m):
    size = lax.axis_size("prow")
    if size != 4:
        return [m] + [swap(m, "prow", d) for d in range(1, size)]
    level = lax.axis_index("prow")
    two = swap(m, "prow", 2)
    one = swap(m, "prow", 1)
    middle = lax.ppermute(m, "prow", [(1, 2), (2, 1)])
    ends = lax.ppermute(two, "prow", [(2, 3), (1, 0)])
    inner = (level == 1) | (level == 2)
    return [m, one, two, jnp.where(inner, middle, ends)]


def gather_col(a):
    size = lax.axis_size("pcol")
    across = {0: a}
    for e in range(2, size, 2):
        across[e] = swap(a, "pcol", e)
    for e in range(0, size, 2):
        across[e ^ 1] = swap(across[e], "pcol", 1)
    return [across[e] for e in range(size)]


def dot(a, b):
    return jnp.dot(a, b, preferred_element_type=f32)


def turn(m):
    width = m.shape[1] // 2
    return jnp.concatenate([-m[:, width:], m[:, :width]], axis=1)


def call(body, out_shape, scalars, operands, specs, out_specs, scratch=(), flops=0, aliases=None):
    return pl.pallas_call(
        body,
        out_shape=out_shape,
        grid_spec=pltpu.PrefetchScalarGridSpec(
            num_scalar_prefetch=1,
            grid=(1,),
            in_specs=specs,
            out_specs=out_specs,
            scratch_shapes=scratch,
        ),
        input_output_aliases=aliases or {},
        compiler_params=pltpu.CompilerParams(vmem_limit_bytes=VMEM_LIMIT),
        cost_estimate=pl.CostEstimate(flops=flops, bytes_accessed=4 << 20, transcendentals=0),
    )(scalars, *operands)


def whole(x):
    return pl.BlockSpec(x.shape, lambda i, ids, n=len(x.shape): (0,) * n)


def add_products(a_all, pieces, distances, ids):
    rows, wide = pieces[0].shape
    count = len(pieces)

    def body(ids_ref, *refs):
        total = None
        for a_ref, m_ref in zip(refs[:count], refs[count : 2 * count]):
            m = m_ref[...]
            term = dot(a_ref[0], m) + dot(a_ref[1], turn(m))
            total = term if total is None else total + term
        refs[-1][...] = total

    a_specs = [
        pl.BlockSpec((2, rows, rows), lambda i, ids, d=d: (0, 0, ids[0] ^ d)) for d in distances
    ]
    shape = jax.ShapeDtypeStruct((rows, wide), f32)
    return call(
        body,
        shape,
        ids,
        [a_all] * count + list(pieces),
        a_specs + [whole(m) for m in pieces],
        whole(shape),
        flops=4 * count * rows * rows * wide,
    )


def finish_products(a_all, piece, distance, total, side, ids, levels, columns):
    rows, wide = piece.shape
    cut = rows // columns
    share = S // levels

    def body(ids_ref, a_ref, m_ref, total_ref, side_ref, *refs):
        y_out = refs[:columns]
        p_out = refs[columns : columns + levels]
        y_ref, p_ref = refs[columns + levels :]
        m = m_ref[...]
        y_ref[...] = -(total_ref[...] + dot(a_ref[0], m) + dot(a_ref[1], turn(m)))
        chosen = y_ref[...].astype(bf16)
        p_ref[...] = dot(side_ref[0], chosen) + dot(side_ref[1], turn(chosen))
        for d in range(levels):
            start = pl.multiple_of((ids_ref[0] ^ d) * share, share)
            p_out[d][...] = p_ref[pl.ds(start, share), :].astype(p_out[d].dtype)
        for e in range(columns):
            start = pl.multiple_of((ids_ref[1] ^ e) * cut, cut)
            y_out[e][...] = y_ref[pl.ds(start, cut), :]

    shapes = [jax.ShapeDtypeStruct((cut, wide), f32)] * columns
    shapes += [jax.ShapeDtypeStruct((share, wide), f32 if d == 0 else bf16) for d in range(levels)]
    out = call(
        body,
        shapes,
        ids,
        [a_all, piece, total, side],
        [
            pl.BlockSpec((2, rows, rows), lambda i, ids: (0, 0, ids[0] ^ distance)),
            whole(piece),
            whole(total),
            whole(side),
        ],
        [whole(s) for s in shapes],
        [pltpu.VMEM((rows, wide), f32), pltpu.VMEM((S, wide), f32)],
        flops=4 * rows * wide * (rows + S),
    )
    return out[:columns], out[columns:]


def lay_rows(pieces, ids):
    cut, wide = pieces[0].shape
    width = wide // 2
    columns = len(pieces)

    def body(ids_ref, *refs):
        for e in range(columns):
            start = pl.multiple_of((ids_ref[1] ^ e) * width, width)
            for part in range(2):
                refs[-1][:, part, pl.ds(start, width)] = refs[e][:, part * width : (part + 1) * width]

    shape = jax.ShapeDtypeStruct((cut, 2, columns * width), f32)
    return call(body, shape, ids, pieces, [whole(p) for p in pieces], whole(shape))


def take_off(pivot, groups, flip, ids, rest=None):
    flat = [p for group in groups for p in group]
    share, wide = flat[0].shape
    width = wide // 2
    per_node = S // width
    levels = len(groups[0])

    def body(ids_ref, pivot_ref, *refs):
        out_ref = refs[-1]
        for n, ref in enumerate(refs[: len(flat)]):
            e, d = n // levels, n % levels
            top = pl.multiple_of((ids_ref[0] ^ d) * share, share)
            left = pl.multiple_of(((ids_ref[1] ^ e) % per_node) * width, width)
            for part in range(2):
                at = (0, part, pl.ds(top, share), pl.ds(left, width))
                out_ref[at] = pivot_ref[at] - ref[:, part * width : (part + 1) * width].astype(f32)

    spec = pl.BlockSpec((1, 2, S, S), lambda i, ids: (ids[2] ^ flip, 0, 0, 0))
    operands, specs, aliases = [pivot] + flat, [spec] + [whole(p) for p in flat], {}
    if rest is not None:
        operands, specs = operands + [rest], specs + [pl.BlockSpec(memory_space=pl.ANY)]
        aliases = {len(operands): 0}
    return call(
        body, jax.ShapeDtypeStruct(pivot.shape, f32), ids, operands, specs, spec, aliases=aliases
    )


def per_device(inverse_block, factor_column, block_pattern, pivot_inverse):
    levels = lax.axis_size("prow")
    level = lax.axis_index("prow")
    columns = lax.axis_size("pcol")
    column = lax.axis_index("pcol")
    rows = factor_column.shape[0]
    width = factor_column.shape[2] // columns
    per_node = S // width
    blocks = rows // BLK
    node = column // per_node
    ids = jnp.stack([level, column, node]).astype(jnp.int32)

    keep = lax.dynamic_index_in_dim(block_pattern, node, 0, keepdims=False).astype(bf16)
    keep = jnp.broadcast_to(keep[:, None], (blocks, BLK)).reshape(rows, 1, 1)
    own = lax.dynamic_slice_in_dim(factor_column, column * width, width, 2) * keep
    own = own.reshape(rows, 2 * width)
    m_pieces = gather_z(own)
    own, inverse_block = lax.optimization_barrier((own, inverse_block))
    a_pieces = gather_col(inverse_block)
    side = lax.dynamic_slice_in_dim(factor_column, node * S, S, 2) * keep
    side = jnp.transpose(side, (1, 2, 0))

    depth = inverse_block.shape[2]
    a_all = jnp.zeros((2, rows, depth * columns), bf16)
    for e, piece in enumerate(a_pieces):
        a_all = lax.dynamic_update_slice(a_all, piece, (0, 0, (column ^ e) * depth))
    total = add_products(a_all, m_pieces[:-1], range(levels - 1), ids)
    y_parts, p_parts = finish_products(
        a_all, m_pieces[-1], levels - 1, total, side, ids, levels, columns
    )

    sums = p_parts[0]
    for d in range(1, levels):
        sums = sums + swap(p_parts[d], "prow", d).astype(f32)
    sums = sums.astype(bf16)
    own_rows = lay_rows(
        [y_parts[0]] + [swap(y_parts[e], "pcol", e) for e in range(1, columns)], ids
    )

    pieces = [sums] + [swap(sums, "prow", d) for d in range(1, levels)]
    by_column = [gather_col(p) for p in pieces]
    groups = [[by_column[d][e] for d in range(levels)] for e in range(columns)]
    pivot = take_off(pivot_inverse, groups[:per_node], 0, ids)
    pivot = take_off(pivot_inverse, groups[per_node:], 1, ids, pivot)
    return own_rows, pivot


def solution(mesh):
    in_specs = (
        P(None, ("pole", "prow"), "pcol"),
        P(("pole", "prow"), None, None),
        P("pole", "prow"),
        P("pole", None, None, None),
    )
    out_specs = (P(("pole", "prow", "pcol"), None, None), P("pole", None, None, None))
    return jax.shard_map(
        per_device, mesh=mesh, in_specs=in_specs, out_specs=out_specs, check_vma=False
    )
```

time: 147 us -> 98.9 us (0.67)
  local copies, waits for them, and re-layouts: 52.5 us -> 10.2 us
  Pallas kernels: 0 us -> 13.7 us
  other arithmetic: 12.3 us -> 3.7 us
  matrix products: 4.45 us -> 0 us
  starting transfers between devices: 29 us -> 25.7 us
  waiting for transfers between devices: 47.3 us -> 44.5 us
    dynamic_update_slice x21 -> x4, local copies, waits for them, and re-layouts: 16.8 us -> 3.06 us  [per_device(): a_all = lax.dynamic_update_slice(a_all, piece, (0, 0, (column ^ e) * depth))]
    pallas_call x0 -> x5, Pallas kernels: none -> 13.7 us  [call(): pl.pallas_call(body, out_shape=out_shape, grid_spec=pltpu.PrefetchScalarG...]
    convert_element_type x3 -> x0, local copies, waits for them, and re-layouts: 13.4 us -> none  [the longest x2 12.7 us: per_device(): return (own_rows, pivot_inverse - minus.astype(jnp.float32))]
    ppermute x23 -> x26, waiting for transfers between devices: 40.7 us -> 33.6 us  [swap(): return lax.ppermute(x, axis, [(i, i ^ distance) for i in range(size)])]
    sub x1 -> x0, other arithmetic: 6.44 us -> none  [per_device(): return (own_rows, pivot_inverse - minus.astype(jnp.float32))]
    unnamed x6 -> x10, local copies, waits for them, and re-layouts: 10.5 us -> 4.58 us
    reshape x3 -> x0, local copies, waits for them, and re-layouts: 5.39 us -> none  [the longest x2 3.52 us: per_device(): y_all.reshape(columns, cut, 2, width)]
    dot_general x4 -> x0, matrix products: 4.45 us -> none  [the longest x2 3.52 us: per_device(): dot = lambda a, b: jnp.dot(a, b, preferred_element_type=jnp.float32)]
  transfers between devices with their start and end apart: 26 -> 28, of which waited for: 8 -> 10; matrix products, arithmetic and copies ran while one was open for 38% -> 8% of each run, Pallas kernels for 0% -> 4%
where the time goes in v2:
time: 98.9 us; the launch traced here: 98.6 us
  waiting for transfers between devices  44.5 us (45%)
  starting transfers between devices  25.7 us (26%)
  Pallas kernels  13.7 us (14%)
  local copies, waits for them, and re-layouts  10.2 us (10%)
  other arithmetic  3.7 us (4%)
    ppermute x26, waiting for transfers between devices, swap(): return lax.ppermute(x, axis, [(i, i ^ distance) for i in range(size)])  33.6 us
    ppermute x26, starting transfers between devices, swap(): return lax.ppermute(x, axis, [(i, i ^ distance) for i in range(size)])  23.7 us
    pallas_call x5, Pallas kernels, call(): pl.pallas_call(body, out_shape=out_shape, grid_spec=pltpu.PrefetchScalarG...  13.7 us
    ppermute x1, waiting for transfers between devices, gather_z(): ends = lax.ppermute(two, 'prow', [(2, 3), (1, 0)])  10.9 us
    unnamed x10, local copies, waits for them, and re-layouts  4.58 us
    dynamic_update_slice x4, local copies, waits for them, and re-layouts, per_device(): a_all = lax.dynamic_update_slice(a_all, piece, (0, 0, (column ^ e) * depth))  3.06 us
    mul x1, other arithmetic, per_device(): lax.dynamic_slice_in_dim(factor_column, column * width, width, 2) * keep  2.73 us
  transfers between devices with their start and end apart: 28, of which 10 were waited for; matrix products, arithmetic and copies ran while one was open for 8% of the time, Pallas kernels for 4%

profile of v2, /device:TPU:0, one launch (start us, length us, event | category | flops | bytes accessed | tf_op | source)
XLA Modules:
  0.0 98.6 jit_solution(5157582650068851886)
XLA Ops:
  0.6 0.7 fusion.1
  1.3 0.1 broadcast_bitcast_fusion
  1.4 2.7 %dynamic-slice_multiply_fusion = bf16[512,2,256]{2,1,0:T(2,128)(2,1)S(1)} fusion(bf16[512,2,1024]{2,1,0:T(2,128)(2,1)} %param.5, s32[]{:T(128)S(6)} %select_n.36, bf16[512]{0:T(512)(128)(2,1)S(1)} %broadcast_bitcast_fusion), kind=kLoop, calls=%fused_computation.1 | loop fusion | flops 1048576 | bytes 1049604 | tf_op jit(solution)/shard_map/mul | solution.py:198
  4.1 0.1 copy.9
  4.2 3.0 %collective-permute-start.1 = (bf16[2,512,512]{2,1,0:T(8,128)(2,1)}, bf16[2,512,512]{2,1,0:T(8,128)(2,1)}, u32[]{:S(2)}, u32[]{:S(2)}) collective-permute-start(bf16[2,512,512]{2,1,0:T(8,128)(2,1)} %param.4), channel_id=1, source_target_pairs={{0,2},{1,3},{2,0},{3,1},{4,6},{5,7},{6,4},{7,5},{8,10},{9,11},{10,... | collective-permute-start | bytes 3145736 | tf_op jit(solution)/shard_map/ppermute | solution.py:19
  7.2 2.6 %collective-permute-start.4 = (bf16[512,512]{1,0:T(8,128)(2,1)S(1)}, bf16[512,512]{1,0:T(8,128)(2,1)S(1)}, u32[]{:S(2)}, u32[]{:S(2)}) collective-permute-start(bf16[512,512]{1,0:T(8,128)(2,1)S(1)} %bitcast.11), channel_id=1, source_target_pairs={{0,8},{4,12},{8,0},{12,4},{1,9},{5,13},{9,1},{13,5},{2,10},{6,14},... | collective-permute-start | bytes 1572872 | tf_op jit(solution)/shard_map/ppermute | solution.py:19
  9.8 0.7 collective-permute-start.3
  10.5 2.9 %collective-permute-start.6 = (bf16[512,512]{1,0:T(8,128)(2,1)S(1)}, bf16[512,512]{1,0:T(8,128)(2,1)S(1)}, u32[]{:S(2)}, u32[]{:S(2)}) collective-permute-start(bf16[512,512]{1,0:T(8,128)(2,1)S(1)} %bitcast.13), channel_id=1, source_target_pairs={{0,4},{4,0},{8,12},{12,8},{1,5},{5,1},{9,13},{13,9},{2,6},{6,2},{1... | collective-permute-start | bytes 1572872 | tf_op jit(solution)/shard_map/ppermute | solution.py:19
  13.4 1.9 %constant_dynamic-slice_fusion = bf16[512,2,512]{2,1,0:T(2,128)(2,1)S(1)} fusion(bf16[512,2,1024]{2,1,0:T(2,128)(2,1)} %param.5, s32[]{:T(128)S(6)} %select_n.44), kind=kLoop, calls=%fused_computation.4 | loop fusion | bytes 2097156 | tf_op jit(solution)/shard_map/dynamic_slice | solution.py:203
  15.3 2.5 %copy.8 = bf16[512,2,512]{0,2,1:T(8,128)(2,1)} copy(bf16[512,2,512]{2,1,0:T(2,128)(2,1)S(1)} %constant_dynamic-slice_fusion) | data formatting | bytes 2097152
  17.8 12.9 %collective-permute-done.1 = bf16[2,512,512]{2,1,0:T(8,128)(2,1)} collective-permute-done((bf16[2,512,512]{2,1,0:T(8,128)(2,1)}, bf16[2,512,512]{2,1,0:T(8,128)(2,1)}, u32[]{:S(2)}, u32[]{:S(2)}) %collective-permute-start.1) | collective-permute-done | bytes 1048608 | tf_op jit(solution)/shard_map/ppermute | solution.py:19
  30.7 0.1 pad_add_fusion.ids_ref
  30.8 0.5 broadcast_in_dim.4
  31.3 0.2 constant_dynamic-update-slice_fusion.3
  31.5 2.6 %collective-permute-done.4.refs_5_ = bf16[512,512]{1,0:T(8,128)(2,1)S(1)} collective-permute-done((bf16[512,512]{1,0:T(8,128)(2,1)S(1)}, bf16[512,512]{1,0:T(8,128)(2,1)S(1)}, u32[]{:S(2)}, u32[]{:S(2)}) %collective-permute-start.4) | collective-permute-done | bytes 524320 | tf_op jit(solution)/shard_map/ppermute | solution.py:19
  34.1 1.3 %collective-permute-start.5 = (bf16[512,512]{1,0:T(8,128)(2,1)S(1)}, bf16[512,512]{1,0:T(8,128)(2,1)S(1)}, u32[]{:S(2)}, u32[]{:S(2)}) collective-permute-start(bf16[512,512]{1,0:T(8,128)(2,1)S(1)} %collective-permute-done.4.refs_5_), channel_id=1, source_target_pairs={{8,12},{4,0},{9,13},{5,1},{10,14},{6,2},{11,15},{7,3},{24,28},{20,... | collective-permute-start | bytes 1572872 | tf_op jit(solution)/shard_map/ppermute | solution.py:30
  35.4 0.1 multiply_bitcast_fusion.side_ref
  35.5 0.0 collective-permute-done
  35.5 1.4 %constant_dynamic-update-slice_fusion.2 = bf16[2,512,2048]{2,1,0:T(8,128)(2,1)S(1)} fusion(bf16[2,512,2048]{2,1,0:T(8,128)(2,1)S(1)} %constant_dynamic-update-slice_fusion.3, bf16[2,512,512]{2,1,0:T(8,128)(2,1)} %collective-permute-done, s32[]{:T(128)S(6)} %select_n.39), kind=kLoop, calls=%fused_computation.7 | loop fusion | bytes 2097156 | tf_op jit(solution)/shard_map/dynamic_update_slice | solution.py:209
  36.9 1.4 %constant_dynamic-update-slice_fusion.1 = bf16[2,512,2048]{2,1,0:T(8,128)(2,1)S(1)} fusion(bf16[2,512,2048]{2,1,0:T(8,128)(2,1)S(1)} %constant_dynamic-update-slice_fusion.2, bf16[2,512,512]{2,1,0:T(8,128)(2,1)} %collective-permute-done.1, s32[]{:T(128)S(6)} %select_n.40), kind=kLoop, calls=%fused_computation.6 | loop fusion | bytes 2097156 | tf_op jit(solution)/shard_map/dynamic_update_slice | solution.py:209
  38.3 0.0 collective-permute-done.3
  38.3 10.9 %collective-permute-done.5 = bf16[512,512]{1,0:T(8,128)(2,1)S(1)} collective-permute-done((bf16[512,512]{1,0:T(8,128)(2,1)S(1)}, bf16[512,512]{1,0:T(8,128)(2,1)S(1)}, u32[]{:S(2)}, u32[]{:S(2)}) %collective-permute-start.5) | collective-permute-done | bytes 524320 | tf_op jit(solution)/shard_map/ppermute | solution.py:30
  49.2 0.1 broadcast_select_fusion.m_ref
  49.3 0.0 collective-permute-done.2
  49.3 0.2 constant_dynamic-update-slice_fusion.refs_0_.refs_1_.refs_2_.a_ref
  49.5 0.0 copy-start.1
  49.5 0.0 collective-permute-done.6.refs_4_
  49.5 2.0 %copy-done.1 = bf16[2,512,2048]{2,1,0:T(8,128)(2,1)} copy-done((bf16[2,512,2048]{2,1,0:T(8,128)(2,1)}, bf16[2,512,2048]{2,1,0:T(8,128)(2,1)S(1)}, u32[]{:S(2)}) %copy-start.1) | copy-done | bytes 4194328
  51.5 4.2 %shard_map.59.total_ref = f32[512,512]{1,0:T(8,128)S(1)} custom-call(s32[3]{0:T(128)S(1)} %pad_add_fusion.ids_ref, bf16[2,512,2048]{2,1,0:T(8,128)(2,1)} %copy-done.1, bf16[2,512,2048]{2,1,0:T(8,128)(2,1)} %copy-done.1, bf16[2,512,2048]{2,1,0:T(8,128)(2,1)} %copy-done.1, bf16[512,512]{1,0:T(8,128)(2,1)S(1)} %bitcast.14, ...), custom_call_target="tpu_custom_call" | custom-call | flops 1610612736 | bytes 4194304 | tf_op jit(solution)/shard_map/pallas_call | solution.py:55
  55.7 0.0 copy-start
  55.7 3.5 %shard_map.60 = (f32[128,512]{1,0:T(8,128)S(1)}, f32[128,512]{1,0:T(8,128)S(1)}, f32[128,512]{1,0:T(8,128)S(1)}, f32[128,512]{1,0:T(8,128)S(1)}, f32[128,512]{1,...) custom-call(s32[3]{0:T(128)S(1)} %pad_add_fusion.ids_ref, ...), custom_call_target="tpu_custom_call" | custom-call | flops 1073741824 | bytes 4194304 | tf_op jit(solution)/shard_map/pallas_call | solution.py:55
  59.2 3.9 %collective-permute-start.12 = (bf16[128,512]{1,0:T(8,128)(2,1)S(1)}, bf16[128,512]{1,0:T(8,128)(2,1)S(1)}, u32[]{:S(2)}, u32[]{:S(2)}) collective-permute-start(bf16[128,512]{1,0:T(8,128)(2,1)S(1)} %get-tuple-element.19), channel_id=1, source_target_pairs={{0,12},{4,8},{8,4},{12,0},{1,13},{5,9},{9,5},{13,1},{2,14},{6,10},... | collective-permute-start | bytes 393224 | tf_op jit(solution)/shard_map/ppermute | solution.py:19
  63.1 0.0 collective-permute-start.11
  63.1 0.6 collective-permute-start.10
  63.7 0.0 collective-permute-start.7
  63.7 0.6 collective-permute-start.8
  64.3 3.2 %collective-permute-done.12 = bf16[128,512]{1,0:T(8,128)(2,1)S(1)} collective-permute-done((bf16[128,512]{1,0:T(8,128)(2,1)S(1)}, bf16[128,512]{1,0:T(8,128)(2,1)S(1)}, u32[]{:S(2)}, u32[]{:S(2)}) %collective-permute-start.12) | collective-permute-done | bytes 131104 | tf_op jit(solution)/shard_map/ppermute | solution.py:19
  67.5 5.0 %collective-permute-done.11 = bf16[128,512]{1,0:T(8,128)(2,1)S(1)} collective-permute-done((bf16[128,512]{1,0:T(8,128)(2,1)S(1)}, bf16[128,512]{1,0:T(8,128)(2,1)S(1)}, u32[]{:S(2)}, u32[]{:S(2)}) %collective-permute-start.11) | collective-permute-done | bytes 131104 | tf_op jit(solution)/shard_map/ppermute | solution.py:19
  72.6 0.1 add_convert_fusion.refs_0_
  72.6 0.8 collective-permute-start.14
  73.5 2.7 %collective-permute-start.16 = (bf16[128,512]{1,0:T(8,128)(2,1)S(1)}, bf16[128,512]{1,0:T(8,128)(2,1)S(1)}, u32[]{:S(2)}, u32[]{:S(2)}) collective-permute-start(bf16[128,512]{1,0:T(8,128)(2,1)S(1)} %add_convert_fusion.refs_0_), channel_id=1, source_target_pairs={{0,8},{4,12},{8,0},{12,4},{1,9},{5,13},{9,1},{13,5},{2,10},{6,14},... | collective-permute-start | bytes 393224 | tf_op jit(solution)/shard_map/ppermute | solution.py:19
  76.2 0.9 collective-permute-start.18
  77.1 0.0 collective-permute-done.8.refs_2_
  77.1 0.5 collective-permute-start.13
  77.6 0.1 collective-permute-done.9.refs_3_
  77.7 0.5 collective-permute-start.24
  78.2 0.8 collective-permute-done.14.refs_1_
  79.0 1.5 %collective-permute-start.15 = (bf16[128,512]{1,0:T(8,128)(2,1)S(1)}, bf16[128,512]{1,0:T(8,128)(2,1)S(1)}, u32[]{:S(2)}, u32[]{:S(2)}) collective-permute-start(bf16[128,512]{1,0:T(8,128)(2,1)S(1)} %collective-permute-done.14.refs_1_), channel_id=1, source_target_pairs={{0,2},{1,3},{2,0},{3,1},{4,6},{5,7},{6,4},{7,5},{8,10},{9,11},{10,... | collective-permute-start | bytes 393224 | tf_op jit(solution)/shard_map/ppermute | solution.py:19
  80.5 5.1 %collective-permute-done.16.refs_2_ = bf16[128,512]{1,0:T(8,128)(2,1)S(1)} collective-permute-done((bf16[128,512]{1,0:T(8,128)(2,1)S(1)}, bf16[128,512]{1,0:T(8,128)(2,1)S(1)}, u32[]{:S(2)}, u32[]{:S(2)}) %collective-permute-start.16) | collective-permute-done | bytes 131104 | tf_op jit(solution)/shard_map/ppermute | solution.py:19
  85.6 0.9 collective-permute-start.17
  86.6 1.1 %collective-permute-start.19 = (bf16[128,512]{1,0:T(8,128)(2,1)S(1)}, bf16[128,512]{1,0:T(8,128)(2,1)S(1)}, u32[]{:S(2)}, u32[]{:S(2)}) collective-permute-start(bf16[128,512]{1,0:T(8,128)(2,1)S(1)} %collective-permute-done.18.refs_3_), channel_id=1, source_target_pairs={{0,2},{1,3},{2,0},{3,1},{4,6},{5,7},{6,4},{7,5},{8,10},{9,11},{10,... | collective-permute-start | bytes 393224 | tf_op jit(solution)/shard_map/ppermute | solution.py:19
  87.7 0.0 collective-permute-start.25
  87.7 0.0 collective-permute-done.24.refs_4_
  87.7 0.5 collective-permute-start.26
  88.2 0.1 collective-permute-start.27
  88.3 2.3 %collective-permute-done.17.refs_2_ = bf16[128,512]{1,0:T(8,128)(2,1)S(1)} collective-permute-done((bf16[128,512]{1,0:T(8,128)(2,1)S(1)}, bf16[128,512]{1,0:T(8,128)(2,1)S(1)}, u32[]{:S(2)}, u32[]{:S(2)}) %collective-permute-start.17) | collective-permute-done | bytes 131104 | tf_op jit(solution)/shard_map/ppermute | solution.py:19
  90.6 0.0 collective-permute-start.20
  90.6 1.4 %collective-permute-done.19.refs_3_ = bf16[128,512]{1,0:T(8,128)(2,1)S(1)} collective-permute-done((bf16[128,512]{1,0:T(8,128)(2,1)S(1)}, bf16[128,512]{1,0:T(8,128)(2,1)S(1)}, u32[]{:S(2)}, u32[]{:S(2)}) %collective-permute-start.19) | collective-permute-done | bytes 131104 | tf_op jit(solution)/shard_map/ppermute | solution.py:19
  92.0 0.5 collective-permute-start.22
  92.5 0.1 collective-permute-start.23
  92.6 1.9 %shard_map.61 = f32[128,2,1024]{2,1,0:T(2,128)} custom-call(s32[3]{0:T(128)S(1)} %pad_add_fusion.ids_ref, f32[128,512]{1,0:T(8,128)S(1)} %get-tuple-element.12.refs_0_, f32[128,512]{1,0:T(8,128)S(1)} %collective-permute-done.7.refs_1_, f32[128,512]{1,0:T(8,128)S(1)} %collective-permute-done.8.refs_2_, f32[128,512]{1,0:T(8,128)S(1)} %collective-permute-done.9.refs_3_), custom_call_target="tpu_custom_call" | custom-call | bytes 4194304 | tf_op jit(solution)/shard_map/pallas_call | solution.py:55
  94.5 2.1 %shard_map.62.refs_8_ = f32[2,2,512,512]{3,2,1,0:T(8,128)} custom-call(s32[3]{0:T(128)S(1)} %pad_add_fusion.ids_ref, f32[2,2,512,512]{3,2,1,0:T(8,128)S(1)} %copy-done, bf16[128,512]{1,0:T(8,128)(2,1)S(1)} %add_convert_fusion.refs_0_, bf16[128,512]{1,0:T(8,128)(2,1)S(1)} %collective-permute-done.14.refs_1_, ...), custom_call_target="tpu_custom_call" | custom-call | bytes 4194304 | tf_op jit(solution)/shard_map/pallas_call | solution.py:55
  96.5 0.0 collective-permute-done.20.refs_4_
  96.5 2.1 %shard_map.63 = f32[2,2,512,512]{3,2,1,0:T(8,128)} custom-call(s32[3]{0:T(128)S(1)} %pad_add_fusion.ids_ref, f32[2,2,512,512]{3,2,1,0:T(8,128)S(1)} %copy-done, bf16[128,512]{1,0:T(8,128)(2,1)S(1)} %collective-permute-done.13.refs_0_, bf16[128,512]{1,0:T(8,128)(2,1)S(1)} %collective-permute-done.15.refs_1_, ...), custom_call_target="tpu_custom_call", output_to_operand_aliasing={{}: (10, {})} | custom-call | bytes 4194304 | tf_op jit(solution)/shard_map/pallas_call | solution.py:55
  (20 shorter events, 0.0 us)
Async XLA Ops:
  4.2 26.5 %collective-permute-start.1 = (bf16[2,512,512]{2,1,0:T(8,128)(2,1)}, bf16[2,512,512]{2,1,0:T(8,128)(2,1)}, u32[]{:S(2)}, u32[]{:S(2)}) collective-permute-start(bf16[2,512,512]{2,1,0:T(8,128)(2,1)} %param.4), channel_id=1, source_target_pairs={{0,2},{1,3},{2,0},{3,1},{4,6},{5,7},{6,4},{7,5},{8,10},{9,11},{10,... | collective-permute-start | bytes 3145736 | tf_op jit(solution)/shard_map/ppermute | solution.py:19
  7.2 28.3 %collective-permute-start = (bf16[2,512,512]{2,1,0:T(8,128)(2,1)}, bf16[2,512,512]{2,1,0:T(8,128)(2,1)}, u32[]{:S(2)}, u32[]{:S(2)}) collective-permute-start(bf16[2,512,512]{2,1,0:T(8,128)(2,1)} %param.4), channel_id=1, source_target_pairs={{0,1},{1,0},{2,3},{3,2},{4,5},{5,4},{6,7},{7,6},{8,9},{9,8},{10,11... | collective-permute-start | bytes 3145736 | tf_op jit(solution)/shard_map/ppermute | solution.py:19
  7.2 26.9 %collective-permute-start.4 = (bf16[512,512]{1,0:T(8,128)(2,1)S(1)}, bf16[512,512]{1,0:T(8,128)(2,1)S(1)}, u32[]{:S(2)}, u32[]{:S(2)}) collective-permute-start(bf16[512,512]{1,0:T(8,128)(2,1)S(1)} %bitcast.11), channel_id=1, source_target_pairs={{0,8},{4,12},{8,0},{12,4},{1,9},{5,13},{9,1},{13,5},{2,10},{6,14},... | collective-permute-start | bytes 1572872 | tf_op jit(solution)/shard_map/ppermute | solution.py:19
  9.8 28.5 %collective-permute-start.3 = (bf16[512,512]{1,0:T(8,128)(2,1)S(1)}, bf16[512,512]{1,0:T(8,128)(2,1)S(1)}, u32[]{:S(2)}, u32[]{:S(2)}) collective-permute-start(bf16[512,512]{1,0:T(8,128)(2,1)S(1)} %bitcast.12), channel_id=1, source_target_pairs={{4,8},{8,4},{5,9},{9,5},{6,10},{10,6},{7,11},{11,7},{20,24},{24,20... | collective-permute-start | bytes 1572872 | tf_op jit(solution)/shard_map/ppermute | solution.py:29
  10.5 38.9 %collective-permute-start.6 = (bf16[512,512]{1,0:T(8,128)(2,1)S(1)}, bf16[512,512]{1,0:T(8,128)(2,1)S(1)}, u32[]{:S(2)}, u32[]{:S(2)}) collective-permute-start(bf16[512,512]{1,0:T(8,128)(2,1)S(1)} %bitcast.13), channel_id=1, source_target_pairs={{0,4},{4,0},{8,12},{12,8},{1,5},{5,1},{9,13},{13,9},{2,6},{6,2},{1... | collective-permute-start | bytes 1572872 | tf_op jit(solution)/shard_map/ppermute | solution.py:19
  17.8 17.6 %copy-start.2 = (bf16[512,2,512]{0,2,1:T(8,128)(2,1)S(1)}, bf16[512,2,512]{0,2,1:T(8,128)(2,1)}, u32[]{:S(2)}) copy-start(bf16[512,2,512]{0,2,1:T(8,128)(2,1)} %copy.8) | copy-start | bytes 3145732
  17.8 13.5 %copy-start.3 = (bf16[2,512,512]{2,1,0:T(8,128)(2,1)S(1)}, bf16[2,512,512]{2,1,0:T(8,128)(2,1)}, u32[]{:S(2)}) copy-start(bf16[2,512,512]{2,1,0:T(8,128)(2,1)} %param.4) | copy-start | bytes 3145732
  30.7 18.6 %collective-permute-start.2 = (bf16[2,512,512]{2,1,0:T(8,128)(2,1)}, bf16[2,512,512]{2,1,0:T(8,128)(2,1)S(1)}, u32[]{:S(2)}, u32[]{:S(2)}) collective-permute-start(bf16[2,512,512]{2,1,0:T(8,128)(2,1)} %collective-permute-done.1), channel_id=1, source_target_pairs={{0,1},{1,0},{2,3},{3,2},{4,5},{5,4},{6,7},{7,6},{8,9},{9,8},{10,11... | collective-permute-start | bytes 3145736 | tf_op jit(solution)/shard_map/ppermute | solution.py:19
  34.1 15.1 %collective-permute-start.5 = (bf16[512,512]{1,0:T(8,128)(2,1)S(1)}, bf16[512,512]{1,0:T(8,128)(2,1)S(1)}, u32[]{:S(2)}, u32[]{:S(2)}) collective-permute-start(bf16[512,512]{1,0:T(8,128)(2,1)S(1)} %collective-permute-done.4.refs_5_), channel_id=1, source_target_pairs={{8,12},{4,0},{9,13},{5,1},{10,14},{6,2},{11,15},{7,3},{24,28},{20,... | collective-permute-start | bytes 1572872 | tf_op jit(solution)/shard_map/ppermute | solution.py:30
  49.5 2.0 %copy-start.1 = (bf16[2,512,2048]{2,1,0:T(8,128)(2,1)}, bf16[2,512,2048]{2,1,0:T(8,128)(2,1)S(1)}, u32[]{:S(2)}) copy-start(bf16[2,512,2048]{2,1,0:T(8,128)(2,1)S(1)} %constant_dynamic-update-slice_fusion.refs_0_.refs_1_.refs_2_.a_ref) | copy-start | bytes 12582916
  55.7 38.8 %copy-start = (f32[2,2,512,512]{3,2,1,0:T(8,128)S(1)}, f32[2,2,512,512]{3,2,1,0:T(8,128)}, u32[]{:S(2)}) copy-start(f32[2,2,512,512]{3,2,1,0:T(8,128)} %pivot_ref.3) | copy-start | bytes 12582916
  59.2 8.3 %collective-permute-start.12 = (bf16[128,512]{1,0:T(8,128)(2,1)S(1)}, bf16[128,512]{1,0:T(8,128)(2,1)S(1)}, u32[]{:S(2)}, u32[]{:S(2)}) collective-permute-start(bf16[128,512]{1,0:T(8,128)(2,1)S(1)} %get-tuple-element.19), channel_id=1, source_target_pairs={{0,12},{4,8},{8,4},{12,0},{1,13},{5,9},{9,5},{13,1},{2,14},{6,10},... | collective-permute-start | bytes 393224 | tf_op jit(solution)/shard_map/ppermute | solution.py:19
  63.1 9.5 %collective-permute-start.11 = (bf16[128,512]{1,0:T(8,128)(2,1)S(1)}, bf16[128,512]{1,0:T(8,128)(2,1)S(1)}, u32[]{:S(2)}, u32[]{:S(2)}) collective-permute-start(bf16[128,512]{1,0:T(8,128)(2,1)S(1)} %get-tuple-element.18), channel_id=1, source_target_pairs={{0,8},{4,12},{8,0},{12,4},{1,9},{5,13},{9,1},{13,5},{2,10},{6,14},... | collective-permute-start | bytes 393224 | tf_op jit(solution)/shard_map/ppermute | solution.py:19
  63.1 9.5 %collective-permute-start.10 = (bf16[128,512]{1,0:T(8,128)(2,1)S(1)}, bf16[128,512]{1,0:T(8,128)(2,1)S(1)}, u32[]{:S(2)}, u32[]{:S(2)}) collective-permute-start(bf16[128,512]{1,0:T(8,128)(2,1)S(1)} %get-tuple-element.17), channel_id=1, source_target_pairs={{0,4},{4,0},{8,12},{12,8},{1,5},{5,1},{9,13},{13,9},{2,6},{6,2},{1... | collective-permute-start | bytes 393224 | tf_op jit(solution)/shard_map/ppermute | solution.py:19
  63.7 12.4 %collective-permute-start.7 = (f32[128,512]{1,0:T(8,128)S(1)}, f32[128,512]{1,0:T(8,128)S(1)}, u32[]{:S(2)}, u32[]{:S(2)}) collective-permute-start(f32[128,512]{1,0:T(8,128)S(1)} %get-tuple-element.13), channel_id=1, source_target_pairs={{0,1},{1,0},{2,3},{3,2},{4,5},{5,4},{6,7},{7,6},{8,9},{9,8},{10,11... | collective-permute-start | bytes 786440 | tf_op jit(solution)/shard_map/ppermute | solution.py:19
  63.7 13.4 %collective-permute-start.8 = (f32[128,512]{1,0:T(8,128)S(1)}, f32[128,512]{1,0:T(8,128)S(1)}, u32[]{:S(2)}, u32[]{:S(2)}) collective-permute-start(f32[128,512]{1,0:T(8,128)S(1)} %get-tuple-element.14), channel_id=1, source_target_pairs={{0,2},{1,3},{2,0},{3,1},{4,6},{5,7},{6,4},{7,5},{8,10},{9,11},{10,... | collective-permute-start | bytes 786440 | tf_op jit(solution)/shard_map/ppermute | solution.py:19
  67.5 10.2 %collective-permute-start.9 = (f32[128,512]{1,0:T(8,128)S(1)}, f32[128,512]{1,0:T(8,128)S(1)}, u32[]{:S(2)}, u32[]{:S(2)}) collective-permute-start(f32[128,512]{1,0:T(8,128)S(1)} %get-tuple-element.15), channel_id=1, source_target_pairs={{0,3},{1,2},{2,1},{3,0},{4,7},{5,6},{6,5},{7,4},{8,11},{9,10},{10,... | collective-permute-start | bytes 786440 | tf_op jit(solution)/shard_map/ppermute | solution.py:19
  72.6 6.4 %collective-permute-start.14 = (bf16[128,512]{1,0:T(8,128)(2,1)S(1)}, bf16[128,512]{1,0:T(8,128)(2,1)S(1)}, u32[]{:S(2)}, u32[]{:S(2)}) collective-permute-start(bf16[128,512]{1,0:T(8,128)(2,1)S(1)} %add_convert_fusion.refs_0_), channel_id=1, source_target_pairs={{0,4},{4,0},{8,12},{12,8},{1,5},{5,1},{9,13},{13,9},{2,6},{6,2},{1... | collective-permute-start | bytes 393224 | tf_op jit(solution)/shard_map/ppermute | solution.py:19
  73.5 12.2 %collective-permute-start.16 = (bf16[128,512]{1,0:T(8,128)(2,1)S(1)}, bf16[128,512]{1,0:T(8,128)(2,1)S(1)}, u32[]{:S(2)}, u32[]{:S(2)}) collective-permute-start(bf16[128,512]{1,0:T(8,128)(2,1)S(1)} %add_convert_fusion.refs_0_), channel_id=1, source_target_pairs={{0,8},{4,12},{8,0},{12,4},{1,9},{5,13},{9,1},{13,5},{2,10},{6,14},... | collective-permute-start | bytes 393224 | tf_op jit(solution)/shard_map/ppermute | solution.py:19
  76.2 10.4 %collective-permute-start.18 = (bf16[128,512]{1,0:T(8,128)(2,1)S(1)}, bf16[128,512]{1,0:T(8,128)(2,1)S(1)}, u32[]{:S(2)}, u32[]{:S(2)}) collective-permute-start(bf16[128,512]{1,0:T(8,128)(2,1)S(1)} %add_convert_fusion.refs_0_), channel_id=1, source_target_pairs={{0,12},{4,8},{8,4},{12,0},{1,13},{5,9},{9,5},{13,1},{2,14},{6,10},... | collective-permute-start | bytes 393224 | tf_op jit(solution)/shard_map/ppermute | solution.py:19
  77.1 10.6 %collective-permute-start.13 = (bf16[128,512]{1,0:T(8,128)(2,1)S(1)}, bf16[128,512]{1,0:T(8,128)(2,1)S(1)}, u32[]{:S(2)}, u32[]{:S(2)}) collective-permute-start(bf16[128,512]{1,0:T(8,128)(2,1)S(1)} %add_convert_fusion.refs_0_), channel_id=1, source_target_pairs={{0,2},{1,3},{2,0},{3,1},{4,6},{5,7},{6,4},{7,5},{8,10},{9,11},{10,... | collective-permute-start | bytes 393224 | tf_op jit(solution)/shard_map/ppermute | solution.py:19
  77.7 10.0 %collective-permute-start.24 = (bf16[128,512]{1,0:T(8,128)(2,1)S(1)}, bf16[128,512]{1,0:T(8,128)(2,1)S(1)}, u32[]{:S(2)}, u32[]{:S(2)}) collective-permute-start(bf16[128,512]{1,0:T(8,128)(2,1)S(1)} %add_convert_fusion.refs_0_), channel_id=1, source_target_pairs={{0,1},{1,0},{2,3},{3,2},{4,5},{5,4},{6,7},{7,6},{8,9},{9,8},{10,11... | collective-permute-start | bytes 393224 | tf_op jit(solution)/shard_map/ppermute | solution.py:19
  79.0 9.1 %collective-permute-start.15 = (bf16[128,512]{1,0:T(8,128)(2,1)S(1)}, bf16[128,512]{1,0:T(8,128)(2,1)S(1)}, u32[]{:S(2)}, u32[]{:S(2)}) collective-permute-start(bf16[128,512]{1,0:T(8,128)(2,1)S(1)} %collective-permute-done.14.refs_1_), channel_id=1, source_target_pairs={{0,2},{1,3},{2,0},{3,1},{4,6},{5,7},{6,4},{7,5},{8,10},{9,11},{10,... | collective-permute-start | bytes 393224 | tf_op jit(solution)/shard_map/ppermute | solution.py:19
  85.6 5.0 %collective-permute-start.17 = (bf16[128,512]{1,0:T(8,128)(2,1)S(1)}, bf16[128,512]{1,0:T(8,128)(2,1)S(1)}, u32[]{:S(2)}, u32[]{:S(2)}) collective-permute-start(bf16[128,512]{1,0:T(8,128)(2,1)S(1)} %collective-permute-done.16.refs_2_), channel_id=1, source_target_pairs={{0,2},{1,3},{2,0},{3,1},{4,6},{5,7},{6,4},{7,5},{8,10},{9,11},{10,... | collective-permute-start | bytes 393224 | tf_op jit(solution)/shard_map/ppermute | solution.py:19
  86.6 5.5 %collective-permute-start.19 = (bf16[128,512]{1,0:T(8,128)(2,1)S(1)}, bf16[128,512]{1,0:T(8,128)(2,1)S(1)}, u32[]{:S(2)}, u32[]{:S(2)}) collective-permute-start(bf16[128,512]{1,0:T(8,128)(2,1)S(1)} %collective-permute-done.18.refs_3_), channel_id=1, source_target_pairs={{0,2},{1,3},{2,0},{3,1},{4,6},{5,7},{6,4},{7,5},{8,10},{9,11},{10,... | collective-permute-start | bytes 393224 | tf_op jit(solution)/shard_map/ppermute | solution.py:19
  87.7 4.3 %collective-permute-start.25 = (bf16[128,512]{1,0:T(8,128)(2,1)S(1)}, bf16[128,512]{1,0:T(8,128)(2,1)S(1)}, u32[]{:S(2)}, u32[]{:S(2)}) collective-permute-start(bf16[128,512]{1,0:T(8,128)(2,1)S(1)} %collective-permute-done.14.refs_1_), channel_id=1, source_target_pairs={{0,1},{1,0},{2,3},{3,2},{4,5},{5,4},{6,7},{7,6},{8,9},{9,8},{10,11... | collective-permute-start | bytes 393224 | tf_op jit(solution)/shard_map/ppermute | solution.py:19
  87.7 4.8 %collective-permute-start.26 = (bf16[128,512]{1,0:T(8,128)(2,1)S(1)}, bf16[128,512]{1,0:T(8,128)(2,1)S(1)}, u32[]{:S(2)}, u32[]{:S(2)}) collective-permute-start(bf16[128,512]{1,0:T(8,128)(2,1)S(1)} %collective-permute-done.16.refs_2_), channel_id=1, source_target_pairs={{0,1},{1,0},{2,3},{3,2},{4,5},{5,4},{6,7},{7,6},{8,9},{9,8},{10,11... | collective-permute-start | bytes 393224 | tf_op jit(solution)/shard_map/ppermute | solution.py:19
  88.2 6.3 %collective-permute-start.27 = (bf16[128,512]{1,0:T(8,128)(2,1)S(1)}, bf16[128,512]{1,0:T(8,128)(2,1)S(1)}, u32[]{:S(2)}, u32[]{:S(2)}) collective-permute-start(bf16[128,512]{1,0:T(8,128)(2,1)S(1)} %collective-permute-done.18.refs_3_), channel_id=1, source_target_pairs={{0,1},{1,0},{2,3},{3,2},{4,5},{5,4},{6,7},{7,6},{8,9},{9,8},{10,11... | collective-permute-start | bytes 393224 | tf_op jit(solution)/shard_map/ppermute | solution.py:19
  90.6 5.9 %collective-permute-start.20 = (bf16[128,512]{1,0:T(8,128)(2,1)S(1)}, bf16[128,512]{1,0:T(8,128)(2,1)S(1)}, u32[]{:S(2)}, u32[]{:S(2)}) collective-permute-start(bf16[128,512]{1,0:T(8,128)(2,1)S(1)} %collective-permute-done.13.refs_0_), channel_id=1, source_target_pairs={{0,1},{1,0},{2,3},{3,2},{4,5},{5,4},{6,7},{7,6},{8,9},{9,8},{10,11... | collective-permute-start | bytes 393224 | tf_op jit(solution)/shard_map/ppermute | solution.py:19
  92.0 4.5 %collective-permute-start.21 = (bf16[128,512]{1,0:T(8,128)(2,1)S(1)}, bf16[128,512]{1,0:T(8,128)(2,1)S(1)}, u32[]{:S(2)}, u32[]{:S(2)}) collective-permute-start(bf16[128,512]{1,0:T(8,128)(2,1)S(1)} %collective-permute-done.15.refs_1_), channel_id=1, source_target_pairs={{0,1},{1,0},{2,3},{3,2},{4,5},{5,4},{6,7},{7,6},{8,9},{9,8},{10,11... | collective-permute-start | bytes 393224 | tf_op jit(solution)/shard_map/ppermute | solution.py:19
  92.0 4.5 %collective-permute-start.22 = (bf16[128,512]{1,0:T(8,128)(2,1)S(1)}, bf16[128,512]{1,0:T(8,128)(2,1)S(1)}, u32[]{:S(2)}, u32[]{:S(2)}) collective-permute-start(bf16[128,512]{1,0:T(8,128)(2,1)S(1)} %collective-permute-done.17.refs_2_), channel_id=1, source_target_pairs={{0,1},{1,0},{2,3},{3,2},{4,5},{5,4},{6,7},{7,6},{8,9},{9,8},{10,11... | collective-permute-start | bytes 393224 | tf_op jit(solution)/shard_map/ppermute | solution.py:19
  92.5 4.0 %collective-permute-start.23 = (bf16[128,512]{1,0:T(8,128)(2,1)S(1)}, bf16[128,512]{1,0:T(8,128)(2,1)S(1)}, u32[]{:S(2)}, u32[]{:S(2)}) collective-permute-start(bf16[128,512]{1,0:T(8,128)(2,1)S(1)} %collective-permute-done.19.refs_3_), channel_id=1, source_target_pairs={{0,1},{1,0},{2,3},{3,2},{4,5},{5,4},{6,7},{7,6},{8,9},{9,8},{10,11... | collective-permute-start | bytes 393224 | tf_op jit(solution)/shard_map/ppermute | solution.py:19

commit v3 on v2

v3 whole, which is shorter than its diff:
```python
import functools

import jax
import jax.numpy as jnp
from jax import lax
from jax.experimental import pallas as pl
from jax.experimental.pallas import tpu as pltpu
from jax.sharding import PartitionSpec as P

S = 512
BLK = 128
COST = 1 << 16
VMEM_LIMIT = 48 * 1024 * 1024
bf16 = jnp.bfloat16
f32 = jnp.float32


def swap(x, axis, distance):
    size = lax.axis_size(axis)
    return lax.ppermute(x, axis, [(i, i ^ distance) for i in range(size)])


def gather_z(m, beside):
    size = lax.axis_size("prow")
    pieces = {0: m}
    step = size // 2
    while step > 1:
        pieces |= {d ^ step: swap(p, "prow", step) for d, p in pieces.items()}
        step //= 2
    far = pieces.copy()
    pieces |= {d ^ 1: swap(p, "prow", 1) for d, p in far.items() if d != size - 2}
    pieces, beside = lax.optimization_barrier((pieces, beside))
    last = swap(pieces[size - 2], "prow", 1)
    return [pieces[d] for d in range(size - 1)], last, beside


def gather_x(a):
    size = lax.axis_size("pcol")
    return {e: swap(a, "pcol", e) for e in range(2, size, 2)}


def gather_core(a):
    return [p for e in sorted(a) for p in (a[e], swap(a[e], "pcol", 1))]


def dot(a, b):
    return jnp.dot(a, b, preferred_element_type=f32)


def turn(m):
    width = m.shape[1] // 2
    return jnp.concatenate([-m[:, width:], m[:, :width]], axis=1)


def call(body, out_shape, scalars, operands, specs, out_specs, scratch=(), aliases=None):
    return pl.pallas_call(
        body,
        out_shape=out_shape,
        grid_spec=pltpu.PrefetchScalarGridSpec(
            num_scalar_prefetch=1,
            grid=(1,),
            in_specs=specs,
            out_specs=out_specs,
            scratch_shapes=scratch,
        ),
        input_output_aliases=aliases or {},
        compiler_params=pltpu.CompilerParams(vmem_limit_bytes=VMEM_LIMIT),
        cost_estimate=pl.CostEstimate(flops=0, bytes_accessed=COST, transcendentals=0),
    )(scalars, *operands)


def whole(x):
    return pl.BlockSpec(x.shape, lambda i, ids, n=len(x.shape): (0,) * n)


def add_products(a_pieces, m_pieces, ids, levels):
    rows, wide = m_pieces[0].shape
    columns = len(a_pieces)
    per = levels // columns

    def body(ids_ref, *refs):
        a_refs, m_refs = refs[:columns], refs[columns : columns + levels - 1]
        total_ref, left_ref, m_all = refs[columns + levels - 1 :]
        missing = ids_ref[0] ^ (levels - 1)
        for d, m_ref in enumerate(m_refs):
            m_all[ids_ref[0] ^ d] = m_ref[...]
        total_ref[...] = jnp.zeros_like(total_ref)
        for e, a_ref in enumerate(a_refs):
            for n in range(per):
                at = (ids_ref[1] ^ e) * per + n
                cut = slice(n * rows, (n + 1) * rows)

                @pl.when(at != missing)
                def _():
                    m = m_all[at]
                    total_ref[...] += dot(a_ref[0, :, cut], m) + dot(a_ref[1, :, cut], turn(m))

                @pl.when(at == missing)
                def _():
                    left_ref[...] = a_ref[:, :, cut]

    shapes = [jax.ShapeDtypeStruct((rows, wide), f32), jax.ShapeDtypeStruct((2, rows, rows), bf16)]
    return call(
        body,
        shapes,
        ids,
        list(a_pieces) + list(m_pieces),
        [whole(x) for x in a_pieces] + [whole(m) for m in m_pieces],
        [whole(x) for x in shapes],
        [pltpu.VMEM((levels, rows, wide), bf16)],
    )


def finish_products(left, last, total, side, ids, levels, columns):
    rows, wide = last.shape
    cut = rows // columns
    share = S // levels

    def body(ids_ref, a_ref, m_ref, total_ref, side_ref, *refs):
        y_out = refs[:columns]
        p_out = refs[columns : columns + levels]
        y_ref, p_ref = refs[columns + levels :]
        m = m_ref[...]
        y_ref[...] = -(total_ref[...] + dot(a_ref[0], m) + dot(a_ref[1], turn(m)))
        chosen = y_ref[...].astype(bf16)
        p_ref[...] = dot(side_ref[0], chosen) + dot(side_ref[1], turn(chosen))
        for d in range(levels):
            start = pl.multiple_of((ids_ref[0] ^ d) * share, share)
            p_out[d][...] = p_ref[pl.ds(start, share), :].astype(p_out[d].dtype)
        for e in range(columns):
            start = pl.multiple_of((ids_ref[1] ^ e) * cut, cut)
            y_out[e][...] = y_ref[pl.ds(start, cut), :]

    shapes = [jax.ShapeDtypeStruct((cut, wide), f32)] * columns
    shapes += [jax.ShapeDtypeStruct((share, wide), f32 if d == 0 else bf16) for d in range(levels)]
    out = call(
        body,
        shapes,
        ids,
        [left, last, total, side],
        [whole(x) for x in (left, last, total, side)],
        [whole(s) for s in shapes],
        [pltpu.VMEM((rows, wide), f32), pltpu.VMEM((S, wide), f32)],
    )
    return out[:columns], out[columns:]


def lay_rows(pieces, ids):
    cut, wide = pieces[0].shape
    width = wide // 2
    columns = len(pieces)

    def body(ids_ref, *refs):
        for e in range(columns):
            start = pl.multiple_of((ids_ref[1] ^ e) * width, width)
            for part in range(2):
                refs[-1][:, part, pl.ds(start, width)] = refs[e][:, part * width : (part + 1) * width]

    shape = jax.ShapeDtypeStruct((cut, 2, columns * width), f32)
    return call(body, shape, ids, pieces, [whole(p) for p in pieces], whole(shape))


def take_off(pivot, groups, flip, ids, rest=None):
    flat = [p for group in groups for p in group]
    wide = flat[0].shape[1]
    width = wide // 2
    per_node = S // width
    share = flat[0].shape[0]

    def body(ids_ref, pivot_ref, *refs):
        out_ref = refs[-1]
        n = 0
        for e, group in enumerate(groups):
            left = pl.multiple_of(((ids_ref[1] ^ e) % per_node) * width, width)
            d = 0
            for stack in group:
                for start in range(0, stack.shape[0], share):
                    top = pl.multiple_of((ids_ref[0] ^ d) * share, share)
                    for part in range(2):
                        at = (0, part, pl.ds(top, share), pl.ds(left, width))
                        piece = refs[n][start : start + share, part * width : (part + 1) * width]
                        out_ref[at] = pivot_ref[at] - piece.astype(f32)
                    d += 1
                n += 1

    spec = pl.BlockSpec((1, 2, S, S), lambda i, ids: (ids[2] ^ flip, 0, 0, 0))
    operands, specs, aliases = [pivot] + flat, [spec] + [whole(p) for p in flat], {}
    if rest is not None:
        operands, specs = operands + [rest], specs + [pl.BlockSpec(memory_space=pl.ANY)]
        aliases = {len(operands): 0}
    return call(
        body, jax.ShapeDtypeStruct(pivot.shape, f32), ids, operands, specs, spec, aliases=aliases
    )


def per_device(inverse_block, factor_column, block_pattern, pivot_inverse):
    levels = lax.axis_size("prow")
    level = lax.axis_index("prow")
    columns = lax.axis_size("pcol")
    column = lax.axis_index("pcol")
    rows = factor_column.shape[0]
    width = factor_column.shape[2] // columns
    per_node = S // width
    blocks = rows // BLK
    node = column // per_node
    ids = jnp.stack([level, column, node]).astype(jnp.int32)

    keep = lax.dynamic_index_in_dim(block_pattern, node, 0, keepdims=False).astype(bf16)
    keep = jnp.broadcast_to(keep[:, None], (blocks, BLK)).reshape(rows, 1, 1)
    own = lax.dynamic_slice_in_dim(factor_column, column * width, width, 2) * keep
    own = own.reshape(rows, 2 * width)
    own, inverse_block = lax.optimization_barrier((own, inverse_block))
    side = lax.dynamic_slice_in_dim(factor_column, node * S, S, 2) * keep
    side = jnp.transpose(side, (1, 2, 0))
    m_pieces, last, (a_across, side) = gather_z(own, (gather_x(inverse_block), side))
    a_pieces = gather_core({0: inverse_block} | a_across)
    total, left = add_products(a_pieces, m_pieces, ids, levels)
    y_parts, p_parts = finish_products(left, last, total, side, ids, levels, columns)

    sums = p_parts[0]
    for d in range(1, levels):
        sums = sums + swap(p_parts[d], "prow", d).astype(f32)
    sums = sums.astype(bf16)
    own_rows = lay_rows(
        [y_parts[0]] + [swap(y_parts[e], "pcol", e) for e in range(1, columns)], ids
    )

    half = levels // 2
    early = [sums] + [swap(sums, "prow", d) for d in range(1, half)]
    late = [swap(sums, "prow", d) for d in range(half, levels)]
    early_across = [gather_x(p) for p in early]
    late, early_across, own_rows = lax.optimization_barrier((late, early_across, own_rows))
    late = [jnp.concatenate(late, 0)]
    late_across = [gather_x(p) for p in late]
    near = [gather_core({0: p}) for p in early + late]
    near = [[g[e] for g in near] for e in range(2)]
    if per_node == 2:
        pivot = take_off(pivot_inverse, near, 0, ids)
        late_across, pivot = lax.optimization_barrier((late_across, pivot))
    there = [gather_core(a) for a in early_across + late_across]
    groups = near + [[g[e] for g in there] for e in range(columns - 2)]
    if per_node != 2:
        pivot = take_off(pivot_inverse, groups[:per_node], 0, ids)
    pivot = take_off(pivot_inverse, groups[per_node:], 1, ids, pivot)
    return own_rows, pivot


def solution(mesh):
    in_specs = (
        P(None, ("pole", "prow"), "pcol"),
        P(("pole", "prow"), None, None),
        P("pole", "prow"),
        P("pole", None, None, None),
    )
    out_specs = (P(("pole", "prow", "pcol"), None, None), P("pole", None, None, None))
    return jax.shard_map(
        per_device, mesh=mesh, in_specs=in_specs, out_specs=out_specs, check_vma=False
    )
```

time: 98.9 us -> 93.3 us (0.943)
  local copies, waits for them, and re-layouts: 10.2 us -> 4.61 us
  starting transfers between devices: 25.7 us -> 21.3 us
  waiting for transfers between devices: 44.5 us -> 47.5 us
  other arithmetic: 3.7 us -> 4.94 us
    ppermute x26 -> x24, waiting for transfers between devices: 33.6 us -> 47.5 us  [swap(): return lax.ppermute(x, axis, [(i, i ^ distance) for i in range(size)])]
    ppermute x2 -> x0, waiting for transfers between devices: 10.9 us -> none  [the longest x1 10.9 us: gather_z(): ends = lax.ppermute(two, 'prow', [(2, 3), (1, 0)])]
    dynamic_update_slice x4 -> x0, local copies, waits for them, and re-layouts: 3.06 us -> none  [per_device(): a_all = lax.dynamic_update_slice(a_all, piece, (0, 0, (column ^ e) * depth))]
    ppermute x26 -> x24, starting transfers between devices: 23.7 us -> 21.3 us  [swap(): return lax.ppermute(x, axis, [(i, i ^ distance) for i in range(size)])]
    unnamed x10 -> x7, local copies, waits for them, and re-layouts: 4.58 us -> 2.58 us
    ppermute x2 -> x0, starting transfers between devices: 1.96 us -> none  [the longest x1 1.28 us: gather_z(): ends = lax.ppermute(two, 'prow', [(2, 3), (1, 0)])]
    transpose x1, other arithmetic: 0.07 us -> 1.3 us  [per_device(): side = jnp.transpose(side, (1, 2, 0))]
  transfers between devices with their start and end apart: 28 -> 24, of which waited for: 10 -> 15; matrix products, arithmetic and copies ran while one was open for 8% -> 6% of each run, Pallas kernels for 4% -> 10%
where the time goes in v3:
time: 93.3 us; the launch traced here: 93 us
  waiting for transfers between devices  47.5 us (51%)
  starting transfers between devices  21.3 us (23%)
  Pallas kernels  13.9 us (15%)
  other arithmetic  4.94 us (5%)
  local copies, waits for them, and re-layouts  4.61 us (5%)
    ppermute x24, waiting for transfers between devices, swap(): return lax.ppermute(x, axis, [(i, i ^ distance) for i in range(size)])  47.5 us
    ppermute x24, starting transfers between devices, swap(): return lax.ppermute(x, axis, [(i, i ^ distance) for i in range(size)])  21.3 us
    pallas_call x5, Pallas kernels, call(): pl.pallas_call(body, out_shape=out_shape, grid_spec=pltpu.PrefetchScalarG...  13.9 us
    mul x1, other arithmetic, per_device(): lax.dynamic_slice_in_dim(factor_column, column * width, width, 2) * keep  2.82 us
    unnamed x7, local copies, waits for them, and re-layouts  2.58 us
    dynamic_slice x1, local copies, waits for them, and re-layouts, per_device(): side = lax.dynamic_slice_in_dim(factor_column, node * S, S, 2) * keep  1.94 us
  transfers between devices with their start and end apart: 24, of which 15 were waited for; matrix products, arithmetic and copies ran while one was open for 6% of the time, Pallas kernels for 10%

profile of v3, /device:TPU:0, one launch (start us, length us, event | category | flops | bytes accessed | tf_op | source)
XLA Modules:
  0.0 93.0 jit_solution(1618528265150843209)
XLA Ops:
  0.6 0.7 fusion.1
  1.3 0.1 broadcast_bitcast_fusion
  1.4 2.8 %dynamic-slice_multiply_fusion = bf16[512,2,256]{2,1,0:T(2,128)(2,1)S(1)} fusion(bf16[512,2,1024]{2,1,0:T(2,128)(2,1)} %param.5, s32[]{:T(128)S(6)} %select_n.16, bf16[512]{0:T(512)(128)(2,1)S(1)} %broadcast_bitcast_fusion), kind=kLoop, calls=%fused_computation.1 | loop fusion | flops 1048576 | bytes 1049604 | tf_op jit(solution)/shard_map/mul | solution.py:210
  4.2 0.1 copy.9
  4.3 3.0 %collective-permute-start.3 = (bf16[2,512,512]{2,1,0:T(8,128)(2,1)}, bf16[2,512,512]{2,1,0:T(8,128)(2,1)}, u32[]{:S(2)}, u32[]{:S(2)}) collective-permute-start(bf16[2,512,512]{2,1,0:T(8,128)(2,1)} %refs_0_), channel_id=1, source_target_pairs={{0,2},{1,3},{2,0},{3,1},{4,6},{5,7},{6,4},{7,5},{8,10},{9,11},{10,... | collective-permute-start | bytes 3145736 | tf_op jit(solution)/shard_map/ppermute | solution.py:20
  7.3 2.6 %collective-permute-start.2 = (bf16[512,512]{1,0:T(8,128)(2,1)S(1)}, bf16[512,512]{1,0:T(8,128)(2,1)S(1)}, u32[]{:S(2)}, u32[]{:S(2)}) collective-permute-start(bf16[512,512]{1,0:T(8,128)(2,1)S(1)} %bitcast.11), channel_id=1, source_target_pairs={{0,8},{4,12},{8,0},{12,4},{1,9},{5,13},{9,1},{13,5},{2,10},{6,14},... | collective-permute-start | bytes 1572872 | tf_op jit(solution)/shard_map/ppermute | solution.py:20
  9.9 1.6 %collective-permute-start.1 = (bf16[512,512]{1,0:T(8,128)(2,1)S(1)}, bf16[512,512]{1,0:T(8,128)(2,1)}, u32[]{:S(2)}, u32[]{:S(2)}) collective-permute-start(bf16[512,512]{1,0:T(8,128)(2,1)S(1)} %bitcast.12), channel_id=1, source_target_pairs={{0,4},{4,0},{8,12},{12,8},{1,5},{5,1},{9,13},{13,9},{2,6},{6,2},{1... | collective-permute-start | bytes 1572872 | tf_op jit(solution)/shard_map/ppermute | solution.py:20
  11.5 0.0 collective-permute-start
  11.5 1.9 %constant_dynamic-slice_fusion = bf16[512,2,512]{2,1,0:T(2,128)(2,1)S(1)} fusion(bf16[512,2,1024]{2,1,0:T(2,128)(2,1)} %param.5, s32[]{:T(128)S(6)} %select_n.18), kind=kLoop, calls=%fused_computation.5 | loop fusion | bytes 2097156 | tf_op jit(solution)/shard_map/dynamic_slice | solution.py:213
  13.5 2.5 %copy.8 = bf16[512,2,512]{0,2,1:T(8,128)(2,1)} copy(bf16[512,2,512]{2,1,0:T(2,128)(2,1)S(1)} %constant_dynamic-slice_fusion) | data formatting | bytes 2097152
  15.9 1.3 %multiply_bitcast_fusion.side_ref = bf16[2,512,512]{2,1,0:T(8,128)(2,1)S(1)} fusion(bf16[512,2,512]{0,2,1:T(8,128)(2,1)} %copy.8, bf16[512]{0:T(512)(128)(2,1)S(1)} %broadcast_bitcast_fusion), kind=kLoop, calls=%fused_computation | loop fusion | flops 524288 | bytes 2098176 | tf_op jit(solution)/shard_map/transpose | solution.py:214
  17.2 15.7 %collective-permute-done.2.refs_6_ = bf16[512,512]{1,0:T(8,128)(2,1)S(1)} collective-permute-done((bf16[512,512]{1,0:T(8,128)(2,1)S(1)}, bf16[512,512]{1,0:T(8,128)(2,1)S(1)}, u32[]{:S(2)}, u32[]{:S(2)}) %collective-permute-start.2) | collective-permute-done | bytes 524320 | tf_op jit(solution)/shard_map/ppermute | solution.py:20
  33.0 0.3 collective-permute-done.1.refs_5_
  33.3 0.0 collective-permute-done.3.refs_2_
  33.3 0.0 collective-permute-start.4
  33.3 1.4 %collective-permute-start.5 = (bf16[512,512]{1,0:T(8,128)(2,1)S(1)}, bf16[512,512]{1,0:T(8,128)(2,1)}, u32[]{:S(2)}, u32[]{:S(2)}) collective-permute-start(bf16[512,512]{1,0:T(8,128)(2,1)S(1)} %collective-permute-done.2.refs_6_), channel_id=1, source_target_pairs={{0,4},{4,0},{8,12},{12,8},{1,5},{5,1},{9,13},{13,9},{2,6},{6,2},{1... | collective-permute-start | bytes 1572872 | tf_op jit(solution)/shard_map/ppermute | solution.py:20
  34.7 0.1 pad_add_fusion.ids_ref
  34.8 0.0 collective-permute-done.refs_1_
  34.8 1.5 %collective-permute-done.4.refs_3_ = bf16[2,512,512]{2,1,0:T(8,128)(2,1)} collective-permute-done((bf16[2,512,512]{2,1,0:T(8,128)(2,1)}, bf16[2,512,512]{2,1,0:T(8,128)(2,1)}, u32[]{:S(2)}, u32[]{:S(2)}) %collective-permute-start.4) | collective-permute-done | bytes 1048608 | tf_op jit(solution)/shard_map/ppermute | solution.py:20
  36.3 0.0 copy-done.1
  36.3 4.9 %shard_map.59 = (f32[512,512]{1,0:T(8,128)S(1)}, bf16[2,512,512]{2,1,0:T(8,128)(2,1)S(1)}) custom-call(s32[3]{0:T(128)S(1)} %pad_add_fusion.ids_ref, bf16[2,512,512]{2,1,0:T(8,128)(2,1)S(1)} %copy-done.1, bf16[2,512,512]{2,1,0:T(8,128)(2,1)} %collective-permute-done.refs_1_, bf16[2,512,512]{2,1,0:T(8,128)(2,1)} %collective-permute-done.3.refs_2_, ...), custom_call_target="tpu_custom_call" | custom-call | bytes 65536 | tf_op jit(solution)/shard_map/pallas_call | solution.py:56
  41.2 0.0 copy-start
  41.2 6.5 %collective-permute-done.5.m_ref = bf16[512,512]{1,0:T(8,128)(2,1)} collective-permute-done((bf16[512,512]{1,0:T(8,128)(2,1)S(1)}, bf16[512,512]{1,0:T(8,128)(2,1)}, u32[]{:S(2)}, u32[]{:S(2)}) %collective-permute-start.5) | collective-permute-done | bytes 524320 | tf_op jit(solution)/shard_map/ppermute | solution.py:20
  47.7 3.0 %shard_map.60 = (f32[128,512]{1,0:T(8,128)S(1)}, f32[128,512]{1,0:T(8,128)S(1)}, f32[128,512]{1,0:T(8,128)S(1)}, f32[128,512]{1,0:T(8,128)S(1)}, f32[128,512]{1,...) custom-call(s32[3]{0:T(128)S(1)} %pad_add_fusion.ids_ref, ...), custom_call_target="tpu_custom_call" | custom-call | bytes 65536 | tf_op jit(solution)/shard_map/pallas_call | solution.py:56
  50.7 1.5 %collective-permute-start.6 = (bf16[128,512]{1,0:T(8,128)(2,1)S(1)}, bf16[128,512]{1,0:T(8,128)(2,1)S(1)}, u32[]{:S(2)}, u32[]{:S(2)}) collective-permute-start(bf16[128,512]{1,0:T(8,128)(2,1)S(1)} %get-tuple-element.36), channel_id=1, source_target_pairs={{0,4},{4,0},{8,12},{12,8},{1,5},{5,1},{9,13},{13,9},{2,6},{6,2},{1... | collective-permute-start | bytes 393224 | tf_op jit(solution)/shard_map/ppermute | solution.py:20
  52.2 2.2 %collective-permute-start.7 = (bf16[128,512]{1,0:T(8,128)(2,1)S(1)}, bf16[128,512]{1,0:T(8,128)(2,1)S(1)}, u32[]{:S(2)}, u32[]{:S(2)}) collective-permute-start(bf16[128,512]{1,0:T(8,128)(2,1)S(1)} %get-tuple-element.37), channel_id=1, source_target_pairs={{0,8},{4,12},{8,0},{12,4},{1,9},{5,13},{9,1},{13,5},{2,10},{6,14},... | collective-permute-start | bytes 393224 | tf_op jit(solution)/shard_map/ppermute | solution.py:20
  54.4 0.7 collective-permute-start.8
  55.2 0.0 collective-permute-start.14
  55.2 0.5 collective-permute-start.15
  55.6 1.8 %collective-permute-done.6 = bf16[128,512]{1,0:T(8,128)(2,1)S(1)} collective-permute-done((bf16[128,512]{1,0:T(8,128)(2,1)S(1)}, bf16[128,512]{1,0:T(8,128)(2,1)S(1)}, u32[]{:S(2)}, u32[]{:S(2)}) %collective-permute-start.6) | collective-permute-done | bytes 131104 | tf_op jit(solution)/shard_map/ppermute | solution.py:20
  57.5 0.0 collective-permute-start.16
  57.5 7.5 %collective-permute-done.7 = bf16[128,512]{1,0:T(8,128)(2,1)S(1)} collective-permute-done((bf16[128,512]{1,0:T(8,128)(2,1)S(1)}, bf16[128,512]{1,0:T(8,128)(2,1)S(1)}, u32[]{:S(2)}, u32[]{:S(2)}) %collective-permute-start.7) | collective-permute-done | bytes 131104 | tf_op jit(solution)/shard_map/ppermute | solution.py:20
  65.0 0.0 collective-permute-done.8
  65.0 0.1 add_convert_fusion.refs_0_
  65.0 2.1 %collective-permute-start.12 = (bf16[128,512]{1,0:T(8,128)(2,1)S(1)}, bf16[128,512]{1,0:T(8,128)(2,1)S(1)}, u32[]{:S(2)}, u32[]{:S(2)}) collective-permute-start(bf16[128,512]{1,0:T(8,128)(2,1)S(1)} %add_convert_fusion.refs_0_), channel_id=1, source_target_pairs={{0,4},{4,0},{8,12},{12,8},{1,5},{5,1},{9,13},{13,9},{2,6},{6,2},{1... | collective-permute-start | bytes 393224 | tf_op jit(solution)/shard_map/ppermute | solution.py:20
  67.1 0.5 collective-permute-start.11
  67.7 0.0 collective-permute-done.14.refs_1_
  67.7 2.0 %collective-permute-start.10 = (bf16[128,512]{1,0:T(8,128)(2,1)S(1)}, bf16[128,512]{1,0:T(8,128)(2,1)S(1)}, u32[]{:S(2)}, u32[]{:S(2)}) collective-permute-start(bf16[128,512]{1,0:T(8,128)(2,1)S(1)} %add_convert_fusion.refs_0_), channel_id=1, source_target_pairs={{0,12},{4,8},{8,4},{12,0},{1,13},{5,9},{9,5},{13,1},{2,14},{6,10},... | collective-permute-start | bytes 393224 | tf_op jit(solution)/shard_map/ppermute | solution.py:20
  69.7 0.0 collective-permute-done.15.refs_2_
  69.7 0.0 collective-permute-start.9
  69.7 1.3 %collective-permute-done.12.refs_1_ = bf16[128,512]{1,0:T(8,128)(2,1)S(1)} collective-permute-done((bf16[128,512]{1,0:T(8,128)(2,1)S(1)}, bf16[128,512]{1,0:T(8,128)(2,1)S(1)}, u32[]{:S(2)}, u32[]{:S(2)}) %collective-permute-start.12) | collective-permute-done | bytes 131104 | tf_op jit(solution)/shard_map/ppermute | solution.py:20
  71.0 0.2 collective-permute-start.13
  71.3 0.0 collective-permute-done.16.refs_3_
  71.3 1.9 %shard_map.61 = f32[128,2,1024]{2,1,0:T(2,128)} custom-call(s32[3]{0:T(128)S(1)} %pad_add_fusion.ids_ref, f32[128,512]{1,0:T(8,128)S(1)} %get-tuple-element.39.refs_0_, f32[128,512]{1,0:T(8,128)S(1)} %collective-permute-done.14.refs_1_, f32[128,512]{1,0:T(8,128)S(1)} %collective-permute-done.15.refs_2_, f32[128,512]{1,0:T(8,128)S(1)} %collective-permute-done.16.refs_3_), custom_call_target="tpu_custom_call" | custom-call | bytes 65536 | tf_op jit(solution)/shard_map/pallas_call | solution.py:56
  73.1 0.4 collective-permute-done.11.refs_0_
  73.6 2.4 %collective-permute-done.10 = bf16[128,512]{1,0:T(8,128)(2,1)S(1)} collective-permute-done((bf16[128,512]{1,0:T(8,128)(2,1)S(1)}, bf16[128,512]{1,0:T(8,128)(2,1)S(1)}, u32[]{:S(2)}, u32[]{:S(2)}) %collective-permute-start.10) | collective-permute-done | bytes 131104 | tf_op jit(solution)/shard_map/ppermute | solution.py:20
  76.0 4.2 %collective-permute-done.9 = bf16[128,512]{1,0:T(8,128)(2,1)S(1)} collective-permute-done((bf16[128,512]{1,0:T(8,128)(2,1)S(1)}, bf16[128,512]{1,0:T(8,128)(2,1)S(1)}, u32[]{:S(2)}, u32[]{:S(2)}) %collective-permute-start.9) | collective-permute-done | bytes 131104 | tf_op jit(solution)/shard_map/ppermute | solution.py:20
  80.2 0.0 collective-permute-done.13.refs_1_
  80.2 0.1 collective-permute-start.20
  80.3 1.7 %collective-permute-start.17 = (bf16[256,512]{1,0:T(8,128)(2,1)S(1)}, bf16[256,512]{1,0:T(8,128)(2,1)S(1)}, u32[]{:S(2)}, u32[]{:S(2)}) collective-permute-start(bf16[256,512]{1,0:T(8,128)(2,1)S(1)} %constant_dynamic-update-slice_fusion.refs_2_), channel_id=1, source_target_pairs={{0,2},{1,3},{2,0},{3,1},{4,6},{5,7},{6,4},{7,5},{8,10},{9,11},{10,... | collective-permute-start | bytes 786440 | tf_op jit(solution)/shard_map/ppermute | solution.py:20
  82.0 0.2 collective-permute-start.18
  82.1 0.3 collective-permute-start.19
  82.5 0.8 collective-permute-done.18.refs_3_
  83.3 0.2 collective-permute-done.19.refs_4_
  83.5 0.0 collective-permute-done.20.refs_5_
  83.5 2.1 %shard_map.62.refs_6_ = f32[2,2,512,512]{3,2,1,0:T(8,128)} custom-call(s32[3]{0:T(128)S(1)} %pad_add_fusion.ids_ref, f32[2,2,512,512]{3,2,1,0:T(8,128)S(1)} %copy-done, bf16[128,512]{1,0:T(8,128)(2,1)S(1)} %add_convert_fusion.refs_0_, bf16[128,512]{1,0:T(8,128)(2,1)S(1)} %collective-permute-done.12.refs_1_, ...), custom_call_target="tpu_custom_call" | custom-call | bytes 65536 | tf_op jit(solution)/shard_map/pallas_call | solution.py:56
  85.6 3.4 %collective-permute-done.17.refs_2_ = bf16[256,512]{1,0:T(8,128)(2,1)S(1)} collective-permute-done((bf16[256,512]{1,0:T(8,128)(2,1)S(1)}, bf16[256,512]{1,0:T(8,128)(2,1)S(1)}, u32[]{:S(2)}, u32[]{:S(2)}) %collective-permute-start.17) | collective-permute-done | bytes 262176 | tf_op jit(solution)/shard_map/ppermute | solution.py:20
  89.0 0.0 collective-permute-start.23
  89.0 0.5 collective-permute-start.21
  89.5 0.0 collective-permute-start.22
  89.5 1.2 %collective-permute-done.21.refs_3_ = bf16[128,512]{1,0:T(8,128)(2,1)S(1)} collective-permute-done((bf16[128,512]{1,0:T(8,128)(2,1)S(1)}, bf16[128,512]{1,0:T(8,128)(2,1)S(1)}, u32[]{:S(2)}, u32[]{:S(2)}) %collective-permute-start.21) | collective-permute-done | bytes 131104 | tf_op jit(solution)/shard_map/ppermute | solution.py:20
  90.7 0.2 collective-permute-done.22.refs_4_
  90.9 0.0 collective-permute-done.23.refs_5_
  90.9 2.1 %shard_map.63 = f32[2,2,512,512]{3,2,1,0:T(8,128)} custom-call(s32[3]{0:T(128)S(1)} %pad_add_fusion.ids_ref, f32[2,2,512,512]{3,2,1,0:T(8,128)S(1)} %copy-done, bf16[128,512]{1,0:T(8,128)(2,1)S(1)} %collective-permute-done.11.refs_0_, bf16[128,512]{1,0:T(8,128)(2,1)S(1)} %collective-permute-done.13.refs_1_, ...), custom_call_target="tpu_custom_call", output_to_operand_aliasing={{}: (8, {})} | custom-call | bytes 65536 | tf_op jit(solution)/shard_map/pallas_call | solution.py:56
  (4 shorter events, 0.0 us)
Async XLA Ops:
  1.4 34.9 %copy-start.1 = (bf16[2,512,512]{2,1,0:T(8,128)(2,1)S(1)}, bf16[2,512,512]{2,1,0:T(8,128)(2,1)}, u32[]{:S(2)}) copy-start(bf16[2,512,512]{2,1,0:T(8,128)(2,1)} %refs_0_) | copy-start | bytes 3145732
  4.3 28.9 %collective-permute-start.3 = (bf16[2,512,512]{2,1,0:T(8,128)(2,1)}, bf16[2,512,512]{2,1,0:T(8,128)(2,1)}, u32[]{:S(2)}, u32[]{:S(2)}) collective-permute-start(bf16[2,512,512]{2,1,0:T(8,128)(2,1)} %refs_0_), channel_id=1, source_target_pairs={{0,2},{1,3},{2,0},{3,1},{4,6},{5,7},{6,4},{7,5},{8,10},{9,11},{10,... | collective-permute-start | bytes 3145736 | tf_op jit(solution)/shard_map/ppermute | solution.py:20
  7.3 25.6 %collective-permute-start.2 = (bf16[512,512]{1,0:T(8,128)(2,1)S(1)}, bf16[512,512]{1,0:T(8,128)(2,1)S(1)}, u32[]{:S(2)}, u32[]{:S(2)}) collective-permute-start(bf16[512,512]{1,0:T(8,128)(2,1)S(1)} %bitcast.11), channel_id=1, source_target_pairs={{0,8},{4,12},{8,0},{12,4},{1,9},{5,13},{9,1},{13,5},{2,10},{6,14},... | collective-permute-start | bytes 1572872 | tf_op jit(solution)/shard_map/ppermute | solution.py:20
  9.9 23.3 %collective-permute-start.1 = (bf16[512,512]{1,0:T(8,128)(2,1)S(1)}, bf16[512,512]{1,0:T(8,128)(2,1)}, u32[]{:S(2)}, u32[]{:S(2)}) collective-permute-start(bf16[512,512]{1,0:T(8,128)(2,1)S(1)} %bitcast.12), channel_id=1, source_target_pairs={{0,4},{4,0},{8,12},{12,8},{1,5},{5,1},{9,13},{13,9},{2,6},{6,2},{1... | collective-permute-start | bytes 1572872 | tf_op jit(solution)/shard_map/ppermute | solution.py:20
  11.5 23.3 %collective-permute-start = (bf16[2,512,512]{2,1,0:T(8,128)(2,1)}, bf16[2,512,512]{2,1,0:T(8,128)(2,1)}, u32[]{:S(2)}, u32[]{:S(2)}) collective-permute-start(bf16[2,512,512]{2,1,0:T(8,128)(2,1)} %refs_0_), channel_id=1, source_target_pairs={{0,1},{1,0},{2,3},{3,2},{4,5},{5,4},{6,7},{7,6},{8,9},{9,8},{10,11... | collective-permute-start | bytes 3145736 | tf_op jit(solution)/shard_map/ppermute | solution.py:20
  33.3 3.0 %collective-permute-start.4 = (bf16[2,512,512]{2,1,0:T(8,128)(2,1)}, bf16[2,512,512]{2,1,0:T(8,128)(2,1)}, u32[]{:S(2)}, u32[]{:S(2)}) collective-permute-start(bf16[2,512,512]{2,1,0:T(8,128)(2,1)} %collective-permute-done.3.refs_2_), channel_id=1, source_target_pairs={{0,1},{1,0},{2,3},{3,2},{4,5},{5,4},{6,7},{7,6},{8,9},{9,8},{10,11... | collective-permute-start | bytes 3145736 | tf_op jit(solution)/shard_map/ppermute | solution.py:20
  33.3 14.4 %collective-permute-start.5 = (bf16[512,512]{1,0:T(8,128)(2,1)S(1)}, bf16[512,512]{1,0:T(8,128)(2,1)}, u32[]{:S(2)}, u32[]{:S(2)}) collective-permute-start(bf16[512,512]{1,0:T(8,128)(2,1)S(1)} %collective-permute-done.2.refs_6_), channel_id=1, source_target_pairs={{0,4},{4,0},{8,12},{12,8},{1,5},{5,1},{9,13},{13,9},{2,6},{6,2},{1... | collective-permute-start | bytes 1572872 | tf_op jit(solution)/shard_map/ppermute | solution.py:20
  41.2 42.3 %copy-start = (f32[2,2,512,512]{3,2,1,0:T(8,128)S(1)}, f32[2,2,512,512]{3,2,1,0:T(8,128)}, u32[]{:S(2)}) copy-start(f32[2,2,512,512]{3,2,1,0:T(8,128)} %pivot_ref.3) | copy-start | bytes 12582916
  50.7 6.8 %collective-permute-start.6 = (bf16[128,512]{1,0:T(8,128)(2,1)S(1)}, bf16[128,512]{1,0:T(8,128)(2,1)S(1)}, u32[]{:S(2)}, u32[]{:S(2)}) collective-permute-start(bf16[128,512]{1,0:T(8,128)(2,1)S(1)} %get-tuple-element.36), channel_id=1, source_target_pairs={{0,4},{4,0},{8,12},{12,8},{1,5},{5,1},{9,13},{13,9},{2,6},{6,2},{1... | collective-permute-start | bytes 393224 | tf_op jit(solution)/shard_map/ppermute | solution.py:20
  52.2 12.7 %collective-permute-start.7 = (bf16[128,512]{1,0:T(8,128)(2,1)S(1)}, bf16[128,512]{1,0:T(8,128)(2,1)S(1)}, u32[]{:S(2)}, u32[]{:S(2)}) collective-permute-start(bf16[128,512]{1,0:T(8,128)(2,1)S(1)} %get-tuple-element.37), channel_id=1, source_target_pairs={{0,8},{4,12},{8,0},{12,4},{1,9},{5,13},{9,1},{13,5},{2,10},{6,14},... | collective-permute-start | bytes 393224 | tf_op jit(solution)/shard_map/ppermute | solution.py:20
  54.4 10.5 %collective-permute-start.8 = (bf16[128,512]{1,0:T(8,128)(2,1)S(1)}, bf16[128,512]{1,0:T(8,128)(2,1)S(1)}, u32[]{:S(2)}, u32[]{:S(2)}) collective-permute-start(bf16[128,512]{1,0:T(8,128)(2,1)S(1)} %get-tuple-element.38), channel_id=1, source_target_pairs={{0,12},{4,8},{8,4},{12,0},{1,13},{5,9},{9,5},{13,1},{2,14},{6,10},... | collective-permute-start | bytes 393224 | tf_op jit(solution)/shard_map/ppermute | solution.py:20
  55.2 12.5 %collective-permute-start.14 = (f32[128,512]{1,0:T(8,128)S(1)}, f32[128,512]{1,0:T(8,128)S(1)}, u32[]{:S(2)}, u32[]{:S(2)}) collective-permute-start(f32[128,512]{1,0:T(8,128)S(1)} %get-tuple-element.40), channel_id=1, source_target_pairs={{0,1},{1,0},{2,3},{3,2},{4,5},{5,4},{6,7},{7,6},{8,9},{9,8},{10,11... | collective-permute-start | bytes 786440 | tf_op jit(solution)/shard_map/ppermute | solution.py:20
  55.2 14.5 %collective-permute-start.15 = (f32[128,512]{1,0:T(8,128)S(1)}, f32[128,512]{1,0:T(8,128)S(1)}, u32[]{:S(2)}, u32[]{:S(2)}) collective-permute-start(f32[128,512]{1,0:T(8,128)S(1)} %get-tuple-element.41), channel_id=1, source_target_pairs={{0,2},{1,3},{2,0},{3,1},{4,6},{5,7},{6,4},{7,5},{8,10},{9,11},{10,... | collective-permute-start | bytes 786440 | tf_op jit(solution)/shard_map/ppermute | solution.py:20
  57.5 13.8 %collective-permute-start.16 = (f32[128,512]{1,0:T(8,128)S(1)}, f32[128,512]{1,0:T(8,128)S(1)}, u32[]{:S(2)}, u32[]{:S(2)}) collective-permute-start(f32[128,512]{1,0:T(8,128)S(1)} %get-tuple-element.42), channel_id=1, source_target_pairs={{0,3},{1,2},{2,1},{3,0},{4,7},{5,6},{6,5},{7,4},{8,11},{9,10},{10,... | collective-permute-start | bytes 786440 | tf_op jit(solution)/shard_map/ppermute | solution.py:20
  65.0 6.0 %collective-permute-start.12 = (bf16[128,512]{1,0:T(8,128)(2,1)S(1)}, bf16[128,512]{1,0:T(8,128)(2,1)S(1)}, u32[]{:S(2)}, u32[]{:S(2)}) collective-permute-start(bf16[128,512]{1,0:T(8,128)(2,1)S(1)} %add_convert_fusion.refs_0_), channel_id=1, source_target_pairs={{0,4},{4,0},{8,12},{12,8},{1,5},{5,1},{9,13},{13,9},{2,6},{6,2},{1... | collective-permute-start | bytes 393224 | tf_op jit(solution)/shard_map/ppermute | solution.py:20
  67.1 6.4 %collective-permute-start.11 = (bf16[128,512]{1,0:T(8,128)(2,1)S(1)}, bf16[128,512]{1,0:T(8,128)(2,1)S(1)}, u32[]{:S(2)}, u32[]{:S(2)}) collective-permute-start(bf16[128,512]{1,0:T(8,128)(2,1)S(1)} %add_convert_fusion.refs_0_), channel_id=1, source_target_pairs={{0,2},{1,3},{2,0},{3,1},{4,6},{5,7},{6,4},{7,5},{8,10},{9,11},{10,... | collective-permute-start | bytes 393224 | tf_op jit(solution)/shard_map/ppermute | solution.py:20
  67.7 8.3 %collective-permute-start.10 = (bf16[128,512]{1,0:T(8,128)(2,1)S(1)}, bf16[128,512]{1,0:T(8,128)(2,1)S(1)}, u32[]{:S(2)}, u32[]{:S(2)}) collective-permute-start(bf16[128,512]{1,0:T(8,128)(2,1)S(1)} %add_convert_fusion.refs_0_), channel_id=1, source_target_pairs={{0,12},{4,8},{8,4},{12,0},{1,13},{5,9},{9,5},{13,1},{2,14},{6,10},... | collective-permute-start | bytes 393224 | tf_op jit(solution)/shard_map/ppermute | solution.py:20
  69.7 10.5 %collective-permute-start.9 = (bf16[128,512]{1,0:T(8,128)(2,1)S(1)}, bf16[128,512]{1,0:T(8,128)(2,1)S(1)}, u32[]{:S(2)}, u32[]{:S(2)}) collective-permute-start(bf16[128,512]{1,0:T(8,128)(2,1)S(1)} %add_convert_fusion.refs_0_), channel_id=1, source_target_pairs={{0,8},{4,12},{8,0},{12,4},{1,9},{5,13},{9,1},{13,5},{2,10},{6,14},... | collective-permute-start | bytes 393224 | tf_op jit(solution)/shard_map/ppermute | solution.py:20
  71.0 9.1 %collective-permute-start.13 = (bf16[128,512]{1,0:T(8,128)(2,1)S(1)}, bf16[128,512]{1,0:T(8,128)(2,1)S(1)}, u32[]{:S(2)}, u32[]{:S(2)}) collective-permute-start(bf16[128,512]{1,0:T(8,128)(2,1)S(1)} %collective-permute-done.12.refs_1_), channel_id=1, source_target_pairs={{0,2},{1,3},{2,0},{3,1},{4,6},{5,7},{6,4},{7,5},{8,10},{9,11},{10,... | collective-permute-start | bytes 393224 | tf_op jit(solution)/shard_map/ppermute | solution.py:20
  80.2 3.3 %collective-permute-start.20 = (bf16[256,512]{1,0:T(8,128)(2,1)S(1)}, bf16[256,512]{1,0:T(8,128)(2,1)S(1)}, u32[]{:S(2)}, u32[]{:S(2)}) collective-permute-start(bf16[256,512]{1,0:T(8,128)(2,1)S(1)} %constant_dynamic-update-slice_fusion.refs_2_), channel_id=1, source_target_pairs={{0,1},{1,0},{2,3},{3,2},{4,5},{5,4},{6,7},{7,6},{8,9},{9,8},{10,11... | collective-permute-start | bytes 786440 | tf_op jit(solution)/shard_map/ppermute | solution.py:20
  80.3 8.7 %collective-permute-start.17 = (bf16[256,512]{1,0:T(8,128)(2,1)S(1)}, bf16[256,512]{1,0:T(8,128)(2,1)S(1)}, u32[]{:S(2)}, u32[]{:S(2)}) collective-permute-start(bf16[256,512]{1,0:T(8,128)(2,1)S(1)} %constant_dynamic-update-slice_fusion.refs_2_), channel_id=1, source_target_pairs={{0,2},{1,3},{2,0},{3,1},{4,6},{5,7},{6,4},{7,5},{8,10},{9,11},{10,... | collective-permute-start | bytes 786440 | tf_op jit(solution)/shard_map/ppermute | solution.py:20
  82.0 1.3 %collective-permute-start.18 = (bf16[128,512]{1,0:T(8,128)(2,1)S(1)}, bf16[128,512]{1,0:T(8,128)(2,1)S(1)}, u32[]{:S(2)}, u32[]{:S(2)}) collective-permute-start(bf16[128,512]{1,0:T(8,128)(2,1)S(1)} %add_convert_fusion.refs_0_), channel_id=1, source_target_pairs={{0,1},{1,0},{2,3},{3,2},{4,5},{5,4},{6,7},{7,6},{8,9},{9,8},{10,11... | collective-permute-start | bytes 393224 | tf_op jit(solution)/shard_map/ppermute | solution.py:20
  82.1 1.4 %collective-permute-start.19 = (bf16[128,512]{1,0:T(8,128)(2,1)S(1)}, bf16[128,512]{1,0:T(8,128)(2,1)S(1)}, u32[]{:S(2)}, u32[]{:S(2)}) collective-permute-start(bf16[128,512]{1,0:T(8,128)(2,1)S(1)} %collective-permute-done.12.refs_1_), channel_id=1, source_target_pairs={{0,1},{1,0},{2,3},{3,2},{4,5},{5,4},{6,7},{7,6},{8,9},{9,8},{10,11... | collective-permute-start | bytes 393224 | tf_op jit(solution)/shard_map/ppermute | solution.py:20
  89.0 1.9 %collective-permute-start.23 = (bf16[256,512]{1,0:T(8,128)(2,1)S(1)}, bf16[256,512]{1,0:T(8,128)(2,1)S(1)}, u32[]{:S(2)}, u32[]{:S(2)}) collective-permute-start(bf16[256,512]{1,0:T(8,128)(2,1)S(1)} %collective-permute-done.17.refs_2_), channel_id=1, source_target_pairs={{0,1},{1,0},{2,3},{3,2},{4,5},{5,4},{6,7},{7,6},{8,9},{9,8},{10,11... | collective-permute-start | bytes 786440 | tf_op jit(solution)/shard_map/ppermute | solution.py:20
  89.0 1.7 %collective-permute-start.21 = (bf16[128,512]{1,0:T(8,128)(2,1)S(1)}, bf16[128,512]{1,0:T(8,128)(2,1)S(1)}, u32[]{:S(2)}, u32[]{:S(2)}) collective-permute-start(bf16[128,512]{1,0:T(8,128)(2,1)S(1)} %collective-permute-done.11.refs_0_), channel_id=1, source_target_pairs={{0,1},{1,0},{2,3},{3,2},{4,5},{5,4},{6,7},{7,6},{8,9},{9,8},{10,11... | collective-permute-start | bytes 393224 | tf_op jit(solution)/shard_map/ppermute | solution.py:20
  89.5 1.4 %collective-permute-start.22 = (bf16[128,512]{1,0:T(8,128)(2,1)S(1)}, bf16[128,512]{1,0:T(8,128)(2,1)S(1)}, u32[]{:S(2)}, u32[]{:S(2)}) collective-permute-start(bf16[128,512]{1,0:T(8,128)(2,1)S(1)} %collective-permute-done.13.refs_1_), channel_id=1, source_target_pairs={{0,1},{1,0},{2,3},{3,2},{4,5},{5,4},{6,7},{7,6},{8,9},{9,8},{10,11... | collective-permute-start | bytes 393224 | tf_op jit(solution)/shard_map/ppermute | solution.py:20

commit v4 on v3

v4 whole, which is shorter than its diff:
```python
import functools

import jax
import jax.numpy as jnp
from jax import lax
from jax.experimental import pallas as pl
from jax.experimental.pallas import tpu as pltpu
from jax.sharding import PartitionSpec as P

S = 512
BLK = 128
CHUNKS = 2
COST = 1 << 16
VMEM_LIMIT = 48 * 1024 * 1024
bf16 = jnp.bfloat16
f32 = jnp.float32


def swap(x, axis, distance):
    size = lax.axis_size(axis)
    return lax.ppermute(x, axis, [(i, i ^ distance) for i in range(size)])


def gather_z(chunks, side, beside):
    size = lax.axis_size("prow")
    gathered = []
    for m in chunks:
        pieces = {0: m}
        step = size // 2
        while step > 1:
            pieces |= {d ^ step: swap(p, "prow", step) for d, p in pieces.items()}
            step //= 2
        pieces |= {d ^ 1: swap(p, "prow", 1) for d, p in pieces.items() if d != size - 2}
        gathered.append(pieces)
    last = []
    for n, pieces in enumerate(gathered):
        if n == len(chunks) - 1:
            gathered, beside = lax.optimization_barrier((gathered, beside))
        else:
            far = pieces[size - 2]
            pieces[size - 2], side = lax.optimization_barrier((far, side))
        last.append(swap(gathered[n][size - 2], "prow", 1))
    return gathered, last, side, beside


def gather_x(a):
    size = lax.axis_size("pcol")
    return {e: swap(a, "pcol", e) for e in range(2, size, 2)}


def gather_core(a):
    return [p for e in sorted(a) for p in (a[e], swap(a[e], "pcol", 1))]


def dot(a, b):
    return jnp.dot(a, b, preferred_element_type=f32)


def turn(m):
    width = m.shape[1] // 2
    return jnp.concatenate([-m[:, width:], m[:, :width]], axis=1)


def call(body, out_shape, scalars, operands, specs, out_specs, scratch=(), aliases=None):
    return pl.pallas_call(
        body,
        out_shape=out_shape,
        grid_spec=pltpu.PrefetchScalarGridSpec(
            num_scalar_prefetch=1,
            grid=(1,),
            in_specs=specs,
            out_specs=out_specs,
            scratch_shapes=scratch,
        ),
        input_output_aliases=aliases or {},
        compiler_params=pltpu.CompilerParams(vmem_limit_bytes=VMEM_LIMIT),
        cost_estimate=pl.CostEstimate(flops=0, bytes_accessed=COST, transcendentals=0),
    )(scalars, *operands)


def call_here(body, out_shape, scalars, operands, scratch=()):
    return pl.pallas_call(
        body,
        out_shape=out_shape,
        in_specs=[pl.BlockSpec(memory_space=pltpu.SMEM)]
        + [pl.BlockSpec(memory_space=pltpu.VMEM)] * len(operands),
        out_specs=jax.tree.map(lambda _: pl.BlockSpec(memory_space=pltpu.VMEM), out_shape),
        scratch_shapes=scratch,
        compiler_params=pltpu.CompilerParams(vmem_limit_bytes=VMEM_LIMIT),
        cost_estimate=pl.CostEstimate(flops=0, bytes_accessed=COST, transcendentals=0),
    )(scalars, *operands)


def whole(x):
    return pl.BlockSpec(x.shape, lambda i, ids, n=len(x.shape): (0,) * n)


def add_products(a_pieces, m_chunks, ids, levels):
    rows, wide = m_chunks[0][0].shape
    columns, count = len(a_pieces), len(m_chunks)
    per = levels // columns

    def body(ids_ref, *refs):
        a_refs, refs = refs[:columns], refs[columns:]
        m_refs, refs = refs[: count * (levels - 1)], refs[count * (levels - 1) :]
        total_refs, left_ref, m_all = refs[:count], refs[count], refs[count + 1]
        missing = ids_ref[0] ^ (levels - 1)
        for n, m_ref in enumerate(m_refs):
            m_all[n // (levels - 1), ids_ref[0] ^ (n % (levels - 1))] = m_ref[...]
        for total_ref in total_refs:
            total_ref[...] = jnp.zeros_like(total_ref)
        for e, a_ref in enumerate(a_refs):
            for n in range(per):
                at = (ids_ref[1] ^ e) * per + n
                cut = slice(n * rows, (n + 1) * rows)

                @pl.when(at != missing)
                def _():
                    for c, total_ref in enumerate(total_refs):
                        m = m_all[c, at]
                        total_ref[...] += dot(a_ref[0, :, cut], m) + dot(a_ref[1, :, cut], turn(m))

                @pl.when(at == missing)
                def _():
                    left_ref[...] = a_ref[:, :, cut]

    shapes = [jax.ShapeDtypeStruct((rows, wide), f32)] * count
    shapes += [jax.ShapeDtypeStruct((2, rows, rows), bf16)]
    flat = list(a_pieces) + [chunk[d] for chunk in m_chunks for d in range(levels - 1)]
    out = call_here(
        body,
        shapes,
        ids,
        flat,
        [pltpu.VMEM((count, levels, rows, wide), bf16)],
    )
    return out[:count], out[count]


def finish_products(left, last, total, side, before, ids, levels, columns, final):
    rows, wide = last.shape
    cut = rows // columns
    share = S // levels

    def body(ids_ref, left_ref, m_ref, total_ref, side_ref, *refs):
        before_refs, refs = refs[: len(before)], refs[len(before) :]
        p_out, y_out, y_ref, p_ref = refs[:levels], refs[levels:-2], refs[-2], refs[-1]
        m = m_ref[...]
        y_ref[...] = -(total_ref[...] + dot(left_ref[0], m) + dot(left_ref[1], turn(m)))
        chosen = y_ref[...].astype(bf16)
        p_ref[...] = dot(side_ref[0], chosen) + dot(side_ref[1], turn(chosen))
        for d in range(levels):
            start = pl.multiple_of((ids_ref[0] ^ d) * share, share)
            p_out[d][...] = p_ref[pl.ds(start, share), :].astype(p_out[d].dtype)
        if not final:
            y_out[0][...] = y_ref[...]
            return
        for e in range(columns):
            start = pl.multiple_of((ids_ref[1] ^ e) * cut, cut)
            at = slice(e % 2 * cut, (e % 2 + 1) * cut)
            for n, ref in enumerate(list(before_refs) + [y_ref]):
                value = ref[pl.ds(start, cut), :].astype(y_out[e // 2].dtype)
                y_out[e // 2][at, n * wide : (n + 1) * wide] = value

    shapes = [jax.ShapeDtypeStruct((share, wide), f32 if d == 0 else bf16) for d in range(levels)]
    if final:
        stack = (2 * cut, wide * (1 + len(before)))
        shapes += [jax.ShapeDtypeStruct(stack, bf16 if n else f32) for n in range(columns // 2)]
    else:
        shapes += [jax.ShapeDtypeStruct((rows, wide), f32)]
    operands = [left, last, total, side] + before
    out = call_here(
        body,
        shapes,
        ids,
        operands,
        [pltpu.VMEM((rows, wide), f32), pltpu.VMEM((S, wide), f32)],
    )
    return out[:levels], out[levels:]


def cross_rows(stacks):
    return [stacks[0]] + [swap(y, "pcol", 2 * n) for n, y in enumerate(stacks) if n]


def lay_rows(stacks, chunks, ids):
    columns = len(stacks)
    cut, wide = stacks[0].shape[0] // 2, stacks[0].shape[1]
    width = wide // 2
    some = width // chunks

    def body(ids_ref, *refs):
        for n in range(columns):
            odd = n // (columns // 2)
            e = 2 * (n % (columns // 2)) + odd
            at = slice(odd * cut, (odd + 1) * cut)
            for c in range(chunks):
                for part in range(2):
                    start = pl.multiple_of((ids_ref[1] ^ e) * width + c * some, some)
                    source = (2 * c + part) * some
                    value = refs[n][at, source : source + some].astype(f32)
                    refs[-1][:, part, pl.ds(start, some)] = value

    shape = jax.ShapeDtypeStruct((cut, 2, columns * width), f32)
    return call_here(body, shape, ids, stacks)


def take_off(pivot, stacks, flip, late, levels, ids, rest=None):
    wide = stacks[0].shape[1]
    width = wide // 2
    per_node = S // width
    half = levels // 2
    share = S // levels
    first = per_node * flip

    def body(ids_ref, pivot_ref, *refs):
        for e, ref in enumerate(refs[: len(stacks)]):
            left = pl.multiple_of(((ids_ref[1] ^ (first + e)) % per_node) * width, width)
            for d in range(half):
                top = pl.multiple_of(((ids_ref[0] ^ d) % half) * share, share)
                for part in range(2):
                    at = (0, part, pl.ds(top, share), pl.ds(left, width))
                    piece = ref[d * share : (d + 1) * share, part * width : (part + 1) * width]
                    refs[-1][at] = pivot_ref[at] - piece.astype(f32)

    spec = pl.BlockSpec(
        (1, 2, S // 2, S), lambda i, ids: (ids[2] ^ flip, 0, (ids[0] // half) ^ late, 0)
    )
    operands, specs, aliases = [pivot] + stacks, [spec] + [whole(p) for p in stacks], {}
    if rest is not None:
        operands, specs = operands + [rest], specs + [pl.BlockSpec(memory_space=pl.ANY)]
        aliases = {len(operands): 0}
    return call(
        body, jax.ShapeDtypeStruct(pivot.shape, f32), ids, operands, specs, spec, aliases=aliases
    )


def join(sums):
    some = sums[0].shape[1] // 2
    return jnp.concatenate([s[:, :some] for s in sums] + [s[:, some:] for s in sums], 1)


def per_device(inverse_block, factor_column, block_pattern, pivot_inverse):
    levels = lax.axis_size("prow")
    level = lax.axis_index("prow")
    columns = lax.axis_size("pcol")
    column = lax.axis_index("pcol")
    rows = factor_column.shape[0]
    width = factor_column.shape[2] // columns
    per_node = S // width
    blocks = rows // BLK
    node = column // per_node
    ids = jnp.stack([level, column, node]).astype(jnp.int32)

    chunks = CHUNKS if width % (CHUNKS * 128) == 0 else 1
    some = width // chunks
    raw = lax.dynamic_slice_in_dim(factor_column, column * width, width, 2)
    raw, keep = lax.optimization_barrier(
        (raw, lax.dynamic_index_in_dim(block_pattern, node, 0, keepdims=False))
    )
    keep = jnp.broadcast_to(keep.astype(bf16)[:, None], (blocks, BLK)).reshape(rows, 1)
    own = [raw[:, :, n : n + some].reshape(rows, 2 * some) for n in range(0, width, some)]
    own = [part * keep for part in lax.optimization_barrier(own)]
    keep = keep[:, :, None]
    side = lax.dynamic_slice_in_dim(factor_column, node * S, S, 2) * keep
    side = jnp.transpose(side, (1, 2, 0))
    m_chunks, last, side, a_across = gather_z(own, side, gather_x(inverse_block))
    a_pieces = gather_core({0: inverse_block} | a_across)
    totals, left = add_products(a_pieces, m_chunks, ids, levels)

    before, parts = [], []
    for c in range(chunks):
        p_parts, y_parts = finish_products(
            left, last[c], totals[c], side, before, ids, levels, columns, c == chunks - 1
        )
        before = before + list(y_parts)
        parts.append(p_parts)
    y_stacks = cross_rows(before[chunks - 1 :])

    parts = [
        [p[0]] + [swap(p[d], "prow", d) for d in range(1, levels)] for p in parts
    ]
    parts[-1], y_stacks = lax.optimization_barrier((parts[-1], y_stacks))
    sums = [sum((p.astype(f32) for p in received[1:]), received[0]) for received in parts]
    sums = [total.astype(bf16) for total in sums]

    half = levels // 2
    sums = join(sums)
    pieces = [sums] + [swap(sums, "prow", d) for d in range(1, levels)]
    early = pieces[:half]
    early_across = [gather_x(p) for p in early]
    late, early_across, y_stacks = lax.optimization_barrier(
        (pieces[half:], early_across, y_stacks)
    )
    y_stacks = y_stacks + [swap(y, "pcol", 1) for y in y_stacks]
    own_rows = lay_rows(y_stacks, chunks, ids)
    late = jnp.concatenate(late, 0)
    late_across = gather_x(late)
    early = jnp.concatenate(early, 0)
    early_across = {e: jnp.concatenate([a[e] for a in early_across], 0) for e in late_across}
    take = functools.partial(take_off, pivot_inverse, levels=levels, ids=ids)
    if per_node == 2:
        pivot = take(gather_core({0: early}), 0, 0)
        pivot = take(gather_core({0: late}), 0, 1, rest=pivot)
        pivot = take(gather_core(early_across), 1, 0, rest=pivot)
        late_across, pivot, own_rows = lax.optimization_barrier((late_across, pivot, own_rows))
        pivot = take(gather_core(late_across), 1, 1, rest=pivot)
    else:
        early = gather_core({0: early} | early_across)
        late = gather_core({0: late} | late_across)
        pivot = take(early[:per_node], 0, 0)
        pivot = take(late[:per_node], 0, 1, rest=pivot)
        pivot = take(early[per_node:], 1, 0, rest=pivot)
        pivot = take(late[per_node:], 1, 1, rest=pivot)
    return own_rows, pivot


def solution(mesh):
    in_specs = (
        P(None, ("pole", "prow"), "pcol"),
        P(("pole", "prow"), None, None),
        P("pole", "prow"),
        P("pole", None, None, None),
    )
    out_specs = (P(("pole", "prow", "pcol"), None, None), P("pole", None, None, None))
    return jax.shard_map(
        per_device, mesh=mesh, in_specs=in_specs, out_specs=out_specs, check_vma=False
    )
```

time: 93.3 us -> 86.3 us (0.925)
  waiting for transfers between devices: 47.5 us -> 30 us
  starting transfers between devices: 21.3 us -> 28.4 us
  Pallas kernels: 13.9 us -> 18.4 us
  other arithmetic: 4.94 us -> 2.33 us
  local copies, waits for them, and re-layouts: 4.61 us -> 6.05 us
    ppermute x24 -> x28, waiting for transfers between devices: 47.5 us -> 30 us  [swap(): return lax.ppermute(x, axis, [(i, i ^ distance) for i in range(size)])]
    pallas_call x0 -> x4, Pallas kernels: none -> 11.5 us  [call_here(): pl.pallas_call(body, out_shape=out_shape, in_specs=[pl.BlockSpec(memory_s...]
    ppermute x24 -> x28, starting transfers between devices: 21.3 us -> 28.4 us  [swap(): return lax.ppermute(x, axis, [(i, i ^ distance) for i in range(size)])]
    pallas_call x5 -> x4, Pallas kernels: 13.9 us -> 6.85 us  [call(): pl.pallas_call(body, out_shape=out_shape, grid_spec=pltpu.PrefetchScalarG...]
    mul x1, other arithmetic: 2.82 us -> 0.84 us  [per_device(): own = [part * keep for part in lax.optimization_barrier(own)]]
    dynamic_slice x1, local copies, waits for them, and re-layouts: 1.94 us -> 0.72 us  [per_device(): side = lax.dynamic_slice_in_dim(factor_column, node * S, S, 2) * keep]
    unnamed x7 -> x9, local copies, waits for them, and re-layouts: 2.58 us -> 3.74 us
  transfers between devices with their start and end apart: 24 -> 28, of which waited for: 15 -> 12; matrix products, arithmetic and copies ran while one was open for 6% -> 8% of each run, Pallas kernels for 10% -> 19%
where the time goes in v4:
time: 86.3 us; the launch traced here: 86 us
  waiting for transfers between devices  30 us (35%)
  starting transfers between devices  28.4 us (33%)
  Pallas kernels  18.4 us (21%)
  local copies, waits for them, and re-layouts  6.05 us (7%)
  other arithmetic  2.33 us (3%)
    ppermute x28, waiting for transfers between devices, swap(): return lax.ppermute(x, axis, [(i, i ^ distance) for i in range(size)])  30 us
    ppermute x28, starting transfers between devices, swap(): return lax.ppermute(x, axis, [(i, i ^ distance) for i in range(size)])  28.4 us
    pallas_call x4, Pallas kernels, call_here(): pl.pallas_call(body, out_shape=out_shape, in_specs=[pl.BlockSpec(memory_s...  11.5 us
    pallas_call x4, Pallas kernels, call(): pl.pallas_call(body, out_shape=out_shape, grid_spec=pltpu.PrefetchScalarG...  6.85 us
    unnamed x9, local copies, waits for them, and re-layouts  3.74 us
  transfers between devices with their start and end apart: 28, of which 12 were waited for; matrix products, arithmetic and copies ran while one was open for 8% of the time, Pallas kernels for 19%

profile of v4, /device:TPU:0, one launch (start us, length us, event | category | flops | bytes accessed | tf_op | source)
XLA Modules:
  0.0 86.0 jit_solution(9682407695056702058)
XLA Ops:
  0.6 0.0 copy-start
  0.6 3.0 %collective-permute-start.5 = (bf16[2,512,512]{2,1,0:T(8,128)(2,1)}, bf16[2,512,512]{2,1,0:T(8,128)(2,1)}, u32[]{:S(2)}, u32[]{:S(2)}) collective-permute-start(bf16[2,512,512]{2,1,0:T(8,128)(2,1)} %refs_0_.1), channel_id=1, source_target_pairs={{0,2},{1,3},{2,0},{3,1},{4,6},{5,7},{6,4},{7,5},{8,10},{9,11},{10,... | collective-permute-start | bytes 3145736 | tf_op jit(solution)/shard_map/ppermute | solution.py:21
  3.6 0.7 fusion
  4.3 0.4 constant_dynamic-slice_fusion.2
  4.7 0.4 fusion.1
  5.1 0.1 copy_bitcast_fusion
  5.2 0.1 broadcast_bitcast_fusion
  5.2 0.8 broadcast_multiply_fusion
  6.1 2.6 %collective-permute-start.2 = (bf16[512,256]{1,0:T(8,128)(2,1)}, bf16[512,256]{1,0:T(8,128)(2,1)}, u32[]{:S(2)}, u32[]{:S(2)}) collective-permute-start(bf16[512,256]{1,0:T(8,128)(2,1)} %get-tuple-element.50.refs_4_), channel_id=1, source_target_pairs={{0,8},{4,12},{8,0},{12,4},{1,9},{5,13},{9,1},{13,5},{2,10},{6,14},... | collective-permute-start | bytes 786440 | tf_op jit(solution)/shard_map/ppermute | solution.py:21
  8.7 1.6 %collective-permute-start.1 = (bf16[512,256]{1,0:T(8,128)(2,1)}, bf16[512,256]{1,0:T(8,128)(2,1)}, u32[]{:S(2)}, u32[]{:S(2)}) collective-permute-start(bf16[512,256]{1,0:T(8,128)(2,1)} %get-tuple-element.50.refs_4_), channel_id=1, source_target_pairs={{0,4},{4,0},{8,12},{12,8},{1,5},{5,1},{9,13},{13,9},{2,6},{6,2},{1... | collective-permute-start | bytes 786440 | tf_op jit(solution)/shard_map/ppermute | solution.py:21
  10.2 0.4 collective-permute-start.3
  10.7 0.3 collective-permute-start.4
  11.0 0.7 constant_dynamic-slice_fusion
  11.8 2.5 %copy.10 = bf16[512,2,512]{0,2,1:T(8,128)(2,1)} copy(bf16[512,2,512]{2,1,0:T(2,128)(2,1)S(1)} %constant_dynamic-slice_fusion) | data formatting | bytes 2097152
  14.2 1.3 %multiply_bitcast_fusion.side_ref = bf16[2,512,512]{2,1,0:T(8,128)(2,1)S(1)} fusion(bf16[512,2,512]{0,2,1:T(8,128)(2,1)} %copy.10, bf16[512]{0:T(512)(128)(2,1)S(1)} %broadcast_bitcast_fusion), kind=kLoop, calls=%fused_computation | loop fusion | flops 524288 | bytes 2098176 | tf_op jit(solution)/shard_map/transpose | solution.py:266
  15.5 6.4 %collective-permute-done.2.refs_6_ = bf16[512,256]{1,0:T(8,128)(2,1)} collective-permute-done((bf16[512,256]{1,0:T(8,128)(2,1)}, bf16[512,256]{1,0:T(8,128)(2,1)}, u32[]{:S(2)}, u32[]{:S(2)}) %collective-permute-start.2) | collective-permute-done | bytes 262176 | tf_op jit(solution)/shard_map/ppermute | solution.py:21
  21.9 6.4 %collective-permute-done.1.refs_5_ = bf16[512,256]{1,0:T(8,128)(2,1)} collective-permute-done((bf16[512,256]{1,0:T(8,128)(2,1)}, bf16[512,256]{1,0:T(8,128)(2,1)}, u32[]{:S(2)}, u32[]{:S(2)}) %collective-permute-start.1) | collective-permute-done | bytes 262176 | tf_op jit(solution)/shard_map/ppermute | solution.py:21
  28.4 3.9 %collective-permute-done.3.refs_8_ = bf16[512,256]{1,0:T(8,128)(2,1)} collective-permute-done((bf16[512,256]{1,0:T(8,128)(2,1)S(1)}, bf16[512,256]{1,0:T(8,128)(2,1)}, u32[]{:S(2)}, u32[]{:S(2)}) %collective-permute-start.3) | collective-permute-done | bytes 262176 | tf_op jit(solution)/shard_map/ppermute | solution.py:21
  32.2 0.0 collective-permute-done.5.refs_2_
  32.2 0.0 collective-permute-start.6
  32.2 1.3 %collective-permute-start.7 = (bf16[512,256]{1,0:T(8,128)(2,1)}, bf16[512,256]{1,0:T(8,128)(2,1)}, u32[]{:S(2)}, u32[]{:S(2)}) collective-permute-start(bf16[512,256]{1,0:T(8,128)(2,1)} %collective-permute-done.2.refs_6_), channel_id=1, source_target_pairs={{0,4},{4,0},{8,12},{12,8},{1,5},{5,1},{9,13},{13,9},{2,6},{6,2},{1... | collective-permute-start | bytes 786440 | tf_op jit(solution)/shard_map/ppermute | solution.py:21
  33.5 0.8 collective-permute-start.11
  34.3 0.1 pad_add_fusion.ids_ref
  34.4 0.0 collective-permute-done.refs_1_
  34.4 0.8 collective-permute-done.6.refs_3_
  35.2 1.2 %copy-done.2 = bf16[2,512,512]{2,1,0:T(8,128)(2,1)S(1)} copy-done((bf16[2,512,512]{2,1,0:T(8,128)(2,1)S(1)}, bf16[2,512,512]{2,1,0:T(8,128)(2,1)}, u32[]{:S(2)}) %copy-start.2) | copy-done | bytes 1048600
  36.4 4.6 %shard_map.59 = (f32[512,256]{1,0:T(8,128)S(1)}, f32[512,256]{1,0:T(8,128)S(1)}, bf16[2,512,512]{2,1,0:T(8,128)(2,1)S(1)}) custom-call(s32[3]{0:T(128)S(1)} %pad_add_fusion.ids_ref, bf16[2,512,512]{2,1,0:T(8,128)(2,1)S(1)} %copy-done.2, bf16[2,512,512]{2,1,0:T(8,128)(2,1)} %collective-permute-done.refs_1_, ...), custom_call_target="tpu_custom_call" | custom-call | bytes 65536 | tf_op jit(solution)/shard_map/pallas_call | solution.py:82
  41.1 0.6 collective-permute-done.7.m_ref
  41.7 2.4 %shard_map.60 = (f32[128,256]{1,0:T(8,128)S(1)}, bf16[128,256]{1,0:T(8,128)(2,1)S(1)}, bf16[128,256]{1,0:T(8,128)(2,1)S(1)}, bf16[128,256]{1,0:T(8,128)(2,1)S(1)}, f32[512,256]{1,0:T(8,128)S(1)}) custom-call(s32[3]{0:T(128)S(1)} %pad_add_fusion.ids_ref, bf16[2,512,512]{2,1,0:T(8,128)(2,1)S(1)} %get-tuple-element.56.left_ref, ...), custom_call_target="tpu_custom_call" | custom-call | bytes 65536 | tf_op jit(solution)/shard_map/pallas_call | solution.py:82
  44.2 2.5 %collective-permute-start.10 = (bf16[128,256]{1,0:T(8,128)(2,1)S(1)}, bf16[128,256]{1,0:T(8,128)(2,1)S(1)}, u32[]{:S(2)}, u32[]{:S(2)}) collective-permute-start(bf16[128,256]{1,0:T(8,128)(2,1)S(1)} %get-tuple-element.62), channel_id=1, source_target_pairs={{0,12},{4,8},{8,4},{12,0},{1,13},{5,9},{9,5},{13,1},{2,14},{6,10},... | collective-permute-start | bytes 196616 | tf_op jit(solution)/shard_map/ppermute | solution.py:21
  46.7 0.4 collective-permute-start.8
  47.0 1.6 %collective-permute-start.9 = (bf16[128,256]{1,0:T(8,128)(2,1)S(1)}, bf16[128,256]{1,0:T(8,128)(2,1)S(1)}, u32[]{:S(2)}, u32[]{:S(2)}) collective-permute-start(bf16[128,256]{1,0:T(8,128)(2,1)S(1)} %get-tuple-element.61), channel_id=1, source_target_pairs={{0,8},{4,12},{8,0},{12,4},{1,9},{5,13},{9,1},{13,5},{2,10},{6,14},... | collective-permute-start | bytes 196616 | tf_op jit(solution)/shard_map/ppermute | solution.py:21
  48.6 2.3 %shard_map.61 = (f32[128,256]{1,0:T(8,128)S(1)}, bf16[128,256]{1,0:T(8,128)(2,1)S(1)}, bf16[128,256]{1,0:T(8,128)(2,1)S(1)}, bf16[128,256]{1,0:T(8,128)(2,1)S(1)...) custom-call(s32[3]{0:T(128)S(1)} %pad_add_fusion.ids_ref, bf16[2,512,512]{2,1,0:T(8,128)(2,1)S(1)} %get-tuple-element.56.left_ref, ...), custom_call_target="tpu_custom_call" | custom-call | bytes 65536 | tf_op jit(solution)/shard_map/pallas_call | solution.py:82
  50.9 1.2 %collective-permute-start.15 = (bf16[256,512]{1,0:T(8,128)(2,1)S(1)}, bf16[256,512]{1,0:T(8,128)(2,1)S(1)}, u32[]{:S(2)}, u32[]{:S(2)}) collective-permute-start(bf16[256,512]{1,0:T(8,128)(2,1)S(1)} %get-tuple-element.70), channel_id=1, source_target_pairs={{0,2},{1,3},{2,0},{3,1},{4,6},{5,7},{6,4},{7,5},{8,10},{9,11},{10,... | collective-permute-start | bytes 786440 | tf_op jit(solution)/shard_map/ppermute | solution.py:21
  52.1 0.3 collective-permute-start.12
  52.4 0.0 collective-permute-done.10
  52.4 2.7 %collective-permute-start.13 = (bf16[128,256]{1,0:T(8,128)(2,1)S(1)}, bf16[128,256]{1,0:T(8,128)(2,1)S(1)}, u32[]{:S(2)}, u32[]{:S(2)}) collective-permute-start(bf16[128,256]{1,0:T(8,128)(2,1)S(1)} %get-tuple-element.67), channel_id=1, source_target_pairs={{0,8},{4,12},{8,0},{12,4},{1,9},{5,13},{9,1},{13,5},{2,10},{6,14},... | collective-permute-start | bytes 196616 | tf_op jit(solution)/shard_map/ppermute | solution.py:21
  55.1 1.4 %collective-permute-start.14 = (bf16[128,256]{1,0:T(8,128)(2,1)S(1)}, bf16[128,256]{1,0:T(8,128)(2,1)S(1)}, u32[]{:S(2)}, u32[]{:S(2)}) collective-permute-start(bf16[128,256]{1,0:T(8,128)(2,1)S(1)} %get-tuple-element.68), channel_id=1, source_target_pairs={{0,12},{4,8},{8,4},{12,0},{1,13},{5,9},{9,5},{13,1},{2,14},{6,10},... | collective-permute-start | bytes 196616 | tf_op jit(solution)/shard_map/ppermute | solution.py:21
  56.5 0.0 collective-permute-done.9
  56.5 0.0 collective-permute-done.12
  56.6 2.5 %collective-permute-done.13 = bf16[128,256]{1,0:T(8,128)(2,1)S(1)} collective-permute-done((bf16[128,256]{1,0:T(8,128)(2,1)S(1)}, bf16[128,256]{1,0:T(8,128)(2,1)S(1)}, u32[]{:S(2)}, u32[]{:S(2)}) %collective-permute-start.13) | collective-permute-done | bytes 65568 | tf_op jit(solution)/shard_map/ppermute | solution.py:21
  59.0 2.8 %collective-permute-done.14 = bf16[128,256]{1,0:T(8,128)(2,1)S(1)} collective-permute-done((bf16[128,256]{1,0:T(8,128)(2,1)S(1)}, bf16[128,256]{1,0:T(8,128)(2,1)S(1)}, u32[]{:S(2)}, u32[]{:S(2)}) %collective-permute-start.14) | collective-permute-done | bytes 65568 | tf_op jit(solution)/shard_map/ppermute | solution.py:21
  61.8 0.0 collective-permute-done.15.refs_1_
  61.9 0.1 collective-permute-start.19
  62.0 1.3 %collective-permute-start.16 = (bf16[128,512]{1,0:T(8,128)(2,1)S(1)}, bf16[128,512]{1,0:T(8,128)(2,1)S(1)}, u32[]{:S(2)}, u32[]{:S(2)}) collective-permute-start(bf16[128,512]{1,0:T(8,128)(2,1)S(1)} %pad_maximum_fusion.1), channel_id=1, source_target_pairs={{0,8},{4,12},{8,0},{12,4},{1,9},{5,13},{9,1},{13,5},{2,10},{6,14},... | collective-permute-start | bytes 393224 | tf_op jit(solution)/shard_map/ppermute | solution.py:21
  63.3 3.0 %collective-permute-start.17 = (bf16[128,512]{1,0:T(8,128)(2,1)S(1)}, bf16[128,512]{1,0:T(8,128)(2,1)S(1)}, u32[]{:S(2)}, u32[]{:S(2)}) collective-permute-start(bf16[128,512]{1,0:T(8,128)(2,1)S(1)} %pad_maximum_fusion.1), channel_id=1, source_target_pairs={{0,12},{4,8},{8,4},{12,0},{1,13},{5,9},{9,5},{13,1},{2,14},{6,10},... | collective-permute-start | bytes 393224 | tf_op jit(solution)/shard_map/ppermute | solution.py:21
  66.3 0.9 %collective-permute-start.18 = (bf16[128,512]{1,0:T(8,128)(2,1)S(1)}, bf16[128,512]{1,0:T(8,128)(2,1)S(1)}, u32[]{:S(2)}, u32[]{:S(2)}) collective-permute-start(bf16[128,512]{1,0:T(8,128)(2,1)S(1)} %pad_maximum_fusion.1), channel_id=1, source_target_pairs={{0,2},{1,3},{2,0},{3,1},{4,6},{5,7},{6,4},{7,5},{8,10},{9,11},{10,... | collective-permute-start | bytes 393224 | tf_op jit(solution)/shard_map/ppermute | solution.py:21
  67.2 1.1 %collective-permute-done.19 = bf16[128,512]{1,0:T(8,128)(2,1)S(1)} collective-permute-done((bf16[128,512]{1,0:T(8,128)(2,1)S(1)}, bf16[128,512]{1,0:T(8,128)(2,1)S(1)}, u32[]{:S(2)}, u32[]{:S(2)}) %collective-permute-start.19) | collective-permute-done | bytes 131104 | tf_op jit(solution)/shard_map/ppermute | solution.py:21
  68.3 0.9 %collective-permute-start.20 = (bf16[128,512]{1,0:T(8,128)(2,1)S(1)}, bf16[128,512]{1,0:T(8,128)(2,1)S(1)}, u32[]{:S(2)}, u32[]{:S(2)}) collective-permute-start(bf16[128,512]{1,0:T(8,128)(2,1)S(1)} %collective-permute-done.19), channel_id=1, source_target_pairs={{0,2},{1,3},{2,0},{3,1},{4,6},{5,7},{6,4},{7,5},{8,10},{9,11},{10,... | collective-permute-start | bytes 393224 | tf_op jit(solution)/shard_map/ppermute | solution.py:21
  69.2 0.1 collective-permute-start.24
  69.3 2.4 %collective-permute-done.16 = bf16[128,512]{1,0:T(8,128)(2,1)S(1)} collective-permute-done((bf16[128,512]{1,0:T(8,128)(2,1)S(1)}, bf16[128,512]{1,0:T(8,128)(2,1)S(1)}, u32[]{:S(2)}, u32[]{:S(2)}) %collective-permute-start.16) | collective-permute-done | bytes 131104 | tf_op jit(solution)/shard_map/ppermute | solution.py:21
  71.7 0.0 collective-permute-done.17
  71.7 1.6 %collective-permute-done.20 = bf16[128,512]{1,0:T(8,128)(2,1)S(1)} collective-permute-done((bf16[128,512]{1,0:T(8,128)(2,1)S(1)}, bf16[128,512]{1,0:T(8,128)(2,1)S(1)}, u32[]{:S(2)}, u32[]{:S(2)}) %collective-permute-start.20) | collective-permute-done | bytes 131104 | tf_op jit(solution)/shard_map/ppermute | solution.py:21
  73.3 0.6 collective-permute-start.23
  73.9 0.1 collective-permute-start.22
  74.0 0.5 collective-permute-start.26
  74.5 0.9 %collective-permute-start.21 = (bf16[256,512]{1,0:T(8,128)(2,1)S(1)}, bf16[256,512]{1,0:T(8,128)(2,1)S(1)}, u32[]{:S(2)}, u32[]{:S(2)}) collective-permute-start(bf16[256,512]{1,0:T(8,128)(2,1)S(1)} %constant_dynamic-update-slice_fusion.refs_0_), channel_id=1, source_target_pairs={{0,2},{1,3},{2,0},{3,1},{4,6},{5,7},{6,4},{7,5},{8,10},{9,11},{10,... | collective-permute-start | bytes 786440 | tf_op jit(solution)/shard_map/ppermute | solution.py:21
  75.4 1.7 %shard_map.62.refs_2_ = f32[2,2,512,512]{3,2,1,0:T(8,128)} custom-call(s32[3]{0:T(128)S(1)} %pad_add_fusion.ids_ref, f32[2,2,512,512]{3,2,1,0:T(8,128)S(1)} %copy-done.1, bf16[256,512]{1,0:T(8,128)(2,1)S(1)} %pad_maximum_fusion.refs_0_, bf16[256,512]{1,0:T(8,128)(2,1)S(1)} %collective-permute-done.24.refs_1_), custom_call_target="tpu_custom_call" | custom-call | bytes 65536 | tf_op jit(solution)/shard_map/pallas_call | solution.py:65
  77.1 1.7 %shard_map.63.refs_2_ = f32[2,2,512,512]{3,2,1,0:T(8,128)} custom-call(s32[3]{0:T(128)S(1)} %pad_add_fusion.ids_ref, f32[2,2,512,512]{3,2,1,0:T(8,128)S(1)} %copy-done.1, bf16[256,512]{1,0:T(8,128)(2,1)S(1)} %constant_dynamic-update-slice_fusion.refs_0_, bf16[256,512]{1,0:T(8,128)(2,1)S(1)} %collective-permute-done.23.refs_1_, ...), custom_call_target="tpu_custom_call", output_to_operand_aliasing={{}: (4, {})} | custom-call | bytes 65536 | tf_op jit(solution)/shard_map/pallas_call | solution.py:65
  78.8 1.7 %shard_map.64.refs_2_ = f32[2,2,512,512]{3,2,1,0:T(8,128)} custom-call(s32[3]{0:T(128)S(1)} %pad_add_fusion.ids_ref, f32[2,2,512,512]{3,2,1,0:T(8,128)S(1)} %copy-done.1, bf16[256,512]{1,0:T(8,128)(2,1)S(1)} %constant_dynamic-update-slice_fusion.2.refs_0_, bf16[256,512]{1,0:T(8,128)(2,1)S(1)} %collective-permute-done.22.refs_1_, ...), custom_call_target="tpu_custom_call", output_to_operand_aliasing={{}: (4, {})} | custom-call | bytes 65536 | tf_op jit(solution)/shard_map/pallas_call | solution.py:65
  80.5 2.2 %shard_map.65 = f32[128,2,1024]{2,1,0:T(2,128)} custom-call(s32[3]{0:T(128)S(1)} %pad_add_fusion.ids_ref, f32[256,512]{1,0:T(8,128)S(1)} %get-tuple-element.81.refs_0_, bf16[256,512]{1,0:T(8,128)(2,1)S(1)} %collective-permute-done.15.refs_1_, f32[256,512]{1,0:T(8,128)S(1)} %collective-permute-done.25.refs_2_, ...), custom_call_target="tpu_custom_call" | custom-call | bytes 65536 | tf_op jit(solution)/shard_map/pallas_call | solution.py:82
  82.7 0.1 collective-permute-done.21.refs_0_
  82.8 1.5 %collective-permute-done.27.refs_1_ = bf16[256,512]{1,0:T(8,128)(2,1)S(1)} collective-permute-done((bf16[256,512]{1,0:T(8,128)(2,1)S(1)}, bf16[256,512]{1,0:T(8,128)(2,1)S(1)}, u32[]{:S(2)}, u32[]{:S(2)}) %collective-permute-start.27) | collective-permute-done | bytes 262176 | tf_op jit(solution)/shard_map/ppermute | solution.py:21
  84.3 1.7 %shard_map.66 = f32[2,2,512,512]{3,2,1,0:T(8,128)} custom-call(s32[3]{0:T(128)S(1)} %pad_add_fusion.ids_ref, f32[2,2,512,512]{3,2,1,0:T(8,128)S(1)} %copy-done.1, bf16[256,512]{1,0:T(8,128)(2,1)S(1)} %collective-permute-done.21.refs_0_, bf16[256,512]{1,0:T(8,128)(2,1)S(1)} %collective-permute-done.27.refs_1_, ...), custom_call_target="tpu_custom_call", output_to_operand_aliasing={{}: (4, {})} | custom-call | bytes 65536 | tf_op jit(solution)/shard_map/pallas_call | solution.py:65
  (27 shorter events, 0.2 us)
Async XLA Ops:
  0.6 3.7 %copy-start = (bf16[512,2,1024]{2,1,0:T(2,128)(2,1)S(1)}, bf16[512,2,1024]{2,1,0:T(2,128)(2,1)}, u32[]{:S(2)}) copy-start(bf16[512,2,1024]{2,1,0:T(2,128)(2,1)} %param.5) | copy-start | bytes 6291460
  0.6 31.6 %collective-permute-start.5 = (bf16[2,512,512]{2,1,0:T(8,128)(2,1)}, bf16[2,512,512]{2,1,0:T(8,128)(2,1)}, u32[]{:S(2)}, u32[]{:S(2)}) collective-permute-start(bf16[2,512,512]{2,1,0:T(8,128)(2,1)} %refs_0_.1), channel_id=1, source_target_pairs={{0,2},{1,3},{2,0},{3,1},{4,6},{5,7},{6,4},{7,5},{8,10},{9,11},{10,... | collective-permute-start | bytes 3145736 | tf_op jit(solution)/shard_map/ppermute | solution.py:21
  6.1 15.9 %collective-permute-start.2 = (bf16[512,256]{1,0:T(8,128)(2,1)}, bf16[512,256]{1,0:T(8,128)(2,1)}, u32[]{:S(2)}, u32[]{:S(2)}) collective-permute-start(bf16[512,256]{1,0:T(8,128)(2,1)} %get-tuple-element.50.refs_4_), channel_id=1, source_target_pairs={{0,8},{4,12},{8,0},{12,4},{1,9},{5,13},{9,1},{13,5},{2,10},{6,14},... | collective-permute-start | bytes 786440 | tf_op jit(solution)/shard_map/ppermute | solution.py:21
  8.7 19.7 %collective-permute-start.1 = (bf16[512,256]{1,0:T(8,128)(2,1)}, bf16[512,256]{1,0:T(8,128)(2,1)}, u32[]{:S(2)}, u32[]{:S(2)}) collective-permute-start(bf16[512,256]{1,0:T(8,128)(2,1)} %get-tuple-element.50.refs_4_), channel_id=1, source_target_pairs={{0,4},{4,0},{8,12},{12,8},{1,5},{5,1},{9,13},{13,9},{2,6},{6,2},{1... | collective-permute-start | bytes 786440 | tf_op jit(solution)/shard_map/ppermute | solution.py:21
  10.2 22.0 %collective-permute-start.3 = (bf16[512,256]{1,0:T(8,128)(2,1)S(1)}, bf16[512,256]{1,0:T(8,128)(2,1)}, u32[]{:S(2)}, u32[]{:S(2)}) collective-permute-start(bf16[512,256]{1,0:T(8,128)(2,1)S(1)} %get-tuple-element.53.refs_7_), channel_id=1, source_target_pairs={{0,4},{4,0},{8,12},{12,8},{1,5},{5,1},{9,13},{13,9},{2,6},{6,2},{1... | collective-permute-start | bytes 786440 | tf_op jit(solution)/shard_map/ppermute | solution.py:21
  10.7 21.5 %collective-permute-start.4 = (bf16[512,256]{1,0:T(8,128)(2,1)S(1)}, bf16[512,256]{1,0:T(8,128)(2,1)}, u32[]{:S(2)}, u32[]{:S(2)}) collective-permute-start(bf16[512,256]{1,0:T(8,128)(2,1)S(1)} %get-tuple-element.53.refs_7_), channel_id=1, source_target_pairs={{0,8},{4,12},{8,0},{12,4},{1,9},{5,13},{9,1},{13,5},{2,10},{6,14},... | collective-permute-start | bytes 786440 | tf_op jit(solution)/shard_map/ppermute | solution.py:21
  21.9 12.5 %collective-permute-start = (bf16[2,512,512]{2,1,0:T(8,128)(2,1)}, bf16[2,512,512]{2,1,0:T(8,128)(2,1)}, u32[]{:S(2)}, u32[]{:S(2)}) collective-permute-start(bf16[2,512,512]{2,1,0:T(8,128)(2,1)} %refs_0_.1), channel_id=1, source_target_pairs={{0,1},{1,0},{2,3},{3,2},{4,5},{5,4},{6,7},{7,6},{8,9},{9,8},{10,11... | collective-permute-start | bytes 3145736 | tf_op jit(solution)/shard_map/ppermute | solution.py:21
  32.2 3.0 %collective-permute-start.6 = (bf16[2,512,512]{2,1,0:T(8,128)(2,1)}, bf16[2,512,512]{2,1,0:T(8,128)(2,1)}, u32[]{:S(2)}, u32[]{:S(2)}) collective-permute-start(bf16[2,512,512]{2,1,0:T(8,128)(2,1)} %collective-permute-done.5.refs_2_), channel_id=1, source_target_pairs={{0,1},{1,0},{2,3},{3,2},{4,5},{5,4},{6,7},{7,6},{8,9},{9,8},{10,11... | collective-permute-start | bytes 3145736 | tf_op jit(solution)/shard_map/ppermute | solution.py:21
  32.2 9.5 %collective-permute-start.7 = (bf16[512,256]{1,0:T(8,128)(2,1)}, bf16[512,256]{1,0:T(8,128)(2,1)}, u32[]{:S(2)}, u32[]{:S(2)}) collective-permute-start(bf16[512,256]{1,0:T(8,128)(2,1)} %collective-permute-done.2.refs_6_), channel_id=1, source_target_pairs={{0,4},{4,0},{8,12},{12,8},{1,5},{5,1},{9,13},{13,9},{2,6},{6,2},{1... | collective-permute-start | bytes 786440 | tf_op jit(solution)/shard_map/ppermute | solution.py:21
  33.5 15.1 %collective-permute-start.11 = (bf16[512,256]{1,0:T(8,128)(2,1)}, bf16[512,256]{1,0:T(8,128)(2,1)}, u32[]{:S(2)}, u32[]{:S(2)}) collective-permute-start(bf16[512,256]{1,0:T(8,128)(2,1)} %collective-permute-done.4.refs_9_), channel_id=1, source_target_pairs={{0,4},{4,0},{8,12},{12,8},{1,5},{5,1},{9,13},{13,9},{2,6},{6,2},{1... | collective-permute-start | bytes 786440 | tf_op jit(solution)/shard_map/ppermute | solution.py:21
  35.2 1.2 %copy-start.2 = (bf16[2,512,512]{2,1,0:T(8,128)(2,1)S(1)}, bf16[2,512,512]{2,1,0:T(8,128)(2,1)}, u32[]{:S(2)}) copy-start(bf16[2,512,512]{2,1,0:T(8,128)(2,1)} %refs_0_.1) | copy-start | bytes 3145732
  41.7 33.7 %copy-start.1 = (f32[2,2,512,512]{3,2,1,0:T(8,128)S(1)}, f32[2,2,512,512]{3,2,1,0:T(8,128)}, u32[]{:S(2)}) copy-start(f32[2,2,512,512]{3,2,1,0:T(8,128)} %pivot_ref.7) | copy-start | bytes 12582916
  44.2 8.3 %collective-permute-start.10 = (bf16[128,256]{1,0:T(8,128)(2,1)S(1)}, bf16[128,256]{1,0:T(8,128)(2,1)S(1)}, u32[]{:S(2)}, u32[]{:S(2)}) collective-permute-start(bf16[128,256]{1,0:T(8,128)(2,1)S(1)} %get-tuple-element.62), channel_id=1, source_target_pairs={{0,12},{4,8},{8,4},{12,0},{1,13},{5,9},{9,5},{13,1},{2,14},{6,10},... | collective-permute-start | bytes 196616 | tf_op jit(solution)/shard_map/ppermute | solution.py:21
  46.7 8.4 %collective-permute-start.8 = (bf16[128,256]{1,0:T(8,128)(2,1)S(1)}, bf16[128,256]{1,0:T(8,128)(2,1)S(1)}, u32[]{:S(2)}, u32[]{:S(2)}) collective-permute-start(bf16[128,256]{1,0:T(8,128)(2,1)S(1)} %get-tuple-element.60), channel_id=1, source_target_pairs={{0,4},{4,0},{8,12},{12,8},{1,5},{5,1},{9,13},{13,9},{2,6},{6,2},{1... | collective-permute-start | bytes 196616 | tf_op jit(solution)/shard_map/ppermute | solution.py:21
  47.0 9.5 %collective-permute-start.9 = (bf16[128,256]{1,0:T(8,128)(2,1)S(1)}, bf16[128,256]{1,0:T(8,128)(2,1)S(1)}, u32[]{:S(2)}, u32[]{:S(2)}) collective-permute-start(bf16[128,256]{1,0:T(8,128)(2,1)S(1)} %get-tuple-element.61), channel_id=1, source_target_pairs={{0,8},{4,12},{8,0},{12,4},{1,9},{5,13},{9,1},{13,5},{2,10},{6,14},... | collective-permute-start | bytes 196616 | tf_op jit(solution)/shard_map/ppermute | solution.py:21
  50.9 10.9 %collective-permute-start.15 = (bf16[256,512]{1,0:T(8,128)(2,1)S(1)}, bf16[256,512]{1,0:T(8,128)(2,1)S(1)}, u32[]{:S(2)}, u32[]{:S(2)}) collective-permute-start(bf16[256,512]{1,0:T(8,128)(2,1)S(1)} %get-tuple-element.70), channel_id=1, source_target_pairs={{0,2},{1,3},{2,0},{3,1},{4,6},{5,7},{6,4},{7,5},{8,10},{9,11},{10,... | collective-permute-start | bytes 786440 | tf_op jit(solution)/shard_map/ppermute | solution.py:21
  52.1 4.5 %collective-permute-start.12 = (bf16[128,256]{1,0:T(8,128)(2,1)S(1)}, bf16[128,256]{1,0:T(8,128)(2,1)S(1)}, u32[]{:S(2)}, u32[]{:S(2)}) collective-permute-start(bf16[128,256]{1,0:T(8,128)(2,1)S(1)} %get-tuple-element.66), channel_id=1, source_target_pairs={{0,4},{4,0},{8,12},{12,8},{1,5},{5,1},{9,13},{13,9},{2,6},{6,2},{1... | collective-permute-start | bytes 196616 | tf_op jit(solution)/shard_map/ppermute | solution.py:21
  52.4 6.6 %collective-permute-start.13 = (bf16[128,256]{1,0:T(8,128)(2,1)S(1)}, bf16[128,256]{1,0:T(8,128)(2,1)S(1)}, u32[]{:S(2)}, u32[]{:S(2)}) collective-permute-start(bf16[128,256]{1,0:T(8,128)(2,1)S(1)} %get-tuple-element.67), channel_id=1, source_target_pairs={{0,8},{4,12},{8,0},{12,4},{1,9},{5,13},{9,1},{13,5},{2,10},{6,14},... | collective-permute-start | bytes 196616 | tf_op jit(solution)/shard_map/ppermute | solution.py:21
  55.1 6.7 %collective-permute-start.14 = (bf16[128,256]{1,0:T(8,128)(2,1)S(1)}, bf16[128,256]{1,0:T(8,128)(2,1)S(1)}, u32[]{:S(2)}, u32[]{:S(2)}) collective-permute-start(bf16[128,256]{1,0:T(8,128)(2,1)S(1)} %get-tuple-element.68), channel_id=1, source_target_pairs={{0,12},{4,8},{8,4},{12,0},{1,13},{5,9},{9,5},{13,1},{2,14},{6,10},... | collective-permute-start | bytes 196616 | tf_op jit(solution)/shard_map/ppermute | solution.py:21
  61.9 6.4 %collective-permute-start.19 = (bf16[128,512]{1,0:T(8,128)(2,1)S(1)}, bf16[128,512]{1,0:T(8,128)(2,1)S(1)}, u32[]{:S(2)}, u32[]{:S(2)}) collective-permute-start(bf16[128,512]{1,0:T(8,128)(2,1)S(1)} %pad_maximum_fusion.1), channel_id=1, source_target_pairs={{0,4},{4,0},{8,12},{12,8},{1,5},{5,1},{9,13},{13,9},{2,6},{6,2},{1... | collective-permute-start | bytes 393224 | tf_op jit(solution)/shard_map/ppermute | solution.py:21
  62.0 9.7 %collective-permute-start.16 = (bf16[128,512]{1,0:T(8,128)(2,1)S(1)}, bf16[128,512]{1,0:T(8,128)(2,1)S(1)}, u32[]{:S(2)}, u32[]{:S(2)}) collective-permute-start(bf16[128,512]{1,0:T(8,128)(2,1)S(1)} %pad_maximum_fusion.1), channel_id=1, source_target_pairs={{0,8},{4,12},{8,0},{12,4},{1,9},{5,13},{9,1},{13,5},{2,10},{6,14},... | collective-permute-start | bytes 393224 | tf_op jit(solution)/shard_map/ppermute | solution.py:21
  63.3 8.4 %collective-permute-start.17 = (bf16[128,512]{1,0:T(8,128)(2,1)S(1)}, bf16[128,512]{1,0:T(8,128)(2,1)S(1)}, u32[]{:S(2)}, u32[]{:S(2)}) collective-permute-start(bf16[128,512]{1,0:T(8,128)(2,1)S(1)} %pad_maximum_fusion.1), channel_id=1, source_target_pairs={{0,12},{4,8},{8,4},{12,0},{1,13},{5,9},{9,5},{13,1},{2,14},{6,10},... | collective-permute-start | bytes 393224 | tf_op jit(solution)/shard_map/ppermute | solution.py:21
  66.3 5.4 %collective-permute-start.18 = (bf16[128,512]{1,0:T(8,128)(2,1)S(1)}, bf16[128,512]{1,0:T(8,128)(2,1)S(1)}, u32[]{:S(2)}, u32[]{:S(2)}) collective-permute-start(bf16[128,512]{1,0:T(8,128)(2,1)S(1)} %pad_maximum_fusion.1), channel_id=1, source_target_pairs={{0,2},{1,3},{2,0},{3,1},{4,6},{5,7},{6,4},{7,5},{8,10},{9,11},{10,... | collective-permute-start | bytes 393224 | tf_op jit(solution)/shard_map/ppermute | solution.py:21
  68.3 5.0 %collective-permute-start.20 = (bf16[128,512]{1,0:T(8,128)(2,1)S(1)}, bf16[128,512]{1,0:T(8,128)(2,1)S(1)}, u32[]{:S(2)}, u32[]{:S(2)}) collective-permute-start(bf16[128,512]{1,0:T(8,128)(2,1)S(1)} %collective-permute-done.19), channel_id=1, source_target_pairs={{0,2},{1,3},{2,0},{3,1},{4,6},{5,7},{6,4},{7,5},{8,10},{9,11},{10,... | collective-permute-start | bytes 393224 | tf_op jit(solution)/shard_map/ppermute | solution.py:21
  69.2 5.3 %collective-permute-start.24 = (bf16[256,512]{1,0:T(8,128)(2,1)S(1)}, bf16[256,512]{1,0:T(8,128)(2,1)S(1)}, u32[]{:S(2)}, u32[]{:S(2)}) collective-permute-start(bf16[256,512]{1,0:T(8,128)(2,1)S(1)} %pad_maximum_fusion.refs_0_), channel_id=1, source_target_pairs={{0,1},{1,0},{2,3},{3,2},{4,5},{5,4},{6,7},{7,6},{8,9},{9,8},{10,11... | collective-permute-start | bytes 786440 | tf_op jit(solution)/shard_map/ppermute | solution.py:21
  73.3 7.3 %collective-permute-start.25 = (f32[256,512]{1,0:T(8,128)S(1)}, f32[256,512]{1,0:T(8,128)S(1)}, u32[]{:S(2)}, u32[]{:S(2)}) collective-permute-start(f32[256,512]{1,0:T(8,128)S(1)} %get-tuple-element.81.refs_0_), channel_id=1, source_target_pairs={{0,1},{1,0},{2,3},{3,2},{4,5},{5,4},{6,7},{7,6},{8,9},{9,8},{10,11... | collective-permute-start | bytes 1572872 | tf_op jit(solution)/shard_map/ppermute | solution.py:21
  73.3 3.8 %collective-permute-start.23 = (bf16[256,512]{1,0:T(8,128)(2,1)S(1)}, bf16[256,512]{1,0:T(8,128)(2,1)S(1)}, u32[]{:S(2)}, u32[]{:S(2)}) collective-permute-start(bf16[256,512]{1,0:T(8,128)(2,1)S(1)} %constant_dynamic-update-slice_fusion.refs_0_), channel_id=1, source_target_pairs={{0,1},{1,0},{2,3},{3,2},{4,5},{5,4},{6,7},{7,6},{8,9},{9,8},{10,11... | collective-permute-start | bytes 786440 | tf_op jit(solution)/shard_map/ppermute | solution.py:21
  73.9 4.9 %collective-permute-start.22 = (bf16[256,512]{1,0:T(8,128)(2,1)S(1)}, bf16[256,512]{1,0:T(8,128)(2,1)S(1)}, u32[]{:S(2)}, u32[]{:S(2)}) collective-permute-start(bf16[256,512]{1,0:T(8,128)(2,1)S(1)} %constant_dynamic-update-slice_fusion.2.refs_0_), channel_id=1, source_target_pairs={{0,1},{1,0},{2,3},{3,2},{4,5},{5,4},{6,7},{7,6},{8,9},{9,8},{10,11... | collective-permute-start | bytes 786440 | tf_op jit(solution)/shard_map/ppermute | solution.py:21
  74.0 6.5 %collective-permute-start.26 = (bf16[256,512]{1,0:T(8,128)(2,1)S(1)}, bf16[256,512]{1,0:T(8,128)(2,1)S(1)}, u32[]{:S(2)}, u32[]{:S(2)}) collective-permute-start(bf16[256,512]{1,0:T(8,128)(2,1)S(1)} %collective-permute-done.15.refs_1_), channel_id=1, source_target_pairs={{0,1},{1,0},{2,3},{3,2},{4,5},{5,4},{6,7},{7,6},{8,9},{9,8},{10,11... | collective-permute-start | bytes 786440 | tf_op jit(solution)/shard_map/ppermute | solution.py:21
  74.5 8.3 %collective-permute-start.21 = (bf16[256,512]{1,0:T(8,128)(2,1)S(1)}, bf16[256,512]{1,0:T(8,128)(2,1)S(1)}, u32[]{:S(2)}, u32[]{:S(2)}) collective-permute-start(bf16[256,512]{1,0:T(8,128)(2,1)S(1)} %constant_dynamic-update-slice_fusion.refs_0_), channel_id=1, source_target_pairs={{0,2},{1,3},{2,0},{3,1},{4,6},{5,7},{6,4},{7,5},{8,10},{9,11},{10,... | collective-permute-start | bytes 786440 | tf_op jit(solution)/shard_map/ppermute | solution.py:21
  82.8 1.5 %collective-permute-start.27 = (bf16[256,512]{1,0:T(8,128)(2,1)S(1)}, bf16[256,512]{1,0:T(8,128)(2,1)S(1)}, u32[]{:S(2)}, u32[]{:S(2)}) collective-permute-start(bf16[256,512]{1,0:T(8,128)(2,1)S(1)} %collective-permute-done.21.refs_0_), channel_id=1, source_target_pairs={{0,1},{1,0},{2,3},{3,2},{4,5},{5,4},{6,7},{7,6},{8,9},{9,8},{10,11... | collective-permute-start | bytes 786440 | tf_op jit(solution)/shard_map/ppermute | solution.py:21

commit v5 on v4

--- a/solution.py
+++ b/solution.py
@@ -61,13 +61,13 @@
     return jnp.concatenate([-m[:, width:], m[:, :width]], axis=1)
 
 
-def call(body, out_shape, scalars, operands, specs, out_specs, scratch=(), aliases=None):
+def call(body, out_shape, scalars, operands, specs, out_specs, scratch=(), aliases=None, steps=1):
     return pl.pallas_call(
         body,
         out_shape=out_shape,
         grid_spec=pltpu.PrefetchScalarGridSpec(
             num_scalar_prefetch=1,
-            grid=(1,),
+            grid=(steps,),
             in_specs=specs,
             out_specs=out_specs,
             scratch_shapes=scratch,
@@ -144,23 +144,27 @@
 
     def body(ids_ref, left_ref, m_ref, total_ref, side_ref, *refs):
         before_refs, refs = refs[: len(before)], refs[len(before) :]
-        p_out, y_out, y_ref, p_ref = refs[:levels], refs[levels:-2], refs[-2], refs[-1]
+        p_out, y_out = refs[:levels], refs[levels:-2]
+        chosen_ref, turned_ref = refs[-2:]
         m = m_ref[...]
-        y_ref[...] = -(total_ref[...] + dot(left_ref[0], m) + dot(left_ref[1], turn(m)))
-        chosen = y_ref[...].astype(bf16)
-        p_ref[...] = dot(side_ref[0], chosen) + dot(side_ref[1], turn(chosen))
+        turned = turn(m)
+        for e in range(columns):
+            here = pl.ds(pl.multiple_of((ids_ref[1] ^ e) * cut, cut), cut)
+            y = -(total_ref[here, :] + dot(left_ref[0, here, :], m) + dot(left_ref[1, here, :], turned))
+            chosen = y.astype(bf16)
+            chosen_ref[here, :] = chosen
+            turned_ref[here, :] = turn(chosen)
+            if not final:
+                y_out[0][here, :] = y
+                continue
+            at = slice(e % 2 * cut, (e % 2 + 1) * cut)
+            for n, value in enumerate([ref[here, :] for ref in before_refs] + [y]):
+                y_out[e // 2][at, n * wide : (n + 1) * wide] = value.astype(y_out[e // 2].dtype)
+        chosen, turned = chosen_ref[...], turned_ref[...]
         for d in range(levels):
-            start = pl.multiple_of((ids_ref[0] ^ d) * share, share)
-            p_out[d][...] = p_ref[pl.ds(start, share), :].astype(p_out[d].dtype)
-        if not final:
-            y_out[0][...] = y_ref[...]
-            return
-        for e in range(columns):
-            start = pl.multiple_of((ids_ref[1] ^ e) * cut, cut)
-            at = slice(e % 2 * cut, (e % 2 + 1) * cut)
-            for n, ref in enumerate(list(before_refs) + [y_ref]):
-                value = ref[pl.ds(start, cut), :].astype(y_out[e // 2].dtype)
-                y_out[e // 2][at, n * wide : (n + 1) * wide] = value
+            here = pl.ds(pl.multiple_of((ids_ref[0] ^ d) * share, share), share)
+            part = dot(side_ref[0, here, :], chosen) + dot(side_ref[1, here, :], turned)
+            p_out[d][...] = part.astype(p_out[d].dtype)
 
     shapes = [jax.ShapeDtypeStruct((share, wide), f32 if d == 0 else bf16) for d in range(levels)]
     if final:
@@ -174,7 +178,7 @@
         shapes,
         ids,
         operands,
-        [pltpu.VMEM((rows, wide), f32), pltpu.VMEM((S, wide), f32)],
+        [pltpu.VMEM((rows, wide), bf16)] * 2,
     )
     return out[:levels], out[levels:]
 
@@ -205,34 +209,54 @@
     return call_here(body, shape, ids, stacks)
 
 
-def take_off(pivot, stacks, flip, late, levels, ids, rest=None):
+def take_off(pivot, jobs, levels, ids, rest=None):
+    stacks = [p for _, _, groups in jobs for group in groups for p in group]
     wide = stacks[0].shape[1]
     width = wide // 2
     per_node = S // width
-    half = levels // 2
+    part_levels = levels // 2
     share = S // levels
-    first = per_node * flip
 
     def body(ids_ref, pivot_ref, *refs):
-        for e, ref in enumerate(refs[: len(stacks)]):
-            left = pl.multiple_of(((ids_ref[1] ^ (first + e)) % per_node) * width, width)
-            for d in range(half):
-                top = pl.multiple_of(((ids_ref[0] ^ d) % half) * share, share)
-                for part in range(2):
-                    at = (0, part, pl.ds(top, share), pl.ds(left, width))
-                    piece = ref[d * share : (d + 1) * share, part * width : (part + 1) * width]
-                    refs[-1][at] = pivot_ref[at] - piece.astype(f32)
-
-    spec = pl.BlockSpec(
-        (1, 2, S // 2, S), lambda i, ids: (ids[2] ^ flip, 0, (ids[0] // half) ^ late, 0)
-    )
-    operands, specs, aliases = [pivot] + stacks, [spec] + [whole(p) for p in stacks], {}
+        out_ref, refs = refs[-1], list(refs)
+        for job, (flip, half, groups) in enumerate(jobs):
+            mine = [[(refs.pop(0), p.shape[0]) for p in group] for group in groups]
+
+            @pl.when(pl.program_id(0) == job)
+            def _():
+                base = ((ids_ref[0] // part_levels) ^ half) * (S // 2)
+                for e, group in enumerate(mine):
+                    left = pl.multiple_of(((ids_ref[1] ^ e) % per_node) * width, width)
+                    d = 0
+                    for ref, height in group:
+                        for row in range(0, height, share):
+                            top = pl.multiple_of(((ids_ref[0] ^ d) % part_levels) * share, share)
+                            source = pl.multiple_of(base + top, share)
+                            for part in range(2):
+                                piece = ref[row : row + share, part * width : (part + 1) * width]
+                                old = pivot_ref[
+                                    ids_ref[2] ^ flip, part, pl.ds(source, share), pl.ds(left, width)
+                                ]
+                                out_ref[0, part, pl.ds(top, share), pl.ds(left, width)] = (
+                                    old - piece.astype(f32)
+                                )
+                            d += 1
+
+    def place(i, ids):
+        flip, half = jobs[-1][0], jobs[-1][1]
+        for job in range(len(jobs) - 1):
+            flip = jnp.where(i == job, jobs[job][0], flip)
+            half = jnp.where(i == job, jobs[job][1], half)
+        return ids[2] ^ flip, 0, (ids[0] // part_levels) ^ half, 0
+
+    spec = pl.BlockSpec((1, 2, S // 2, S), place)
+    operands, aliases = [pivot] + stacks, {}
+    specs = [pl.BlockSpec(memory_space=pltpu.VMEM)] * len(operands)
     if rest is not None:
         operands, specs = operands + [rest], specs + [pl.BlockSpec(memory_space=pl.ANY)]
         aliases = {len(operands): 0}
-    return call(
-        body, jax.ShapeDtypeStruct(pivot.shape, f32), ids, operands, specs, spec, aliases=aliases
-    )
+    shape = jax.ShapeDtypeStruct(pivot.shape, f32)
+    return call(body, shape, ids, operands, specs, spec, aliases=aliases, steps=len(jobs))
 
 
 def join(sums):
@@ -280,9 +304,13 @@
     parts = [
         [p[0]] + [swap(p[d], "prow", d) for d in range(1, levels)] for p in parts
     ]
-    parts[-1], y_stacks = lax.optimization_barrier((parts[-1], y_stacks))
-    sums = [sum((p.astype(f32) for p in received[1:]), received[0]) for received in parts]
-    sums = [total.astype(bf16) for total in sums]
+    sums = []
+    for received in parts:
+        if len(sums) == chunks - 1:
+            received, y_stacks = lax.optimization_barrier((received, y_stacks))
+        sums, received = lax.optimization_barrier((sums, received))
+        total = sum((p.astype(f32) for p in received[1:]), received[0])
+        sums = sums + [total.astype(bf16)]
 
     half = levels // 2
     sums = join(sums)
@@ -299,19 +327,22 @@
     early = jnp.concatenate(early, 0)
     early_across = {e: jnp.concatenate([a[e] for a in early_across], 0) for e in late_across}
     take = functools.partial(take_off, pivot_inverse, levels=levels, ids=ids)
+    one = lambda stacks: [[p] for p in stacks]
     if per_node == 2:
-        pivot = take(gather_core({0: early}), 0, 0)
-        pivot = take(gather_core({0: late}), 0, 1, rest=pivot)
-        pivot = take(gather_core(early_across), 1, 0, rest=pivot)
+        pivot = take([(0, 0, one(gather_core({0: early}))), (1, 0, one(gather_core(early_across)))])
+        pivot = take([(0, 1, one(gather_core({0: late})))], rest=pivot)
         late_across, pivot, own_rows = lax.optimization_barrier((late_across, pivot, own_rows))
-        pivot = take(gather_core(late_across), 1, 1, rest=pivot)
+        pivot = take([(1, 1, one(gather_core(late_across)))], rest=pivot)
     else:
-        early = gather_core({0: early} | early_across)
-        late = gather_core({0: late} | late_across)
-        pivot = take(early[:per_node], 0, 0)
-        pivot = take(late[:per_node], 0, 1, rest=pivot)
-        pivot = take(early[per_node:], 1, 0, rest=pivot)
-        pivot = take(late[per_node:], 1, 1, rest=pivot)
+        early = one(gather_core({0: early} | early_across))
+        late = one(gather_core({0: late} | late_across))
+        pivot = take(
+            [
+                (flip, half, part[flip * per_node : (flip + 1) * per_node])
+                for flip in range(2)
+                for half, part in enumerate((early, late))
+            ]
+        )
     return own_rows, pivot
 
 

time: 86.3 us -> 85.1 us (0.986)
  Pallas kernels: 18.4 us -> 16 us
  waiting for transfers between devices: 30 us -> 31.2 us
    pallas_call x4 -> x3, Pallas kernels: 6.85 us -> 5.26 us  [call(): pl.pallas_call(body, out_shape=out_shape, grid_spec=pltpu.PrefetchScalarG...]
    ppermute x28, waiting for transfers between devices: 30 us -> 31.2 us  [swap(): return lax.ppermute(x, axis, [(i, i ^ distance) for i in range(size)])]
  transfers between devices with their start and end apart: 28 -> 28, of which waited for: 12 -> 13; matrix products, arithmetic and copies ran while one was open for 8% -> 8% of each run, Pallas kernels for 19% -> 17%
where the time goes in v5:
time: 85.1 us; the launch traced here: 84.9 us
  waiting for transfers between devices  31.2 us (37%)
  starting transfers between devices  28.5 us (33%)
  Pallas kernels  16 us (19%)
  local copies, waits for them, and re-layouts  6.05 us (7%)
  other arithmetic  2.33 us (3%)
    ppermute x28, waiting for transfers between devices, swap(): return lax.ppermute(x, axis, [(i, i ^ distance) for i in range(size)])  31.2 us
    ppermute x28, starting transfers between devices, swap(): return lax.ppermute(x, axis, [(i, i ^ distance) for i in range(size)])  28.5 us
    pallas_call x4, Pallas kernels, call_here(): pl.pallas_call(body, out_shape=out_shape, in_specs=[pl.BlockSpec(memory_s...  10.7 us
    pallas_call x3, Pallas kernels, call(): pl.pallas_call(body, out_shape=out_shape, grid_spec=pltpu.PrefetchScalarG...  5.26 us
    unnamed x9, local copies, waits for them, and re-layouts  3.74 us
  transfers between devices with their start and end apart: 28, of which 13 were waited for; matrix products, arithmetic and copies ran while one was open for 8% of the time, Pallas kernels for 17%

profile of v5, /device:TPU:0, one launch (start us, length us, event | category | flops | bytes accessed | tf_op | source)
XLA Modules:
  0.0 84.9 jit_solution(7835119004122321322)
XLA Ops:
  0.6 0.0 copy-start
  0.6 3.0 %collective-permute-start.5 = (bf16[2,512,512]{2,1,0:T(8,128)(2,1)}, bf16[2,512,512]{2,1,0:T(8,128)(2,1)}, u32[]{:S(2)}, u32[]{:S(2)}) collective-permute-start(bf16[2,512,512]{2,1,0:T(8,128)(2,1)} %refs_0_.1), channel_id=1, source_target_pairs={{0,2},{1,3},{2,0},{3,1},{4,6},{5,7},{6,4},{7,5},{8,10},{9,11},{10,... | collective-permute-start | bytes 3145736 | tf_op jit(solution)/shard_map/ppermute | solution.py:21
  3.6 0.7 fusion
  4.3 0.4 constant_dynamic-slice_fusion.2
  4.7 0.4 fusion.1
  5.1 0.1 copy_bitcast_fusion
  5.2 0.1 broadcast_bitcast_fusion
  5.2 0.8 broadcast_multiply_fusion
  6.1 2.6 %collective-permute-start.2 = (bf16[512,256]{1,0:T(8,128)(2,1)}, bf16[512,256]{1,0:T(8,128)(2,1)}, u32[]{:S(2)}, u32[]{:S(2)}) collective-permute-start(bf16[512,256]{1,0:T(8,128)(2,1)} %get-tuple-element.59.refs_4_), channel_id=1, source_target_pairs={{0,8},{4,12},{8,0},{12,4},{1,9},{5,13},{9,1},{13,5},{2,10},{6,14},... | collective-permute-start | bytes 786440 | tf_op jit(solution)/shard_map/ppermute | solution.py:21
  8.7 1.6 %collective-permute-start.1 = (bf16[512,256]{1,0:T(8,128)(2,1)}, bf16[512,256]{1,0:T(8,128)(2,1)}, u32[]{:S(2)}, u32[]{:S(2)}) collective-permute-start(bf16[512,256]{1,0:T(8,128)(2,1)} %get-tuple-element.59.refs_4_), channel_id=1, source_target_pairs={{0,4},{4,0},{8,12},{12,8},{1,5},{5,1},{9,13},{13,9},{2,6},{6,2},{1... | collective-permute-start | bytes 786440 | tf_op jit(solution)/shard_map/ppermute | solution.py:21
  10.2 0.4 collective-permute-start.3
  10.7 0.3 collective-permute-start.4
  11.0 0.7 constant_dynamic-slice_fusion
  11.8 2.5 %copy.9 = bf16[512,2,512]{0,2,1:T(8,128)(2,1)} copy(bf16[512,2,512]{2,1,0:T(2,128)(2,1)S(1)} %constant_dynamic-slice_fusion) | data formatting | bytes 2097152
  14.2 1.3 %multiply_bitcast_fusion.side_ref = bf16[2,512,512]{2,1,0:T(8,128)(2,1)S(1)} fusion(bf16[512,2,512]{0,2,1:T(8,128)(2,1)} %copy.9, bf16[512]{0:T(512)(128)(2,1)S(1)} %broadcast_bitcast_fusion), kind=kLoop, calls=%fused_computation | loop fusion | flops 524288 | bytes 2098176 | tf_op jit(solution)/shard_map/transpose | solution.py:290
  15.5 6.4 %collective-permute-done.2.refs_6_ = bf16[512,256]{1,0:T(8,128)(2,1)} collective-permute-done((bf16[512,256]{1,0:T(8,128)(2,1)}, bf16[512,256]{1,0:T(8,128)(2,1)}, u32[]{:S(2)}, u32[]{:S(2)}) %collective-permute-start.2) | collective-permute-done | bytes 262176 | tf_op jit(solution)/shard_map/ppermute | solution.py:21
  21.9 0.0 collective-permute-start
  21.9 6.4 %collective-permute-done.1.refs_5_ = bf16[512,256]{1,0:T(8,128)(2,1)} collective-permute-done((bf16[512,256]{1,0:T(8,128)(2,1)}, bf16[512,256]{1,0:T(8,128)(2,1)}, u32[]{:S(2)}, u32[]{:S(2)}) %collective-permute-start.1) | collective-permute-done | bytes 262176 | tf_op jit(solution)/shard_map/ppermute | solution.py:21
  28.4 3.9 %collective-permute-done.3.refs_8_ = bf16[512,256]{1,0:T(8,128)(2,1)} collective-permute-done((bf16[512,256]{1,0:T(8,128)(2,1)S(1)}, bf16[512,256]{1,0:T(8,128)(2,1)}, u32[]{:S(2)}, u32[]{:S(2)}) %collective-permute-start.3) | collective-permute-done | bytes 262176 | tf_op jit(solution)/shard_map/ppermute | solution.py:21
  32.2 0.0 collective-permute-done.4.refs_9_
  32.2 0.0 collective-permute-done.5.refs_2_
  32.2 1.3 %collective-permute-start.7 = (bf16[512,256]{1,0:T(8,128)(2,1)}, bf16[512,256]{1,0:T(8,128)(2,1)}, u32[]{:S(2)}, u32[]{:S(2)}) collective-permute-start(bf16[512,256]{1,0:T(8,128)(2,1)} %collective-permute-done.2.refs_6_), channel_id=1, source_target_pairs={{0,4},{4,0},{8,12},{12,8},{1,5},{5,1},{9,13},{13,9},{2,6},{6,2},{1... | collective-permute-start | bytes 786440 | tf_op jit(solution)/shard_map/ppermute | solution.py:21
  33.5 0.8 collective-permute-start.11
  34.3 0.1 pad_add_fusion.ids_ref
  34.4 0.8 collective-permute-done.6.refs_3_
  35.2 1.2 %copy-done.2 = bf16[2,512,512]{2,1,0:T(8,128)(2,1)S(1)} copy-done((bf16[2,512,512]{2,1,0:T(8,128)(2,1)S(1)}, bf16[2,512,512]{2,1,0:T(8,128)(2,1)}, u32[]{:S(2)}) %copy-start.2) | copy-done | bytes 1048600
  36.4 4.6 %shard_map.59 = (f32[512,256]{1,0:T(8,128)S(1)}, f32[512,256]{1,0:T(8,128)S(1)}, bf16[2,512,512]{2,1,0:T(8,128)(2,1)S(1)}) custom-call(s32[3]{0:T(128)S(1)} %pad_add_fusion.ids_ref, bf16[2,512,512]{2,1,0:T(8,128)(2,1)S(1)} %copy-done.2, bf16[2,512,512]{2,1,0:T(8,128)(2,1)} %collective-permute-done.refs_1_, ...), custom_call_target="tpu_custom_call" | custom-call | bytes 65536 | tf_op jit(solution)/shard_map/pallas_call | solution.py:82
  41.1 0.6 collective-permute-done.7.m_ref
  41.7 2.0 %shard_map.60 = (f32[128,256]{1,0:T(8,128)S(1)}, bf16[128,256]{1,0:T(8,128)(2,1)S(1)}, bf16[128,256]{1,0:T(8,128)(2,1)S(1)}, bf16[128,256]{1,0:T(8,128)(2,1)S(1)}, f32[512,256]{1,0:T(8,128)S(1)}) custom-call(s32[3]{0:T(128)S(1)} %pad_add_fusion.ids_ref, bf16[2,512,512]{2,1,0:T(8,128)(2,1)S(1)} %get-tuple-element.65.left_ref, ...), custom_call_target="tpu_custom_call" | custom-call | bytes 65536 | tf_op jit(solution)/shard_map/pallas_call | solution.py:82
  43.8 2.5 %collective-permute-start.10 = (bf16[128,256]{1,0:T(8,128)(2,1)S(1)}, bf16[128,256]{1,0:T(8,128)(2,1)S(1)}, u32[]{:S(2)}, u32[]{:S(2)}) collective-permute-start(bf16[128,256]{1,0:T(8,128)(2,1)S(1)} %get-tuple-element.71), channel_id=1, source_target_pairs={{0,12},{4,8},{8,4},{12,0},{1,13},{5,9},{9,5},{13,1},{2,14},{6,10},... | collective-permute-start | bytes 196616 | tf_op jit(solution)/shard_map/ppermute | solution.py:21
  46.3 0.3 collective-permute-start.8
  46.6 1.6 %collective-permute-start.9 = (bf16[128,256]{1,0:T(8,128)(2,1)S(1)}, bf16[128,256]{1,0:T(8,128)(2,1)S(1)}, u32[]{:S(2)}, u32[]{:S(2)}) collective-permute-start(bf16[128,256]{1,0:T(8,128)(2,1)S(1)} %get-tuple-element.70), channel_id=1, source_target_pairs={{0,8},{4,12},{8,0},{12,4},{1,9},{5,13},{9,1},{13,5},{2,10},{6,14},... | collective-permute-start | bytes 196616 | tf_op jit(solution)/shard_map/ppermute | solution.py:21
  48.2 0.0 collective-permute-done.11.m_ref
  48.2 1.9 %shard_map.61 = (f32[128,256]{1,0:T(8,128)S(1)}, bf16[128,256]{1,0:T(8,128)(2,1)S(1)}, bf16[128,256]{1,0:T(8,128)(2,1)S(1)}, bf16[128,256]{1,0:T(8,128)(2,1)S(1)...) custom-call(s32[3]{0:T(128)S(1)} %pad_add_fusion.ids_ref, bf16[2,512,512]{2,1,0:T(8,128)(2,1)S(1)} %get-tuple-element.65.left_ref, ...), custom_call_target="tpu_custom_call" | custom-call | bytes 65536 | tf_op jit(solution)/shard_map/pallas_call | solution.py:82
  50.1 1.2 %collective-permute-start.15 = (bf16[256,512]{1,0:T(8,128)(2,1)S(1)}, bf16[256,512]{1,0:T(8,128)(2,1)S(1)}, u32[]{:S(2)}, u32[]{:S(2)}) collective-permute-start(bf16[256,512]{1,0:T(8,128)(2,1)S(1)} %get-tuple-element.83), channel_id=1, source_target_pairs={{0,2},{1,3},{2,0},{3,1},{4,6},{5,7},{6,4},{7,5},{8,10},{9,11},{10,... | collective-permute-start | bytes 786440 | tf_op jit(solution)/shard_map/ppermute | solution.py:21
  51.3 0.3 collective-permute-start.12
  51.6 2.7 %collective-permute-start.13 = (bf16[128,256]{1,0:T(8,128)(2,1)S(1)}, bf16[128,256]{1,0:T(8,128)(2,1)S(1)}, u32[]{:S(2)}, u32[]{:S(2)}) collective-permute-start(bf16[128,256]{1,0:T(8,128)(2,1)S(1)} %get-tuple-element.80), channel_id=1, source_target_pairs={{0,8},{4,12},{8,0},{12,4},{1,9},{5,13},{9,1},{13,5},{2,10},{6,14},... | collective-permute-start | bytes 196616 | tf_op jit(solution)/shard_map/ppermute | solution.py:21
  54.3 0.0 collective-permute-done.8
  54.3 1.4 %collective-permute-start.14 = (bf16[128,256]{1,0:T(8,128)(2,1)S(1)}, bf16[128,256]{1,0:T(8,128)(2,1)S(1)}, u32[]{:S(2)}, u32[]{:S(2)}) collective-permute-start(bf16[128,256]{1,0:T(8,128)(2,1)S(1)} %get-tuple-element.81), channel_id=1, source_target_pairs={{0,12},{4,8},{8,4},{12,0},{1,13},{5,9},{9,5},{13,1},{2,14},{6,10},... | collective-permute-start | bytes 196616 | tf_op jit(solution)/shard_map/ppermute | solution.py:21
  55.7 0.0 collective-permute-done.9
  55.7 0.0 collective-permute-done.12
  55.7 2.5 %collective-permute-done.13 = bf16[128,256]{1,0:T(8,128)(2,1)S(1)} collective-permute-done((bf16[128,256]{1,0:T(8,128)(2,1)S(1)}, bf16[128,256]{1,0:T(8,128)(2,1)S(1)}, u32[]{:S(2)}, u32[]{:S(2)}) %collective-permute-start.13) | collective-permute-done | bytes 65568 | tf_op jit(solution)/shard_map/ppermute | solution.py:21
  58.2 2.2 %collective-permute-done.14 = bf16[128,256]{1,0:T(8,128)(2,1)S(1)} collective-permute-done((bf16[128,256]{1,0:T(8,128)(2,1)S(1)}, bf16[128,256]{1,0:T(8,128)(2,1)S(1)}, u32[]{:S(2)}, u32[]{:S(2)}) %collective-permute-start.14) | collective-permute-done | bytes 65568 | tf_op jit(solution)/shard_map/ppermute | solution.py:21
  60.4 0.0 collective-permute-done.15.refs_1_
  60.5 0.1 collective-permute-start.19
  60.6 2.0 %collective-permute-start.16 = (bf16[128,512]{1,0:T(8,128)(2,1)S(1)}, bf16[128,512]{1,0:T(8,128)(2,1)S(1)}, u32[]{:S(2)}, u32[]{:S(2)}) collective-permute-start(bf16[128,512]{1,0:T(8,128)(2,1)S(1)} %pad_maximum_fusion.1), channel_id=1, source_target_pairs={{0,8},{4,12},{8,0},{12,4},{1,9},{5,13},{9,1},{13,5},{2,10},{6,14},... | collective-permute-start | bytes 393224 | tf_op jit(solution)/shard_map/ppermute | solution.py:21
  62.6 2.4 %collective-permute-start.17 = (bf16[128,512]{1,0:T(8,128)(2,1)S(1)}, bf16[128,512]{1,0:T(8,128)(2,1)S(1)}, u32[]{:S(2)}, u32[]{:S(2)}) collective-permute-start(bf16[128,512]{1,0:T(8,128)(2,1)S(1)} %pad_maximum_fusion.1), channel_id=1, source_target_pairs={{0,12},{4,8},{8,4},{12,0},{1,13},{5,9},{9,5},{13,1},{2,14},{6,10},... | collective-permute-start | bytes 393224 | tf_op jit(solution)/shard_map/ppermute | solution.py:21
  65.0 0.9 %collective-permute-start.18 = (bf16[128,512]{1,0:T(8,128)(2,1)S(1)}, bf16[128,512]{1,0:T(8,128)(2,1)S(1)}, u32[]{:S(2)}, u32[]{:S(2)}) collective-permute-start(bf16[128,512]{1,0:T(8,128)(2,1)S(1)} %pad_maximum_fusion.1), channel_id=1, source_target_pairs={{0,2},{1,3},{2,0},{3,1},{4,6},{5,7},{6,4},{7,5},{8,10},{9,11},{10,... | collective-permute-start | bytes 393224 | tf_op jit(solution)/shard_map/ppermute | solution.py:21
  65.9 1.3 %collective-permute-done.19 = bf16[128,512]{1,0:T(8,128)(2,1)S(1)} collective-permute-done((bf16[128,512]{1,0:T(8,128)(2,1)S(1)}, bf16[128,512]{1,0:T(8,128)(2,1)S(1)}, u32[]{:S(2)}, u32[]{:S(2)}) %collective-permute-start.19) | collective-permute-done | bytes 131104 | tf_op jit(solution)/shard_map/ppermute | solution.py:21
  67.2 0.9 %collective-permute-start.20 = (bf16[128,512]{1,0:T(8,128)(2,1)S(1)}, bf16[128,512]{1,0:T(8,128)(2,1)S(1)}, u32[]{:S(2)}, u32[]{:S(2)}) collective-permute-start(bf16[128,512]{1,0:T(8,128)(2,1)S(1)} %collective-permute-done.19), channel_id=1, source_target_pairs={{0,2},{1,3},{2,0},{3,1},{4,6},{5,7},{6,4},{7,5},{8,10},{9,11},{10,... | collective-permute-start | bytes 393224 | tf_op jit(solution)/shard_map/ppermute | solution.py:21
  68.2 0.1 collective-permute-start.23
  68.2 2.6 %collective-permute-done.16 = bf16[128,512]{1,0:T(8,128)(2,1)S(1)} collective-permute-done((bf16[128,512]{1,0:T(8,128)(2,1)S(1)}, bf16[128,512]{1,0:T(8,128)(2,1)S(1)}, u32[]{:S(2)}, u32[]{:S(2)}) %collective-permute-start.16) | collective-permute-done | bytes 131104 | tf_op jit(solution)/shard_map/ppermute | solution.py:21
  70.9 1.3 %collective-permute-done.20 = bf16[128,512]{1,0:T(8,128)(2,1)S(1)} collective-permute-done((bf16[128,512]{1,0:T(8,128)(2,1)S(1)}, bf16[128,512]{1,0:T(8,128)(2,1)S(1)}, u32[]{:S(2)}, u32[]{:S(2)}) %collective-permute-start.20) | collective-permute-done | bytes 131104 | tf_op jit(solution)/shard_map/ppermute | solution.py:21
  72.2 0.6 collective-permute-start.24
  72.8 0.1 collective-permute-start.22
  72.9 0.5 collective-permute-start.26
  73.4 0.9 %collective-permute-start.21 = (bf16[256,512]{1,0:T(8,128)(2,1)S(1)}, bf16[256,512]{1,0:T(8,128)(2,1)S(1)}, u32[]{:S(2)}, u32[]{:S(2)}) collective-permute-start(bf16[256,512]{1,0:T(8,128)(2,1)S(1)} %constant_dynamic-update-slice_fusion.refs_0_), channel_id=1, source_target_pairs={{0,2},{1,3},{2,0},{3,1},{4,6},{5,7},{6,4},{7,5},{8,10},{9,11},{10,... | collective-permute-start | bytes 786440 | tf_op jit(solution)/shard_map/ppermute | solution.py:21
  74.3 0.1 collective-permute-done.24.refs_3_
  74.5 2.0 %shard_map.62.refs_2_ = f32[2,2,512,512]{3,2,1,0:T(8,128)} custom-call(s32[3]{0:T(128)S(1)} %pad_add_fusion.ids_ref, f32[2,2,512,512]{3,2,1,0:T(8,128)S(1)} %copy-done.1, bf16[256,512]{1,0:T(8,128)(2,1)S(1)} %pad_maximum_fusion.refs_0_, bf16[256,512]{1,0:T(8,128)(2,1)S(1)} %collective-permute-done.23.refs_1_, ...), custom_call_target="tpu_custom_call" | custom-call | bytes 65536 | tf_op jit(solution)/shard_map/pallas_call | solution.py:65
  76.5 1.6 %shard_map.63.refs_2_ = f32[2,2,512,512]{3,2,1,0:T(8,128)} custom-call(s32[3]{0:T(128)S(1)} %pad_add_fusion.ids_ref, f32[2,2,512,512]{3,2,1,0:T(8,128)S(1)} %copy-done.1, bf16[256,512]{1,0:T(8,128)(2,1)S(1)} %constant_dynamic-update-slice_fusion.refs_0_, bf16[256,512]{1,0:T(8,128)(2,1)S(1)} %collective-permute-done.22.refs_1_, ...), custom_call_target="tpu_custom_call", output_to_operand_aliasing={{}: (4, {})} | custom-call | bytes 65536 | tf_op jit(solution)/shard_map/pallas_call | solution.py:65
  78.1 2.2 %shard_map.64 = f32[128,2,1024]{2,1,0:T(2,128)} custom-call(s32[3]{0:T(128)S(1)} %pad_add_fusion.ids_ref, f32[256,512]{1,0:T(8,128)S(1)} %get-tuple-element.99.refs_0_, bf16[256,512]{1,0:T(8,128)(2,1)S(1)} %collective-permute-done.15.refs_1_, f32[256,512]{1,0:T(8,128)S(1)} %collective-permute-done.25.refs_2_, ...), custom_call_target="tpu_custom_call" | custom-call | bytes 65536 | tf_op jit(solution)/shard_map/pallas_call | solution.py:82
  80.3 1.4 %collective-permute-done.21.refs_0_ = bf16[256,512]{1,0:T(8,128)(2,1)S(1)} collective-permute-done((bf16[256,512]{1,0:T(8,128)(2,1)S(1)}, bf16[256,512]{1,0:T(8,128)(2,1)S(1)}, u32[]{:S(2)}, u32[]{:S(2)}) %collective-permute-start.21) | collective-permute-done | bytes 262176 | tf_op jit(solution)/shard_map/ppermute | solution.py:21
  81.7 1.5 %collective-permute-done.27.refs_1_ = bf16[256,512]{1,0:T(8,128)(2,1)S(1)} collective-permute-done((bf16[256,512]{1,0:T(8,128)(2,1)S(1)}, bf16[256,512]{1,0:T(8,128)(2,1)S(1)}, u32[]{:S(2)}, u32[]{:S(2)}) %collective-permute-start.27) | collective-permute-done | bytes 262176 | tf_op jit(solution)/shard_map/ppermute | solution.py:21
  83.2 1.6 %shard_map.65 = f32[2,2,512,512]{3,2,1,0:T(8,128)} custom-call(s32[3]{0:T(128)S(1)} %pad_add_fusion.ids_ref, f32[2,2,512,512]{3,2,1,0:T(8,128)S(1)} %copy-done.1, bf16[256,512]{1,0:T(8,128)(2,1)S(1)} %collective-permute-done.21.refs_0_, bf16[256,512]{1,0:T(8,128)(2,1)S(1)} %collective-permute-done.27.refs_1_, ...), custom_call_target="tpu_custom_call", output_to_operand_aliasing={{}: (4, {})} | custom-call | bytes 65536 | tf_op jit(solution)/shard_map/pallas_call | solution.py:65
  (26 shorter events, 0.2 us)
Async XLA Ops:
  0.6 3.7 %copy-start = (bf16[512,2,1024]{2,1,0:T(2,128)(2,1)S(1)}, bf16[512,2,1024]{2,1,0:T(2,128)(2,1)}, u32[]{:S(2)}) copy-start(bf16[512,2,1024]{2,1,0:T(2,128)(2,1)} %param.5) | copy-start | bytes 6291460
  0.6 31.6 %collective-permute-start.5 = (bf16[2,512,512]{2,1,0:T(8,128)(2,1)}, bf16[2,512,512]{2,1,0:T(8,128)(2,1)}, u32[]{:S(2)}, u32[]{:S(2)}) collective-permute-start(bf16[2,512,512]{2,1,0:T(8,128)(2,1)} %refs_0_.1), channel_id=1, source_target_pairs={{0,2},{1,3},{2,0},{3,1},{4,6},{5,7},{6,4},{7,5},{8,10},{9,11},{10,... | collective-permute-start | bytes 3145736 | tf_op jit(solution)/shard_map/ppermute | solution.py:21
  6.1 15.9 %collective-permute-start.2 = (bf16[512,256]{1,0:T(8,128)(2,1)}, bf16[512,256]{1,0:T(8,128)(2,1)}, u32[]{:S(2)}, u32[]{:S(2)}) collective-permute-start(bf16[512,256]{1,0:T(8,128)(2,1)} %get-tuple-element.59.refs_4_), channel_id=1, source_target_pairs={{0,8},{4,12},{8,0},{12,4},{1,9},{5,13},{9,1},{13,5},{2,10},{6,14},... | collective-permute-start | bytes 786440 | tf_op jit(solution)/shard_map/ppermute | solution.py:21
  8.7 19.7 %collective-permute-start.1 = (bf16[512,256]{1,0:T(8,128)(2,1)}, bf16[512,256]{1,0:T(8,128)(2,1)}, u32[]{:S(2)}, u32[]{:S(2)}) collective-permute-start(bf16[512,256]{1,0:T(8,128)(2,1)} %get-tuple-element.59.refs_4_), channel_id=1, source_target_pairs={{0,4},{4,0},{8,12},{12,8},{1,5},{5,1},{9,13},{13,9},{2,6},{6,2},{1... | collective-permute-start | bytes 786440 | tf_op jit(solution)/shard_map/ppermute | solution.py:21
  10.2 22.0 %collective-permute-start.3 = (bf16[512,256]{1,0:T(8,128)(2,1)S(1)}, bf16[512,256]{1,0:T(8,128)(2,1)}, u32[]{:S(2)}, u32[]{:S(2)}) collective-permute-start(bf16[512,256]{1,0:T(8,128)(2,1)S(1)} %get-tuple-element.62.refs_7_), channel_id=1, source_target_pairs={{0,4},{4,0},{8,12},{12,8},{1,5},{5,1},{9,13},{13,9},{2,6},{6,2},{1... | collective-permute-start | bytes 786440 | tf_op jit(solution)/shard_map/ppermute | solution.py:21
  10.7 21.5 %collective-permute-start.4 = (bf16[512,256]{1,0:T(8,128)(2,1)S(1)}, bf16[512,256]{1,0:T(8,128)(2,1)}, u32[]{:S(2)}, u32[]{:S(2)}) collective-permute-start(bf16[512,256]{1,0:T(8,128)(2,1)S(1)} %get-tuple-element.62.refs_7_), channel_id=1, source_target_pairs={{0,8},{4,12},{8,0},{12,4},{1,9},{5,13},{9,1},{13,5},{2,10},{6,14},... | collective-permute-start | bytes 786440 | tf_op jit(solution)/shard_map/ppermute | solution.py:21
  21.9 12.5 %collective-permute-start = (bf16[2,512,512]{2,1,0:T(8,128)(2,1)}, bf16[2,512,512]{2,1,0:T(8,128)(2,1)}, u32[]{:S(2)}, u32[]{:S(2)}) collective-permute-start(bf16[2,512,512]{2,1,0:T(8,128)(2,1)} %refs_0_.1), channel_id=1, source_target_pairs={{0,1},{1,0},{2,3},{3,2},{4,5},{5,4},{6,7},{7,6},{8,9},{9,8},{10,11... | collective-permute-start | bytes 3145736 | tf_op jit(solution)/shard_map/ppermute | solution.py:21
  32.2 3.0 %collective-permute-start.6 = (bf16[2,512,512]{2,1,0:T(8,128)(2,1)}, bf16[2,512,512]{2,1,0:T(8,128)(2,1)}, u32[]{:S(2)}, u32[]{:S(2)}) collective-permute-start(bf16[2,512,512]{2,1,0:T(8,128)(2,1)} %collective-permute-done.5.refs_2_), channel_id=1, source_target_pairs={{0,1},{1,0},{2,3},{3,2},{4,5},{5,4},{6,7},{7,6},{8,9},{9,8},{10,11... | collective-permute-start | bytes 3145736 | tf_op jit(solution)/shard_map/ppermute | solution.py:21
  32.2 9.5 %collective-permute-start.7 = (bf16[512,256]{1,0:T(8,128)(2,1)}, bf16[512,256]{1,0:T(8,128)(2,1)}, u32[]{:S(2)}, u32[]{:S(2)}) collective-permute-start(bf16[512,256]{1,0:T(8,128)(2,1)} %collective-permute-done.2.refs_6_), channel_id=1, source_target_pairs={{0,4},{4,0},{8,12},{12,8},{1,5},{5,1},{9,13},{13,9},{2,6},{6,2},{1... | collective-permute-start | bytes 786440 | tf_op jit(solution)/shard_map/ppermute | solution.py:21
  33.5 14.7 %collective-permute-start.11 = (bf16[512,256]{1,0:T(8,128)(2,1)}, bf16[512,256]{1,0:T(8,128)(2,1)}, u32[]{:S(2)}, u32[]{:S(2)}) collective-permute-start(bf16[512,256]{1,0:T(8,128)(2,1)} %collective-permute-done.4.refs_9_), channel_id=1, source_target_pairs={{0,4},{4,0},{8,12},{12,8},{1,5},{5,1},{9,13},{13,9},{2,6},{6,2},{1... | collective-permute-start | bytes 786440 | tf_op jit(solution)/shard_map/ppermute | solution.py:21
  35.2 1.2 %copy-start.2 = (bf16[2,512,512]{2,1,0:T(8,128)(2,1)S(1)}, bf16[2,512,512]{2,1,0:T(8,128)(2,1)}, u32[]{:S(2)}) copy-start(bf16[2,512,512]{2,1,0:T(8,128)(2,1)} %refs_0_.1) | copy-start | bytes 3145732
  41.7 32.7 %copy-start.1 = (f32[2,2,512,512]{3,2,1,0:T(8,128)S(1)}, f32[2,2,512,512]{3,2,1,0:T(8,128)}, u32[]{:S(2)}) copy-start(f32[2,2,512,512]{3,2,1,0:T(8,128)} %pivot_ref.5) | copy-start | bytes 12582916
  43.8 7.8 %collective-permute-start.10 = (bf16[128,256]{1,0:T(8,128)(2,1)S(1)}, bf16[128,256]{1,0:T(8,128)(2,1)S(1)}, u32[]{:S(2)}, u32[]{:S(2)}) collective-permute-start(bf16[128,256]{1,0:T(8,128)(2,1)S(1)} %get-tuple-element.71), channel_id=1, source_target_pairs={{0,12},{4,8},{8,4},{12,0},{1,13},{5,9},{9,5},{13,1},{2,14},{6,10},... | collective-permute-start | bytes 196616 | tf_op jit(solution)/shard_map/ppermute | solution.py:21
  46.3 8.0 %collective-permute-start.8 = (bf16[128,256]{1,0:T(8,128)(2,1)S(1)}, bf16[128,256]{1,0:T(8,128)(2,1)S(1)}, u32[]{:S(2)}, u32[]{:S(2)}) collective-permute-start(bf16[128,256]{1,0:T(8,128)(2,1)S(1)} %get-tuple-element.69), channel_id=1, source_target_pairs={{0,4},{4,0},{8,12},{12,8},{1,5},{5,1},{9,13},{13,9},{2,6},{6,2},{1... | collective-permute-start | bytes 196616 | tf_op jit(solution)/shard_map/ppermute | solution.py:21
  46.6 9.0 %collective-permute-start.9 = (bf16[128,256]{1,0:T(8,128)(2,1)S(1)}, bf16[128,256]{1,0:T(8,128)(2,1)S(1)}, u32[]{:S(2)}, u32[]{:S(2)}) collective-permute-start(bf16[128,256]{1,0:T(8,128)(2,1)S(1)} %get-tuple-element.70), channel_id=1, source_target_pairs={{0,8},{4,12},{8,0},{12,4},{1,9},{5,13},{9,1},{13,5},{2,10},{6,14},... | collective-permute-start | bytes 196616 | tf_op jit(solution)/shard_map/ppermute | solution.py:21
  50.1 10.3 %collective-permute-start.15 = (bf16[256,512]{1,0:T(8,128)(2,1)S(1)}, bf16[256,512]{1,0:T(8,128)(2,1)S(1)}, u32[]{:S(2)}, u32[]{:S(2)}) collective-permute-start(bf16[256,512]{1,0:T(8,128)(2,1)S(1)} %get-tuple-element.83), channel_id=1, source_target_pairs={{0,2},{1,3},{2,0},{3,1},{4,6},{5,7},{6,4},{7,5},{8,10},{9,11},{10,... | collective-permute-start | bytes 786440 | tf_op jit(solution)/shard_map/ppermute | solution.py:21
  51.3 4.4 %collective-permute-start.12 = (bf16[128,256]{1,0:T(8,128)(2,1)S(1)}, bf16[128,256]{1,0:T(8,128)(2,1)S(1)}, u32[]{:S(2)}, u32[]{:S(2)}) collective-permute-start(bf16[128,256]{1,0:T(8,128)(2,1)S(1)} %get-tuple-element.79), channel_id=1, source_target_pairs={{0,4},{4,0},{8,12},{12,8},{1,5},{5,1},{9,13},{13,9},{2,6},{6,2},{1... | collective-permute-start | bytes 196616 | tf_op jit(solution)/shard_map/ppermute | solution.py:21
  51.6 6.6 %collective-permute-start.13 = (bf16[128,256]{1,0:T(8,128)(2,1)S(1)}, bf16[128,256]{1,0:T(8,128)(2,1)S(1)}, u32[]{:S(2)}, u32[]{:S(2)}) collective-permute-start(bf16[128,256]{1,0:T(8,128)(2,1)S(1)} %get-tuple-element.80), channel_id=1, source_target_pairs={{0,8},{4,12},{8,0},{12,4},{1,9},{5,13},{9,1},{13,5},{2,10},{6,14},... | collective-permute-start | bytes 196616 | tf_op jit(solution)/shard_map/ppermute | solution.py:21
  54.3 6.1 %collective-permute-start.14 = (bf16[128,256]{1,0:T(8,128)(2,1)S(1)}, bf16[128,256]{1,0:T(8,128)(2,1)S(1)}, u32[]{:S(2)}, u32[]{:S(2)}) collective-permute-start(bf16[128,256]{1,0:T(8,128)(2,1)S(1)} %get-tuple-element.81), channel_id=1, source_target_pairs={{0,12},{4,8},{8,4},{12,0},{1,13},{5,9},{9,5},{13,1},{2,14},{6,10},... | collective-permute-start | bytes 196616 | tf_op jit(solution)/shard_map/ppermute | solution.py:21
  60.5 6.7 %collective-permute-start.19 = (bf16[128,512]{1,0:T(8,128)(2,1)S(1)}, bf16[128,512]{1,0:T(8,128)(2,1)S(1)}, u32[]{:S(2)}, u32[]{:S(2)}) collective-permute-start(bf16[128,512]{1,0:T(8,128)(2,1)S(1)} %pad_maximum_fusion.1), channel_id=1, source_target_pairs={{0,4},{4,0},{8,12},{12,8},{1,5},{5,1},{9,13},{13,9},{2,6},{6,2},{1... | collective-permute-start | bytes 393224 | tf_op jit(solution)/shard_map/ppermute | solution.py:21
  60.6 10.3 %collective-permute-start.16 = (bf16[128,512]{1,0:T(8,128)(2,1)S(1)}, bf16[128,512]{1,0:T(8,128)(2,1)S(1)}, u32[]{:S(2)}, u32[]{:S(2)}) collective-permute-start(bf16[128,512]{1,0:T(8,128)(2,1)S(1)} %pad_maximum_fusion.1), channel_id=1, source_target_pairs={{0,8},{4,12},{8,0},{12,4},{1,9},{5,13},{9,1},{13,5},{2,10},{6,14},... | collective-permute-start | bytes 393224 | tf_op jit(solution)/shard_map/ppermute | solution.py:21
  62.6 8.3 %collective-permute-start.17 = (bf16[128,512]{1,0:T(8,128)(2,1)S(1)}, bf16[128,512]{1,0:T(8,128)(2,1)S(1)}, u32[]{:S(2)}, u32[]{:S(2)}) collective-permute-start(bf16[128,512]{1,0:T(8,128)(2,1)S(1)} %pad_maximum_fusion.1), channel_id=1, source_target_pairs={{0,12},{4,8},{8,4},{12,0},{1,13},{5,9},{9,5},{13,1},{2,14},{6,10},... | collective-permute-start | bytes 393224 | tf_op jit(solution)/shard_map/ppermute | solution.py:21
  65.0 5.9 %collective-permute-start.18 = (bf16[128,512]{1,0:T(8,128)(2,1)S(1)}, bf16[128,512]{1,0:T(8,128)(2,1)S(1)}, u32[]{:S(2)}, u32[]{:S(2)}) collective-permute-start(bf16[128,512]{1,0:T(8,128)(2,1)S(1)} %pad_maximum_fusion.1), channel_id=1, source_target_pairs={{0,2},{1,3},{2,0},{3,1},{4,6},{5,7},{6,4},{7,5},{8,10},{9,11},{10,... | collective-permute-start | bytes 393224 | tf_op jit(solution)/shard_map/ppermute | solution.py:21
  67.2 5.0 %collective-permute-start.20 = (bf16[128,512]{1,0:T(8,128)(2,1)S(1)}, bf16[128,512]{1,0:T(8,128)(2,1)S(1)}, u32[]{:S(2)}, u32[]{:S(2)}) collective-permute-start(bf16[128,512]{1,0:T(8,128)(2,1)S(1)} %collective-permute-done.19), channel_id=1, source_target_pairs={{0,2},{1,3},{2,0},{3,1},{4,6},{5,7},{6,4},{7,5},{8,10},{9,11},{10,... | collective-permute-start | bytes 393224 | tf_op jit(solution)/shard_map/ppermute | solution.py:21
  68.2 5.2 %collective-permute-start.23 = (bf16[256,512]{1,0:T(8,128)(2,1)S(1)}, bf16[256,512]{1,0:T(8,128)(2,1)S(1)}, u32[]{:S(2)}, u32[]{:S(2)}) collective-permute-start(bf16[256,512]{1,0:T(8,128)(2,1)S(1)} %pad_maximum_fusion.refs_0_), channel_id=1, source_target_pairs={{0,1},{1,0},{2,3},{3,2},{4,5},{5,4},{6,7},{7,6},{8,9},{9,8},{10,11... | collective-permute-start | bytes 786440 | tf_op jit(solution)/shard_map/ppermute | solution.py:21
  72.2 5.9 %collective-permute-start.25 = (f32[256,512]{1,0:T(8,128)S(1)}, f32[256,512]{1,0:T(8,128)S(1)}, u32[]{:S(2)}, u32[]{:S(2)}) collective-permute-start(f32[256,512]{1,0:T(8,128)S(1)} %get-tuple-element.99.refs_0_), channel_id=1, source_target_pairs={{0,1},{1,0},{2,3},{3,2},{4,5},{5,4},{6,7},{7,6},{8,9},{9,8},{10,11... | collective-permute-start | bytes 1572872 | tf_op jit(solution)/shard_map/ppermute | solution.py:21
  72.2 2.2 %collective-permute-start.24 = (bf16[256,512]{1,0:T(8,128)(2,1)S(1)}, bf16[256,512]{1,0:T(8,128)(2,1)S(1)}, u32[]{:S(2)}, u32[]{:S(2)}) collective-permute-start(bf16[256,512]{1,0:T(8,128)(2,1)S(1)} %constant_dynamic-update-slice_fusion.2.refs_2_), channel_id=1, source_target_pairs={{0,1},{1,0},{2,3},{3,2},{4,5},{5,4},{6,7},{7,6},{8,9},{9,8},{10,11... | collective-permute-start | bytes 786440 | tf_op jit(solution)/shard_map/ppermute | solution.py:21
  72.8 3.7 %collective-permute-start.22 = (bf16[256,512]{1,0:T(8,128)(2,1)S(1)}, bf16[256,512]{1,0:T(8,128)(2,1)S(1)}, u32[]{:S(2)}, u32[]{:S(2)}) collective-permute-start(bf16[256,512]{1,0:T(8,128)(2,1)S(1)} %constant_dynamic-update-slice_fusion.refs_0_), channel_id=1, source_target_pairs={{0,1},{1,0},{2,3},{3,2},{4,5},{5,4},{6,7},{7,6},{8,9},{9,8},{10,11... | collective-permute-start | bytes 786440 | tf_op jit(solution)/shard_map/ppermute | solution.py:21
  72.9 5.2 %collective-permute-start.26 = (bf16[256,512]{1,0:T(8,128)(2,1)S(1)}, bf16[256,512]{1,0:T(8,128)(2,1)S(1)}, u32[]{:S(2)}, u32[]{:S(2)}) collective-permute-start(bf16[256,512]{1,0:T(8,128)(2,1)S(1)} %collective-permute-done.15.refs_1_), channel_id=1, source_target_pairs={{0,1},{1,0},{2,3},{3,2},{4,5},{5,4},{6,7},{7,6},{8,9},{9,8},{10,11... | collective-permute-start | bytes 786440 | tf_op jit(solution)/shard_map/ppermute | solution.py:21
  73.4 8.3 %collective-permute-start.21 = (bf16[256,512]{1,0:T(8,128)(2,1)S(1)}, bf16[256,512]{1,0:T(8,128)(2,1)S(1)}, u32[]{:S(2)}, u32[]{:S(2)}) collective-permute-start(bf16[256,512]{1,0:T(8,128)(2,1)S(1)} %constant_dynamic-update-slice_fusion.refs_0_), channel_id=1, source_target_pairs={{0,2},{1,3},{2,0},{3,1},{4,6},{5,7},{6,4},{7,5},{8,10},{9,11},{10,... | collective-permute-start | bytes 786440 | tf_op jit(solution)/shard_map/ppermute | solution.py:21
  81.7 1.5 %collective-permute-start.27 = (bf16[256,512]{1,0:T(8,128)(2,1)S(1)}, bf16[256,512]{1,0:T(8,128)(2,1)S(1)}, u32[]{:S(2)}, u32[]{:S(2)}) collective-permute-start(bf16[256,512]{1,0:T(8,128)(2,1)S(1)} %collective-permute-done.21.refs_0_), channel_id=1, source_target_pairs={{0,1},{1,0},{2,3},{3,2},{4,5},{5,4},{6,7},{7,6},{8,9},{9,8},{10,11... | collective-permute-start | bytes 786440 | tf_op jit(solution)/shard_map/ppermute | solution.py:21

commit v6 on v5

--- a/solution.py
+++ b/solution.py
@@ -144,27 +144,30 @@
 
     def body(ids_ref, left_ref, m_ref, total_ref, side_ref, *refs):
         before_refs, refs = refs[: len(before)], refs[len(before) :]
-        p_out, y_out = refs[:levels], refs[levels:-2]
-        chosen_ref, turned_ref = refs[-2:]
+        p_out, y_out = refs[:levels], refs[levels:-3]
+        chosen_ref, turned_ref, y_all = refs[-3:]
         m = m_ref[...]
         turned = turn(m)
-        for e in range(columns):
-            here = pl.ds(pl.multiple_of((ids_ref[1] ^ e) * cut, cut), cut)
+        tile = rows // 2
+        for top in range(0, rows, tile):
+            here = slice(top, top + tile)
             y = -(total_ref[here, :] + dot(left_ref[0, here, :], m) + dot(left_ref[1, here, :], turned))
-            chosen = y.astype(bf16)
-            chosen_ref[here, :] = chosen
-            turned_ref[here, :] = turn(chosen)
-            if not final:
-                y_out[0][here, :] = y
-                continue
-            at = slice(e % 2 * cut, (e % 2 + 1) * cut)
-            for n, value in enumerate([ref[here, :] for ref in before_refs] + [y]):
-                y_out[e // 2][at, n * wide : (n + 1) * wide] = value.astype(y_out[e // 2].dtype)
+            (y_all if final else y_out[0])[here, :] = y
+            chosen_ref[here, :] = y.astype(bf16)
+            turned_ref[here, :] = turn(y.astype(bf16))
         chosen, turned = chosen_ref[...], turned_ref[...]
         for d in range(levels):
             here = pl.ds(pl.multiple_of((ids_ref[0] ^ d) * share, share), share)
             part = dot(side_ref[0, here, :], chosen) + dot(side_ref[1, here, :], turned)
             p_out[d][...] = part.astype(p_out[d].dtype)
+
+        if not final:
+            return
+        for e in range(columns):
+            here = pl.ds(pl.multiple_of((ids_ref[1] ^ e) * cut, cut), cut)
+            at = slice(e % 2 * cut, (e % 2 + 1) * cut)
+            for n, ref in enumerate(list(before_refs) + [y_all]):
+                y_out[e // 2][at, n * wide : (n + 1) * wide] = ref[here, :].astype(y_out[e // 2].dtype)
 
     shapes = [jax.ShapeDtypeStruct((share, wide), f32 if d == 0 else bf16) for d in range(levels)]
     if final:
@@ -178,7 +181,7 @@
         shapes,
         ids,
         operands,
-        [pltpu.VMEM((rows, wide), bf16)] * 2,
+        [pltpu.VMEM((rows, wide), bf16)] * 2 + [pltpu.VMEM((rows, wide), f32)],
     )
     return out[:levels], out[levels:]
 
@@ -222,8 +225,9 @@
         for job, (flip, half, groups) in enumerate(jobs):
             mine = [[(refs.pop(0), p.shape[0]) for p in group] for group in groups]
 
-            @pl.when(pl.program_id(0) == job)
+            @pl.when(pl.program_id(0) // 2 == job)
             def _():
+                part = pl.program_id(0) % 2
                 base = ((ids_ref[0] // part_levels) ^ half) * (S // 2)
                 for e, group in enumerate(mine):
                     left = pl.multiple_of(((ids_ref[1] ^ e) % per_node) * width, width)
@@ -232,31 +236,34 @@
                         for row in range(0, height, share):
                             top = pl.multiple_of(((ids_ref[0] ^ d) % part_levels) * share, share)
                             source = pl.multiple_of(base + top, share)
-                            for part in range(2):
-                                piece = ref[row : row + share, part * width : (part + 1) * width]
-                                old = pivot_ref[
-                                    ids_ref[2] ^ flip, part, pl.ds(source, share), pl.ds(left, width)
-                                ]
-                                out_ref[0, part, pl.ds(top, share), pl.ds(left, width)] = (
-                                    old - piece.astype(f32)
-                                )
+                            piece = jnp.where(
+                                part == 0,
+                                ref[row : row + share, :width],
+                                ref[row : row + share, width:],
+                            )
+                            old = pivot_ref[
+                                ids_ref[2] ^ flip, part, pl.ds(source, share), pl.ds(left, width)
+                            ]
+                            out_ref[0, 0, pl.ds(top, share), pl.ds(left, width)] = (
+                                old - piece.astype(f32)
+                            )
                             d += 1
 
     def place(i, ids):
         flip, half = jobs[-1][0], jobs[-1][1]
         for job in range(len(jobs) - 1):
-            flip = jnp.where(i == job, jobs[job][0], flip)
-            half = jnp.where(i == job, jobs[job][1], half)
-        return ids[2] ^ flip, 0, (ids[0] // part_levels) ^ half, 0
-
-    spec = pl.BlockSpec((1, 2, S // 2, S), place)
+            flip = jnp.where(i // 2 == job, jobs[job][0], flip)
+            half = jnp.where(i // 2 == job, jobs[job][1], half)
+        return ids[2] ^ flip, i % 2, (ids[0] // part_levels) ^ half, 0
+
+    spec = pl.BlockSpec((1, 1, S // 2, S), place)
     operands, aliases = [pivot] + stacks, {}
     specs = [pl.BlockSpec(memory_space=pltpu.VMEM)] * len(operands)
     if rest is not None:
         operands, specs = operands + [rest], specs + [pl.BlockSpec(memory_space=pl.ANY)]
         aliases = {len(operands): 0}
     shape = jax.ShapeDtypeStruct(pivot.shape, f32)
-    return call(body, shape, ids, operands, specs, spec, aliases=aliases, steps=len(jobs))
+    return call(body, shape, ids, operands, specs, spec, aliases=aliases, steps=2 * len(jobs))
 
 
 def join(sums):

time: 85.1 us -> 85 us (level)
  no operation moved by 1% of the time
where the time goes in v6:
time: 85 us; the launch traced here: 84.8 us
  waiting for transfers between devices  30.7 us (36%)
  starting transfers between devices  28.5 us (34%)
  Pallas kernels  16.4 us (19%)
  local copies, waits for them, and re-layouts  6.05 us (7%)
  other arithmetic  2.33 us (3%)
    ppermute x28, waiting for transfers between devices, swap(): return lax.ppermute(x, axis, [(i, i ^ distance) for i in range(size)])  30.7 us
    ppermute x28, starting transfers between devices, swap(): return lax.ppermute(x, axis, [(i, i ^ distance) for i in range(size)])  28.5 us
    pallas_call x4, Pallas kernels, call_here(): pl.pallas_call(body, out_shape=out_shape, in_specs=[pl.BlockSpec(memory_s...  10.6 us
    pallas_call x3, Pallas kernels, call(): pl.pallas_call(body, out_shape=out_shape, grid_spec=pltpu.PrefetchScalarG...  5.76 us
    unnamed x9, local copies, waits for them, and re-layouts  3.74 us
  transfers between devices with their start and end apart: 28, of which 13 were waited for; matrix products, arithmetic and copies ran while one was open for 8% of the time, Pallas kernels for 17%

profile of v6, /device:TPU:0, one launch (start us, length us, event | category | flops | bytes accessed | tf_op | source)
XLA Modules:
  0.0 84.8 jit_solution(6808528005322799148)
XLA Ops:
  0.6 0.0 copy-start
  0.6 3.0 %collective-permute-start.5 = (bf16[2,512,512]{2,1,0:T(8,128)(2,1)}, bf16[2,512,512]{2,1,0:T(8,128)(2,1)}, u32[]{:S(2)}, u32[]{:S(2)}) collective-permute-start(bf16[2,512,512]{2,1,0:T(8,128)(2,1)} %refs_0_.1), channel_id=1, source_target_pairs={{0,2},{1,3},{2,0},{3,1},{4,6},{5,7},{6,4},{7,5},{8,10},{9,11},{10,... | collective-permute-start | bytes 3145736 | tf_op jit(solution)/shard_map/ppermute | solution.py:21
  3.6 0.7 fusion
  4.3 0.4 constant_dynamic-slice_fusion.2
  4.7 0.4 fusion.1
  5.1 0.1 copy_bitcast_fusion
  5.2 0.1 broadcast_bitcast_fusion
  5.2 0.8 broadcast_multiply_fusion
  6.1 2.6 %collective-permute-start.2 = (bf16[512,256]{1,0:T(8,128)(2,1)}, bf16[512,256]{1,0:T(8,128)(2,1)}, u32[]{:S(2)}, u32[]{:S(2)}) collective-permute-start(bf16[512,256]{1,0:T(8,128)(2,1)} %get-tuple-element.59.refs_4_), channel_id=1, source_target_pairs={{0,8},{4,12},{8,0},{12,4},{1,9},{5,13},{9,1},{13,5},{2,10},{6,14},... | collective-permute-start | bytes 786440 | tf_op jit(solution)/shard_map/ppermute | solution.py:21
  8.7 1.6 %collective-permute-start.1 = (bf16[512,256]{1,0:T(8,128)(2,1)}, bf16[512,256]{1,0:T(8,128)(2,1)}, u32[]{:S(2)}, u32[]{:S(2)}) collective-permute-start(bf16[512,256]{1,0:T(8,128)(2,1)} %get-tuple-element.59.refs_4_), channel_id=1, source_target_pairs={{0,4},{4,0},{8,12},{12,8},{1,5},{5,1},{9,13},{13,9},{2,6},{6,2},{1... | collective-permute-start | bytes 786440 | tf_op jit(solution)/shard_map/ppermute | solution.py:21
  10.2 0.4 collective-permute-start.3
  10.7 0.3 collective-permute-start.4
  11.0 0.7 constant_dynamic-slice_fusion
  11.8 2.5 %copy.9 = bf16[512,2,512]{0,2,1:T(8,128)(2,1)} copy(bf16[512,2,512]{2,1,0:T(2,128)(2,1)S(1)} %constant_dynamic-slice_fusion) | data formatting | bytes 2097152
  14.2 1.3 %multiply_bitcast_fusion.side_ref = bf16[2,512,512]{2,1,0:T(8,128)(2,1)S(1)} fusion(bf16[512,2,512]{0,2,1:T(8,128)(2,1)} %copy.9, bf16[512]{0:T(512)(128)(2,1)S(1)} %broadcast_bitcast_fusion), kind=kLoop, calls=%fused_computation | loop fusion | flops 524288 | bytes 2098176 | tf_op jit(solution)/shard_map/transpose | solution.py:297
  15.5 6.4 %collective-permute-done.2.refs_6_ = bf16[512,256]{1,0:T(8,128)(2,1)} collective-permute-done((bf16[512,256]{1,0:T(8,128)(2,1)}, bf16[512,256]{1,0:T(8,128)(2,1)}, u32[]{:S(2)}, u32[]{:S(2)}) %collective-permute-start.2) | collective-permute-done | bytes 262176 | tf_op jit(solution)/shard_map/ppermute | solution.py:21
  21.9 0.0 collective-permute-start
  21.9 6.4 %collective-permute-done.1.refs_5_ = bf16[512,256]{1,0:T(8,128)(2,1)} collective-permute-done((bf16[512,256]{1,0:T(8,128)(2,1)}, bf16[512,256]{1,0:T(8,128)(2,1)}, u32[]{:S(2)}, u32[]{:S(2)}) %collective-permute-start.1) | collective-permute-done | bytes 262176 | tf_op jit(solution)/shard_map/ppermute | solution.py:21
  28.4 3.9 %collective-permute-done.3.refs_8_ = bf16[512,256]{1,0:T(8,128)(2,1)} collective-permute-done((bf16[512,256]{1,0:T(8,128)(2,1)S(1)}, bf16[512,256]{1,0:T(8,128)(2,1)}, u32[]{:S(2)}, u32[]{:S(2)}) %collective-permute-start.3) | collective-permute-done | bytes 262176 | tf_op jit(solution)/shard_map/ppermute | solution.py:21
  32.2 0.0 collective-permute-done.4.refs_9_
  32.2 0.0 collective-permute-done.5.refs_2_
  32.2 0.0 collective-permute-start.6
  32.2 1.3 %collective-permute-start.7 = (bf16[512,256]{1,0:T(8,128)(2,1)}, bf16[512,256]{1,0:T(8,128)(2,1)}, u32[]{:S(2)}, u32[]{:S(2)}) collective-permute-start(bf16[512,256]{1,0:T(8,128)(2,1)} %collective-permute-done.2.refs_6_), channel_id=1, source_target_pairs={{0,4},{4,0},{8,12},{12,8},{1,5},{5,1},{9,13},{13,9},{2,6},{6,2},{1... | collective-permute-start | bytes 786440 | tf_op jit(solution)/shard_map/ppermute | solution.py:21
  33.5 0.8 collective-permute-start.11
  34.3 0.1 pad_add_fusion.ids_ref
  34.4 0.0 collective-permute-done.refs_1_
  34.4 0.8 collective-permute-done.6.refs_3_
  35.2 1.2 %copy-done.2 = bf16[2,512,512]{2,1,0:T(8,128)(2,1)S(1)} copy-done((bf16[2,512,512]{2,1,0:T(8,128)(2,1)S(1)}, bf16[2,512,512]{2,1,0:T(8,128)(2,1)}, u32[]{:S(2)}) %copy-start.2) | copy-done | bytes 1048600
  36.4 4.6 %shard_map.59 = (f32[512,256]{1,0:T(8,128)S(1)}, f32[512,256]{1,0:T(8,128)S(1)}, bf16[2,512,512]{2,1,0:T(8,128)(2,1)S(1)}) custom-call(s32[3]{0:T(128)S(1)} %pad_add_fusion.ids_ref, bf16[2,512,512]{2,1,0:T(8,128)(2,1)S(1)} %copy-done.2, bf16[2,512,512]{2,1,0:T(8,128)(2,1)} %collective-permute-done.refs_1_, ...), custom_call_target="tpu_custom_call" | custom-call | bytes 65536 | tf_op jit(solution)/shard_map/pallas_call | solution.py:82
  41.1 0.6 collective-permute-done.7.m_ref
  41.7 2.0 %shard_map.60 = (f32[128,256]{1,0:T(8,128)S(1)}, bf16[128,256]{1,0:T(8,128)(2,1)S(1)}, bf16[128,256]{1,0:T(8,128)(2,1)S(1)}, bf16[128,256]{1,0:T(8,128)(2,1)S(1)}, f32[512,256]{1,0:T(8,128)S(1)}) custom-call(s32[3]{0:T(128)S(1)} %pad_add_fusion.ids_ref, bf16[2,512,512]{2,1,0:T(8,128)(2,1)S(1)} %get-tuple-element.65.left_ref, ...), custom_call_target="tpu_custom_call" | custom-call | bytes 65536 | tf_op jit(solution)/shard_map/pallas_call | solution.py:82
  43.7 2.5 %collective-permute-start.10 = (bf16[128,256]{1,0:T(8,128)(2,1)S(1)}, bf16[128,256]{1,0:T(8,128)(2,1)S(1)}, u32[]{:S(2)}, u32[]{:S(2)}) collective-permute-start(bf16[128,256]{1,0:T(8,128)(2,1)S(1)} %get-tuple-element.71), channel_id=1, source_target_pairs={{0,12},{4,8},{8,4},{12,0},{1,13},{5,9},{9,5},{13,1},{2,14},{6,10},... | collective-permute-start | bytes 196616 | tf_op jit(solution)/shard_map/ppermute | solution.py:21
  46.2 0.4 collective-permute-start.8
  46.6 1.6 %collective-permute-start.9 = (bf16[128,256]{1,0:T(8,128)(2,1)S(1)}, bf16[128,256]{1,0:T(8,128)(2,1)S(1)}, u32[]{:S(2)}, u32[]{:S(2)}) collective-permute-start(bf16[128,256]{1,0:T(8,128)(2,1)S(1)} %get-tuple-element.70), channel_id=1, source_target_pairs={{0,8},{4,12},{8,0},{12,4},{1,9},{5,13},{9,1},{13,5},{2,10},{6,14},... | collective-permute-start | bytes 196616 | tf_op jit(solution)/shard_map/ppermute | solution.py:21
  48.1 0.0 collective-permute-done.11.m_ref
  48.1 1.8 %shard_map.61 = (f32[128,256]{1,0:T(8,128)S(1)}, bf16[128,256]{1,0:T(8,128)(2,1)S(1)}, bf16[128,256]{1,0:T(8,128)(2,1)S(1)}, bf16[128,256]{1,0:T(8,128)(2,1)S(1)...) custom-call(s32[3]{0:T(128)S(1)} %pad_add_fusion.ids_ref, bf16[2,512,512]{2,1,0:T(8,128)(2,1)S(1)} %get-tuple-element.65.left_ref, ...), custom_call_target="tpu_custom_call" | custom-call | bytes 65536 | tf_op jit(solution)/shard_map/pallas_call | solution.py:82
  50.0 1.2 %collective-permute-start.15 = (bf16[256,512]{1,0:T(8,128)(2,1)S(1)}, bf16[256,512]{1,0:T(8,128)(2,1)S(1)}, u32[]{:S(2)}, u32[]{:S(2)}) collective-permute-start(bf16[256,512]{1,0:T(8,128)(2,1)S(1)} %get-tuple-element.83), channel_id=1, source_target_pairs={{0,2},{1,3},{2,0},{3,1},{4,6},{5,7},{6,4},{7,5},{8,10},{9,11},{10,... | collective-permute-start | bytes 786440 | tf_op jit(solution)/shard_map/ppermute | solution.py:21
  51.2 0.3 collective-permute-start.12
  51.5 2.7 %collective-permute-start.13 = (bf16[128,256]{1,0:T(8,128)(2,1)S(1)}, bf16[128,256]{1,0:T(8,128)(2,1)S(1)}, u32[]{:S(2)}, u32[]{:S(2)}) collective-permute-start(bf16[128,256]{1,0:T(8,128)(2,1)S(1)} %get-tuple-element.80), channel_id=1, source_target_pairs={{0,8},{4,12},{8,0},{12,4},{1,9},{5,13},{9,1},{13,5},{2,10},{6,14},... | collective-permute-start | bytes 196616 | tf_op jit(solution)/shard_map/ppermute | solution.py:21
  54.2 0.0 collective-permute-done.8
  54.2 1.4 %collective-permute-start.14 = (bf16[128,256]{1,0:T(8,128)(2,1)S(1)}, bf16[128,256]{1,0:T(8,128)(2,1)S(1)}, u32[]{:S(2)}, u32[]{:S(2)}) collective-permute-start(bf16[128,256]{1,0:T(8,128)(2,1)S(1)} %get-tuple-element.81), channel_id=1, source_target_pairs={{0,12},{4,8},{8,4},{12,0},{1,13},{5,9},{9,5},{13,1},{2,14},{6,10},... | collective-permute-start | bytes 196616 | tf_op jit(solution)/shard_map/ppermute | solution.py:21
  55.6 2.5 %collective-permute-done.13 = bf16[128,256]{1,0:T(8,128)(2,1)S(1)} collective-permute-done((bf16[128,256]{1,0:T(8,128)(2,1)S(1)}, bf16[128,256]{1,0:T(8,128)(2,1)S(1)}, u32[]{:S(2)}, u32[]{:S(2)}) %collective-permute-start.13) | collective-permute-done | bytes 65568 | tf_op jit(solution)/shard_map/ppermute | solution.py:21
  58.1 2.2 %collective-permute-done.14 = bf16[128,256]{1,0:T(8,128)(2,1)S(1)} collective-permute-done((bf16[128,256]{1,0:T(8,128)(2,1)S(1)}, bf16[128,256]{1,0:T(8,128)(2,1)S(1)}, u32[]{:S(2)}, u32[]{:S(2)}) %collective-permute-start.14) | collective-permute-done | bytes 65568 | tf_op jit(solution)/shard_map/ppermute | solution.py:21
  60.4 0.1 collective-permute-start.19
  60.5 2.0 %collective-permute-start.16 = (bf16[128,512]{1,0:T(8,128)(2,1)S(1)}, bf16[128,512]{1,0:T(8,128)(2,1)S(1)}, u32[]{:S(2)}, u32[]{:S(2)}) collective-permute-start(bf16[128,512]{1,0:T(8,128)(2,1)S(1)} %pad_maximum_fusion.1), channel_id=1, source_target_pairs={{0,8},{4,12},{8,0},{12,4},{1,9},{5,13},{9,1},{13,5},{2,10},{6,14},... | collective-permute-start | bytes 393224 | tf_op jit(solution)/shard_map/ppermute | solution.py:21
  62.5 2.4 %collective-permute-start.17 = (bf16[128,512]{1,0:T(8,128)(2,1)S(1)}, bf16[128,512]{1,0:T(8,128)(2,1)S(1)}, u32[]{:S(2)}, u32[]{:S(2)}) collective-permute-start(bf16[128,512]{1,0:T(8,128)(2,1)S(1)} %pad_maximum_fusion.1), channel_id=1, source_target_pairs={{0,12},{4,8},{8,4},{12,0},{1,13},{5,9},{9,5},{13,1},{2,14},{6,10},... | collective-permute-start | bytes 393224 | tf_op jit(solution)/shard_map/ppermute | solution.py:21
  64.9 0.9 %collective-permute-start.18 = (bf16[128,512]{1,0:T(8,128)(2,1)S(1)}, bf16[128,512]{1,0:T(8,128)(2,1)S(1)}, u32[]{:S(2)}, u32[]{:S(2)}) collective-permute-start(bf16[128,512]{1,0:T(8,128)(2,1)S(1)} %pad_maximum_fusion.1), channel_id=1, source_target_pairs={{0,2},{1,3},{2,0},{3,1},{4,6},{5,7},{6,4},{7,5},{8,10},{9,11},{10,... | collective-permute-start | bytes 393224 | tf_op jit(solution)/shard_map/ppermute | solution.py:21
  65.8 1.4 %collective-permute-done.19 = bf16[128,512]{1,0:T(8,128)(2,1)S(1)} collective-permute-done((bf16[128,512]{1,0:T(8,128)(2,1)S(1)}, bf16[128,512]{1,0:T(8,128)(2,1)S(1)}, u32[]{:S(2)}, u32[]{:S(2)}) %collective-permute-start.19) | collective-permute-done | bytes 131104 | tf_op jit(solution)/shard_map/ppermute | solution.py:21
  67.1 0.9 %collective-permute-start.20 = (bf16[128,512]{1,0:T(8,128)(2,1)S(1)}, bf16[128,512]{1,0:T(8,128)(2,1)S(1)}, u32[]{:S(2)}, u32[]{:S(2)}) collective-permute-start(bf16[128,512]{1,0:T(8,128)(2,1)S(1)} %collective-permute-done.19), channel_id=1, source_target_pairs={{0,2},{1,3},{2,0},{3,1},{4,6},{5,7},{6,4},{7,5},{8,10},{9,11},{10,... | collective-permute-start | bytes 393224 | tf_op jit(solution)/shard_map/ppermute | solution.py:21
  68.1 0.1 collective-permute-start.23
  68.2 2.6 %collective-permute-done.16 = bf16[128,512]{1,0:T(8,128)(2,1)S(1)} collective-permute-done((bf16[128,512]{1,0:T(8,128)(2,1)S(1)}, bf16[128,512]{1,0:T(8,128)(2,1)S(1)}, u32[]{:S(2)}, u32[]{:S(2)}) %collective-permute-start.16) | collective-permute-done | bytes 131104 | tf_op jit(solution)/shard_map/ppermute | solution.py:21
  70.8 0.0 collective-permute-done.18
  70.8 1.3 %collective-permute-done.20 = bf16[128,512]{1,0:T(8,128)(2,1)S(1)} collective-permute-done((bf16[128,512]{1,0:T(8,128)(2,1)S(1)}, bf16[128,512]{1,0:T(8,128)(2,1)S(1)}, u32[]{:S(2)}, u32[]{:S(2)}) %collective-permute-start.20) | collective-permute-done | bytes 131104 | tf_op jit(solution)/shard_map/ppermute | solution.py:21
  72.1 0.6 collective-permute-start.24
  72.7 0.1 collective-permute-start.22
  72.8 0.5 collective-permute-start.26
  73.3 0.9 %collective-permute-start.21 = (bf16[256,512]{1,0:T(8,128)(2,1)S(1)}, bf16[256,512]{1,0:T(8,128)(2,1)S(1)}, u32[]{:S(2)}, u32[]{:S(2)}) collective-permute-start(bf16[256,512]{1,0:T(8,128)(2,1)S(1)} %constant_dynamic-update-slice_fusion.refs_0_), channel_id=1, source_target_pairs={{0,2},{1,3},{2,0},{3,1},{4,6},{5,7},{6,4},{7,5},{8,10},{9,11},{10,... | collective-permute-start | bytes 786440 | tf_op jit(solution)/shard_map/ppermute | solution.py:21
  74.2 0.1 collective-permute-done.24.refs_3_
  74.4 2.5 %shard_map.62.refs_2_ = f32[2,2,512,512]{3,2,1,0:T(8,128)} custom-call(s32[3]{0:T(128)S(1)} %pad_add_fusion.ids_ref, f32[2,2,512,512]{3,2,1,0:T(8,128)S(1)} %copy-done.1, bf16[256,512]{1,0:T(8,128)(2,1)S(1)} %pad_maximum_fusion.refs_0_, bf16[256,512]{1,0:T(8,128)(2,1)S(1)} %collective-permute-done.23.refs_1_, ...), custom_call_target="tpu_custom_call" | custom-call | bytes 65536 | tf_op jit(solution)/shard_map/pallas_call | solution.py:65
  76.9 1.6 %shard_map.63.refs_2_ = f32[2,2,512,512]{3,2,1,0:T(8,128)} custom-call(s32[3]{0:T(128)S(1)} %pad_add_fusion.ids_ref, f32[2,2,512,512]{3,2,1,0:T(8,128)S(1)} %copy-done.1, bf16[256,512]{1,0:T(8,128)(2,1)S(1)} %constant_dynamic-update-slice_fusion.refs_0_, bf16[256,512]{1,0:T(8,128)(2,1)S(1)} %collective-permute-done.22.refs_1_, ...), custom_call_target="tpu_custom_call", output_to_operand_aliasing={{}: (4, {})} | custom-call | bytes 65536 | tf_op jit(solution)/shard_map/pallas_call | solution.py:65
  78.5 2.2 %shard_map.64 = f32[128,2,1024]{2,1,0:T(2,128)} custom-call(s32[3]{0:T(128)S(1)} %pad_add_fusion.ids_ref, f32[256,512]{1,0:T(8,128)S(1)} %get-tuple-element.99.refs_0_, bf16[256,512]{1,0:T(8,128)(2,1)S(1)} %collective-permute-done.15.refs_1_, f32[256,512]{1,0:T(8,128)S(1)} %collective-permute-done.25.refs_2_, ...), custom_call_target="tpu_custom_call" | custom-call | bytes 65536 | tf_op jit(solution)/shard_map/pallas_call | solution.py:82
  80.7 0.9 %collective-permute-done.21.refs_0_ = bf16[256,512]{1,0:T(8,128)(2,1)S(1)} collective-permute-done((bf16[256,512]{1,0:T(8,128)(2,1)S(1)}, bf16[256,512]{1,0:T(8,128)(2,1)S(1)}, u32[]{:S(2)}, u32[]{:S(2)}) %collective-permute-start.21) | collective-permute-done | bytes 262176 | tf_op jit(solution)/shard_map/ppermute | solution.py:21
  81.6 1.5 %collective-permute-done.27.refs_1_ = bf16[256,512]{1,0:T(8,128)(2,1)S(1)} collective-permute-done((bf16[256,512]{1,0:T(8,128)(2,1)S(1)}, bf16[256,512]{1,0:T(8,128)(2,1)S(1)}, u32[]{:S(2)}, u32[]{:S(2)}) %collective-permute-start.27) | collective-permute-done | bytes 262176 | tf_op jit(solution)/shard_map/ppermute | solution.py:21
  83.1 1.6 %shard_map.65 = f32[2,2,512,512]{3,2,1,0:T(8,128)} custom-call(s32[3]{0:T(128)S(1)} %pad_add_fusion.ids_ref, f32[2,2,512,512]{3,2,1,0:T(8,128)S(1)} %copy-done.1, bf16[256,512]{1,0:T(8,128)(2,1)S(1)} %collective-permute-done.21.refs_0_, bf16[256,512]{1,0:T(8,128)(2,1)S(1)} %collective-permute-done.27.refs_1_, ...), custom_call_target="tpu_custom_call", output_to_operand_aliasing={{}: (4, {})} | custom-call | bytes 65536 | tf_op jit(solution)/shard_map/pallas_call | solution.py:65
  (26 shorter events, 0.2 us)
Async XLA Ops:
  0.6 3.7 %copy-start = (bf16[512,2,1024]{2,1,0:T(2,128)(2,1)S(1)}, bf16[512,2,1024]{2,1,0:T(2,128)(2,1)}, u32[]{:S(2)}) copy-start(bf16[512,2,1024]{2,1,0:T(2,128)(2,1)} %param.5) | copy-start | bytes 6291460
  0.6 31.6 %collective-permute-start.5 = (bf16[2,512,512]{2,1,0:T(8,128)(2,1)}, bf16[2,512,512]{2,1,0:T(8,128)(2,1)}, u32[]{:S(2)}, u32[]{:S(2)}) collective-permute-start(bf16[2,512,512]{2,1,0:T(8,128)(2,1)} %refs_0_.1), channel_id=1, source_target_pairs={{0,2},{1,3},{2,0},{3,1},{4,6},{5,7},{6,4},{7,5},{8,10},{9,11},{10,... | collective-permute-start | bytes 3145736 | tf_op jit(solution)/shard_map/ppermute | solution.py:21
  6.1 15.9 %collective-permute-start.2 = (bf16[512,256]{1,0:T(8,128)(2,1)}, bf16[512,256]{1,0:T(8,128)(2,1)}, u32[]{:S(2)}, u32[]{:S(2)}) collective-permute-start(bf16[512,256]{1,0:T(8,128)(2,1)} %get-tuple-element.59.refs_4_), channel_id=1, source_target_pairs={{0,8},{4,12},{8,0},{12,4},{1,9},{5,13},{9,1},{13,5},{2,10},{6,14},... | collective-permute-start | bytes 786440 | tf_op jit(solution)/shard_map/ppermute | solution.py:21
  8.7 19.7 %collective-permute-start.1 = (bf16[512,256]{1,0:T(8,128)(2,1)}, bf16[512,256]{1,0:T(8,128)(2,1)}, u32[]{:S(2)}, u32[]{:S(2)}) collective-permute-start(bf16[512,256]{1,0:T(8,128)(2,1)} %get-tuple-element.59.refs_4_), channel_id=1, source_target_pairs={{0,4},{4,0},{8,12},{12,8},{1,5},{5,1},{9,13},{13,9},{2,6},{6,2},{1... | collective-permute-start | bytes 786440 | tf_op jit(solution)/shard_map/ppermute | solution.py:21
  10.2 22.0 %collective-permute-start.3 = (bf16[512,256]{1,0:T(8,128)(2,1)S(1)}, bf16[512,256]{1,0:T(8,128)(2,1)}, u32[]{:S(2)}, u32[]{:S(2)}) collective-permute-start(bf16[512,256]{1,0:T(8,128)(2,1)S(1)} %get-tuple-element.62.refs_7_), channel_id=1, source_target_pairs={{0,4},{4,0},{8,12},{12,8},{1,5},{5,1},{9,13},{13,9},{2,6},{6,2},{1... | collective-permute-start | bytes 786440 | tf_op jit(solution)/shard_map/ppermute | solution.py:21
  10.7 21.5 %collective-permute-start.4 = (bf16[512,256]{1,0:T(8,128)(2,1)S(1)}, bf16[512,256]{1,0:T(8,128)(2,1)}, u32[]{:S(2)}, u32[]{:S(2)}) collective-permute-start(bf16[512,256]{1,0:T(8,128)(2,1)S(1)} %get-tuple-element.62.refs_7_), channel_id=1, source_target_pairs={{0,8},{4,12},{8,0},{12,4},{1,9},{5,13},{9,1},{13,5},{2,10},{6,14},... | collective-permute-start | bytes 786440 | tf_op jit(solution)/shard_map/ppermute | solution.py:21
  21.9 12.5 %collective-permute-start = (bf16[2,512,512]{2,1,0:T(8,128)(2,1)}, bf16[2,512,512]{2,1,0:T(8,128)(2,1)}, u32[]{:S(2)}, u32[]{:S(2)}) collective-permute-start(bf16[2,512,512]{2,1,0:T(8,128)(2,1)} %refs_0_.1), channel_id=1, source_target_pairs={{0,1},{1,0},{2,3},{3,2},{4,5},{5,4},{6,7},{7,6},{8,9},{9,8},{10,11... | collective-permute-start | bytes 3145736 | tf_op jit(solution)/shard_map/ppermute | solution.py:21
  32.2 3.0 %collective-permute-start.6 = (bf16[2,512,512]{2,1,0:T(8,128)(2,1)}, bf16[2,512,512]{2,1,0:T(8,128)(2,1)}, u32[]{:S(2)}, u32[]{:S(2)}) collective-permute-start(bf16[2,512,512]{2,1,0:T(8,128)(2,1)} %collective-permute-done.5.refs_2_), channel_id=1, source_target_pairs={{0,1},{1,0},{2,3},{3,2},{4,5},{5,4},{6,7},{7,6},{8,9},{9,8},{10,11... | collective-permute-start | bytes 3145736 | tf_op jit(solution)/shard_map/ppermute | solution.py:21
  32.2 9.5 %collective-permute-start.7 = (bf16[512,256]{1,0:T(8,128)(2,1)}, bf16[512,256]{1,0:T(8,128)(2,1)}, u32[]{:S(2)}, u32[]{:S(2)}) collective-permute-start(bf16[512,256]{1,0:T(8,128)(2,1)} %collective-permute-done.2.refs_6_), channel_id=1, source_target_pairs={{0,4},{4,0},{8,12},{12,8},{1,5},{5,1},{9,13},{13,9},{2,6},{6,2},{1... | collective-permute-start | bytes 786440 | tf_op jit(solution)/shard_map/ppermute | solution.py:21
  33.5 14.6 %collective-permute-start.11 = (bf16[512,256]{1,0:T(8,128)(2,1)}, bf16[512,256]{1,0:T(8,128)(2,1)}, u32[]{:S(2)}, u32[]{:S(2)}) collective-permute-start(bf16[512,256]{1,0:T(8,128)(2,1)} %collective-permute-done.4.refs_9_), channel_id=1, source_target_pairs={{0,4},{4,0},{8,12},{12,8},{1,5},{5,1},{9,13},{13,9},{2,6},{6,2},{1... | collective-permute-start | bytes 786440 | tf_op jit(solution)/shard_map/ppermute | solution.py:21
  35.2 1.2 %copy-start.2 = (bf16[2,512,512]{2,1,0:T(8,128)(2,1)S(1)}, bf16[2,512,512]{2,1,0:T(8,128)(2,1)}, u32[]{:S(2)}) copy-start(bf16[2,512,512]{2,1,0:T(8,128)(2,1)} %refs_0_.1) | copy-start | bytes 3145732
  41.7 32.6 %copy-start.1 = (f32[2,2,512,512]{3,2,1,0:T(8,128)S(1)}, f32[2,2,512,512]{3,2,1,0:T(8,128)}, u32[]{:S(2)}) copy-start(f32[2,2,512,512]{3,2,1,0:T(8,128)} %pivot_ref.5) | copy-start | bytes 12582916
  43.7 7.8 %collective-permute-start.10 = (bf16[128,256]{1,0:T(8,128)(2,1)S(1)}, bf16[128,256]{1,0:T(8,128)(2,1)S(1)}, u32[]{:S(2)}, u32[]{:S(2)}) collective-permute-start(bf16[128,256]{1,0:T(8,128)(2,1)S(1)} %get-tuple-element.71), channel_id=1, source_target_pairs={{0,12},{4,8},{8,4},{12,0},{1,13},{5,9},{9,5},{13,1},{2,14},{6,10},... | collective-permute-start | bytes 196616 | tf_op jit(solution)/shard_map/ppermute | solution.py:21
  46.2 8.0 %collective-permute-start.8 = (bf16[128,256]{1,0:T(8,128)(2,1)S(1)}, bf16[128,256]{1,0:T(8,128)(2,1)S(1)}, u32[]{:S(2)}, u32[]{:S(2)}) collective-permute-start(bf16[128,256]{1,0:T(8,128)(2,1)S(1)} %get-tuple-element.69), channel_id=1, source_target_pairs={{0,4},{4,0},{8,12},{12,8},{1,5},{5,1},{9,13},{13,9},{2,6},{6,2},{1... | collective-permute-start | bytes 196616 | tf_op jit(solution)/shard_map/ppermute | solution.py:21
  46.6 9.0 %collective-permute-start.9 = (bf16[128,256]{1,0:T(8,128)(2,1)S(1)}, bf16[128,256]{1,0:T(8,128)(2,1)S(1)}, u32[]{:S(2)}, u32[]{:S(2)}) collective-permute-start(bf16[128,256]{1,0:T(8,128)(2,1)S(1)} %get-tuple-element.70), channel_id=1, source_target_pairs={{0,8},{4,12},{8,0},{12,4},{1,9},{5,13},{9,1},{13,5},{2,10},{6,14},... | collective-permute-start | bytes 196616 | tf_op jit(solution)/shard_map/ppermute | solution.py:21
  50.0 10.3 %collective-permute-start.15 = (bf16[256,512]{1,0:T(8,128)(2,1)S(1)}, bf16[256,512]{1,0:T(8,128)(2,1)S(1)}, u32[]{:S(2)}, u32[]{:S(2)}) collective-permute-start(bf16[256,512]{1,0:T(8,128)(2,1)S(1)} %get-tuple-element.83), channel_id=1, source_target_pairs={{0,2},{1,3},{2,0},{3,1},{4,6},{5,7},{6,4},{7,5},{8,10},{9,11},{10,... | collective-permute-start | bytes 786440 | tf_op jit(solution)/shard_map/ppermute | solution.py:21
  51.2 4.4 %collective-permute-start.12 = (bf16[128,256]{1,0:T(8,128)(2,1)S(1)}, bf16[128,256]{1,0:T(8,128)(2,1)S(1)}, u32[]{:S(2)}, u32[]{:S(2)}) collective-permute-start(bf16[128,256]{1,0:T(8,128)(2,1)S(1)} %get-tuple-element.79), channel_id=1, source_target_pairs={{0,4},{4,0},{8,12},{12,8},{1,5},{5,1},{9,13},{13,9},{2,6},{6,2},{1... | collective-permute-start | bytes 196616 | tf_op jit(solution)/shard_map/ppermute | solution.py:21
  51.5 6.6 %collective-permute-start.13 = (bf16[128,256]{1,0:T(8,128)(2,1)S(1)}, bf16[128,256]{1,0:T(8,128)(2,1)S(1)}, u32[]{:S(2)}, u32[]{:S(2)}) collective-permute-start(bf16[128,256]{1,0:T(8,128)(2,1)S(1)} %get-tuple-element.80), channel_id=1, source_target_pairs={{0,8},{4,12},{8,0},{12,4},{1,9},{5,13},{9,1},{13,5},{2,10},{6,14},... | collective-permute-start | bytes 196616 | tf_op jit(solution)/shard_map/ppermute | solution.py:21
  54.2 6.1 %collective-permute-start.14 = (bf16[128,256]{1,0:T(8,128)(2,1)S(1)}, bf16[128,256]{1,0:T(8,128)(2,1)S(1)}, u32[]{:S(2)}, u32[]{:S(2)}) collective-permute-start(bf16[128,256]{1,0:T(8,128)(2,1)S(1)} %get-tuple-element.81), channel_id=1, source_target_pairs={{0,12},{4,8},{8,4},{12,0},{1,13},{5,9},{9,5},{13,1},{2,14},{6,10},... | collective-permute-start | bytes 196616 | tf_op jit(solution)/shard_map/ppermute | solution.py:21
  60.4 6.7 %collective-permute-start.19 = (bf16[128,512]{1,0:T(8,128)(2,1)S(1)}, bf16[128,512]{1,0:T(8,128)(2,1)S(1)}, u32[]{:S(2)}, u32[]{:S(2)}) collective-permute-start(bf16[128,512]{1,0:T(8,128)(2,1)S(1)} %pad_maximum_fusion.1), channel_id=1, source_target_pairs={{0,4},{4,0},{8,12},{12,8},{1,5},{5,1},{9,13},{13,9},{2,6},{6,2},{1... | collective-permute-start | bytes 393224 | tf_op jit(solution)/shard_map/ppermute | solution.py:21
  60.5 10.3 %collective-permute-start.16 = (bf16[128,512]{1,0:T(8,128)(2,1)S(1)}, bf16[128,512]{1,0:T(8,128)(2,1)S(1)}, u32[]{:S(2)}, u32[]{:S(2)}) collective-permute-start(bf16[128,512]{1,0:T(8,128)(2,1)S(1)} %pad_maximum_fusion.1), channel_id=1, source_target_pairs={{0,8},{4,12},{8,0},{12,4},{1,9},{5,13},{9,1},{13,5},{2,10},{6,14},... | collective-permute-start | bytes 393224 | tf_op jit(solution)/shard_map/ppermute | solution.py:21
  62.5 8.3 %collective-permute-start.17 = (bf16[128,512]{1,0:T(8,128)(2,1)S(1)}, bf16[128,512]{1,0:T(8,128)(2,1)S(1)}, u32[]{:S(2)}, u32[]{:S(2)}) collective-permute-start(bf16[128,512]{1,0:T(8,128)(2,1)S(1)} %pad_maximum_fusion.1), channel_id=1, source_target_pairs={{0,12},{4,8},{8,4},{12,0},{1,13},{5,9},{9,5},{13,1},{2,14},{6,10},... | collective-permute-start | bytes 393224 | tf_op jit(solution)/shard_map/ppermute | solution.py:21
  64.9 5.9 %collective-permute-start.18 = (bf16[128,512]{1,0:T(8,128)(2,1)S(1)}, bf16[128,512]{1,0:T(8,128)(2,1)S(1)}, u32[]{:S(2)}, u32[]{:S(2)}) collective-permute-start(bf16[128,512]{1,0:T(8,128)(2,1)S(1)} %pad_maximum_fusion.1), channel_id=1, source_target_pairs={{0,2},{1,3},{2,0},{3,1},{4,6},{5,7},{6,4},{7,5},{8,10},{9,11},{10,... | collective-permute-start | bytes 393224 | tf_op jit(solution)/shard_map/ppermute | solution.py:21
  67.1 5.0 %collective-permute-start.20 = (bf16[128,512]{1,0:T(8,128)(2,1)S(1)}, bf16[128,512]{1,0:T(8,128)(2,1)S(1)}, u32[]{:S(2)}, u32[]{:S(2)}) collective-permute-start(bf16[128,512]{1,0:T(8,128)(2,1)S(1)} %collective-permute-done.19), channel_id=1, source_target_pairs={{0,2},{1,3},{2,0},{3,1},{4,6},{5,7},{6,4},{7,5},{8,10},{9,11},{10,... | collective-permute-start | bytes 393224 | tf_op jit(solution)/shard_map/ppermute | solution.py:21
  68.1 5.2 %collective-permute-start.23 = (bf16[256,512]{1,0:T(8,128)(2,1)S(1)}, bf16[256,512]{1,0:T(8,128)(2,1)S(1)}, u32[]{:S(2)}, u32[]{:S(2)}) collective-permute-start(bf16[256,512]{1,0:T(8,128)(2,1)S(1)} %pad_maximum_fusion.refs_0_), channel_id=1, source_target_pairs={{0,1},{1,0},{2,3},{3,2},{4,5},{5,4},{6,7},{7,6},{8,9},{9,8},{10,11... | collective-permute-start | bytes 786440 | tf_op jit(solution)/shard_map/ppermute | solution.py:21
  72.1 6.4 %collective-permute-start.25 = (f32[256,512]{1,0:T(8,128)S(1)}, f32[256,512]{1,0:T(8,128)S(1)}, u32[]{:S(2)}, u32[]{:S(2)}) collective-permute-start(f32[256,512]{1,0:T(8,128)S(1)} %get-tuple-element.99.refs_0_), channel_id=1, source_target_pairs={{0,1},{1,0},{2,3},{3,2},{4,5},{5,4},{6,7},{7,6},{8,9},{9,8},{10,11... | collective-permute-start | bytes 1572872 | tf_op jit(solution)/shard_map/ppermute | solution.py:21
  72.1 2.2 %collective-permute-start.24 = (bf16[256,512]{1,0:T(8,128)(2,1)S(1)}, bf16[256,512]{1,0:T(8,128)(2,1)S(1)}, u32[]{:S(2)}, u32[]{:S(2)}) collective-permute-start(bf16[256,512]{1,0:T(8,128)(2,1)S(1)} %constant_dynamic-update-slice_fusion.2.refs_2_), channel_id=1, source_target_pairs={{0,1},{1,0},{2,3},{3,2},{4,5},{5,4},{6,7},{7,6},{8,9},{9,8},{10,11... | collective-permute-start | bytes 786440 | tf_op jit(solution)/shard_map/ppermute | solution.py:21
  72.7 4.2 %collective-permute-start.22 = (bf16[256,512]{1,0:T(8,128)(2,1)S(1)}, bf16[256,512]{1,0:T(8,128)(2,1)S(1)}, u32[]{:S(2)}, u32[]{:S(2)}) collective-permute-start(bf16[256,512]{1,0:T(8,128)(2,1)S(1)} %constant_dynamic-update-slice_fusion.refs_0_), channel_id=1, source_target_pairs={{0,1},{1,0},{2,3},{3,2},{4,5},{5,4},{6,7},{7,6},{8,9},{9,8},{10,11... | collective-permute-start | bytes 786440 | tf_op jit(solution)/shard_map/ppermute | solution.py:21
  72.8 5.7 %collective-permute-start.26 = (bf16[256,512]{1,0:T(8,128)(2,1)S(1)}, bf16[256,512]{1,0:T(8,128)(2,1)S(1)}, u32[]{:S(2)}, u32[]{:S(2)}) collective-permute-start(bf16[256,512]{1,0:T(8,128)(2,1)S(1)} %collective-permute-done.15.refs_1_), channel_id=1, source_target_pairs={{0,1},{1,0},{2,3},{3,2},{4,5},{5,4},{6,7},{7,6},{8,9},{9,8},{10,11... | collective-permute-start | bytes 786440 | tf_op jit(solution)/shard_map/ppermute | solution.py:21
  73.3 8.3 %collective-permute-start.21 = (bf16[256,512]{1,0:T(8,128)(2,1)S(1)}, bf16[256,512]{1,0:T(8,128)(2,1)S(1)}, u32[]{:S(2)}, u32[]{:S(2)}) collective-permute-start(bf16[256,512]{1,0:T(8,128)(2,1)S(1)} %constant_dynamic-update-slice_fusion.refs_0_), channel_id=1, source_target_pairs={{0,2},{1,3},{2,0},{3,1},{4,6},{5,7},{6,4},{7,5},{8,10},{9,11},{10,... | collective-permute-start | bytes 786440 | tf_op jit(solution)/shard_map/ppermute | solution.py:21
  81.6 1.5 %collective-permute-start.27 = (bf16[256,512]{1,0:T(8,128)(2,1)S(1)}, bf16[256,512]{1,0:T(8,128)(2,1)S(1)}, u32[]{:S(2)}, u32[]{:S(2)}) collective-permute-start(bf16[256,512]{1,0:T(8,128)(2,1)S(1)} %collective-permute-done.21.refs_0_), channel_id=1, source_target_pairs={{0,1},{1,0},{2,3},{3,2},{4,5},{5,4},{6,7},{7,6},{8,9},{9,8},{10,11... | collective-permute-start | bytes 786440 | tf_op jit(solution)/shard_map/ppermute | solution.py:21

commit v7 on v6

--- a/solution.py
+++ b/solution.py
@@ -11,7 +11,7 @@
 BLK = 128
 CHUNKS = 2
 COST = 1 << 16
-VMEM_LIMIT = 48 * 1024 * 1024
+VMEM_ROOM = 8 * 1024 * 1024
 bf16 = jnp.bfloat16
 f32 = jnp.float32
 
@@ -61,6 +61,10 @@
     return jnp.concatenate([-m[:, width:], m[:, :width]], axis=1)
 
 
+def held(arrays):
+    return sum(x.size * x.dtype.itemsize for x in arrays)
+
+
 def call(body, out_shape, scalars, operands, specs, out_specs, scratch=(), aliases=None, steps=1):
     return pl.pallas_call(
         body,
@@ -73,7 +77,7 @@
             scratch_shapes=scratch,
         ),
         input_output_aliases=aliases or {},
-        compiler_params=pltpu.CompilerParams(vmem_limit_bytes=VMEM_LIMIT),
+        compiler_params=pltpu.CompilerParams(vmem_limit_bytes=VMEM_ROOM + held(operands)),
         cost_estimate=pl.CostEstimate(flops=0, bytes_accessed=COST, transcendentals=0),
     )(scalars, *operands)
 
@@ -86,7 +90,7 @@
         + [pl.BlockSpec(memory_space=pltpu.VMEM)] * len(operands),
         out_specs=jax.tree.map(lambda _: pl.BlockSpec(memory_space=pltpu.VMEM), out_shape),
         scratch_shapes=scratch,
-        compiler_params=pltpu.CompilerParams(vmem_limit_bytes=VMEM_LIMIT),
+        compiler_params=pltpu.CompilerParams(vmem_limit_bytes=VMEM_ROOM + held(operands)),
         cost_estimate=pl.CostEstimate(flops=0, bytes_accessed=COST, transcendentals=0),
     )(scalars, *operands)
 

time: 85 us -> 85 us (level)
  no operation moved by 1% of the time
where the time goes in v7:
time: 85 us; the launch traced here: 84.8 us
  waiting for transfers between devices  30.8 us (36%)
  starting transfers between devices  28.4 us (33%)
  Pallas kernels  16.4 us (19%)
  local copies, waits for them, and re-layouts  6.05 us (7%)
  other arithmetic  2.33 us (3%)
    ppermute x28, waiting for transfers between devices, swap(): return lax.ppermute(x, axis, [(i, i ^ distance) for i in range(size)])  30.8 us
    ppermute x28, starting transfers between devices, swap(): return lax.ppermute(x, axis, [(i, i ^ distance) for i in range(size)])  28.4 us
    pallas_call x4, Pallas kernels, call_here(): pl.pallas_call(body, out_shape=out_shape, in_specs=[pl.BlockSpec(memory_s...  10.6 us
    pallas_call x3, Pallas kernels, call(): pl.pallas_call(body, out_shape=out_shape, grid_spec=pltpu.PrefetchScalarG...  5.77 us
    unnamed x9, local copies, waits for them, and re-layouts  3.74 us
  transfers between devices with their start and end apart: 28, of which 13 were waited for; matrix products, arithmetic and copies ran while one was open for 8% of the time, Pallas kernels for 17%

profile of v7, /device:TPU:0, one launch (start us, length us, event | category | flops | bytes accessed | tf_op | source)
XLA Modules:
  0.0 84.8 jit_solution(1691025479651766238)
XLA Ops:
  0.6 0.0 copy-start
  0.6 3.0 %collective-permute-start.5 = (bf16[2,512,512]{2,1,0:T(8,128)(2,1)}, bf16[2,512,512]{2,1,0:T(8,128)(2,1)}, u32[]{:S(2)}, u32[]{:S(2)}) collective-permute-start(bf16[2,512,512]{2,1,0:T(8,128)(2,1)} %refs_0_.1), channel_id=1, source_target_pairs={{0,2},{1,3},{2,0},{3,1},{4,6},{5,7},{6,4},{7,5},{8,10},{9,11},{10,... | collective-permute-start | bytes 3145736 | tf_op jit(solution)/shard_map/ppermute | solution.py:21
  3.6 0.7 fusion
  4.3 0.4 constant_dynamic-slice_fusion.2
  4.7 0.4 fusion.1
  5.1 0.1 copy_bitcast_fusion
  5.2 0.1 broadcast_bitcast_fusion
  5.2 0.8 broadcast_multiply_fusion
  6.1 2.6 %collective-permute-start.2 = (bf16[512,256]{1,0:T(8,128)(2,1)}, bf16[512,256]{1,0:T(8,128)(2,1)}, u32[]{:S(2)}, u32[]{:S(2)}) collective-permute-start(bf16[512,256]{1,0:T(8,128)(2,1)} %get-tuple-element.59.refs_4_), channel_id=1, source_target_pairs={{0,8},{4,12},{8,0},{12,4},{1,9},{5,13},{9,1},{13,5},{2,10},{6,14},... | collective-permute-start | bytes 786440 | tf_op jit(solution)/shard_map/ppermute | solution.py:21
  8.7 1.6 %collective-permute-start.1 = (bf16[512,256]{1,0:T(8,128)(2,1)}, bf16[512,256]{1,0:T(8,128)(2,1)}, u32[]{:S(2)}, u32[]{:S(2)}) collective-permute-start(bf16[512,256]{1,0:T(8,128)(2,1)} %get-tuple-element.59.refs_4_), channel_id=1, source_target_pairs={{0,4},{4,0},{8,12},{12,8},{1,5},{5,1},{9,13},{13,9},{2,6},{6,2},{1... | collective-permute-start | bytes 786440 | tf_op jit(solution)/shard_map/ppermute | solution.py:21
  10.2 0.4 collective-permute-start.3
  10.7 0.3 collective-permute-start.4
  11.0 0.7 constant_dynamic-slice_fusion
  11.8 2.5 %copy.9 = bf16[512,2,512]{0,2,1:T(8,128)(2,1)} copy(bf16[512,2,512]{2,1,0:T(2,128)(2,1)S(1)} %constant_dynamic-slice_fusion) | data formatting | bytes 2097152
  14.2 1.3 %multiply_bitcast_fusion.side_ref = bf16[2,512,512]{2,1,0:T(8,128)(2,1)S(1)} fusion(bf16[512,2,512]{0,2,1:T(8,128)(2,1)} %copy.9, bf16[512]{0:T(512)(128)(2,1)S(1)} %broadcast_bitcast_fusion), kind=kLoop, calls=%fused_computation | loop fusion | flops 524288 | bytes 2098176 | tf_op jit(solution)/shard_map/transpose | solution.py:301
  15.5 6.4 %collective-permute-done.2.refs_6_ = bf16[512,256]{1,0:T(8,128)(2,1)} collective-permute-done((bf16[512,256]{1,0:T(8,128)(2,1)}, bf16[512,256]{1,0:T(8,128)(2,1)}, u32[]{:S(2)}, u32[]{:S(2)}) %collective-permute-start.2) | collective-permute-done | bytes 262176 | tf_op jit(solution)/shard_map/ppermute | solution.py:21
  21.9 6.4 %collective-permute-done.1.refs_5_ = bf16[512,256]{1,0:T(8,128)(2,1)} collective-permute-done((bf16[512,256]{1,0:T(8,128)(2,1)}, bf16[512,256]{1,0:T(8,128)(2,1)}, u32[]{:S(2)}, u32[]{:S(2)}) %collective-permute-start.1) | collective-permute-done | bytes 262176 | tf_op jit(solution)/shard_map/ppermute | solution.py:21
  28.4 3.9 %collective-permute-done.3.refs_8_ = bf16[512,256]{1,0:T(8,128)(2,1)} collective-permute-done((bf16[512,256]{1,0:T(8,128)(2,1)S(1)}, bf16[512,256]{1,0:T(8,128)(2,1)}, u32[]{:S(2)}, u32[]{:S(2)}) %collective-permute-start.3) | collective-permute-done | bytes 262176 | tf_op jit(solution)/shard_map/ppermute | solution.py:21
  32.2 0.0 collective-permute-start.6
  32.2 1.3 %collective-permute-start.7 = (bf16[512,256]{1,0:T(8,128)(2,1)}, bf16[512,256]{1,0:T(8,128)(2,1)}, u32[]{:S(2)}, u32[]{:S(2)}) collective-permute-start(bf16[512,256]{1,0:T(8,128)(2,1)} %collective-permute-done.2.refs_6_), channel_id=1, source_target_pairs={{0,4},{4,0},{8,12},{12,8},{1,5},{5,1},{9,13},{13,9},{2,6},{6,2},{1... | collective-permute-start | bytes 786440 | tf_op jit(solution)/shard_map/ppermute | solution.py:21
  33.5 0.8 collective-permute-start.11
  34.3 0.1 pad_add_fusion.ids_ref
  34.4 0.0 collective-permute-done.refs_1_
  34.4 0.8 collective-permute-done.6.refs_3_
  35.2 1.2 %copy-done.2 = bf16[2,512,512]{2,1,0:T(8,128)(2,1)S(1)} copy-done((bf16[2,512,512]{2,1,0:T(8,128)(2,1)S(1)}, bf16[2,512,512]{2,1,0:T(8,128)(2,1)}, u32[]{:S(2)}) %copy-start.2) | copy-done | bytes 1048600
  36.4 4.6 %shard_map.59 = (f32[512,256]{1,0:T(8,128)S(1)}, f32[512,256]{1,0:T(8,128)S(1)}, bf16[2,512,512]{2,1,0:T(8,128)(2,1)S(1)}) custom-call(s32[3]{0:T(128)S(1)} %pad_add_fusion.ids_ref, bf16[2,512,512]{2,1,0:T(8,128)(2,1)S(1)} %copy-done.2, bf16[2,512,512]{2,1,0:T(8,128)(2,1)} %collective-permute-done.refs_1_, ...), custom_call_target="tpu_custom_call" | custom-call | bytes 65536 | tf_op jit(solution)/shard_map/pallas_call | solution.py:86
  41.1 0.6 collective-permute-done.7.m_ref
  41.7 2.0 %shard_map.60 = (f32[128,256]{1,0:T(8,128)S(1)}, bf16[128,256]{1,0:T(8,128)(2,1)S(1)}, bf16[128,256]{1,0:T(8,128)(2,1)S(1)}, bf16[128,256]{1,0:T(8,128)(2,1)S(1)}, f32[512,256]{1,0:T(8,128)S(1)}) custom-call(s32[3]{0:T(128)S(1)} %pad_add_fusion.ids_ref, bf16[2,512,512]{2,1,0:T(8,128)(2,1)S(1)} %get-tuple-element.65.left_ref, ...), custom_call_target="tpu_custom_call" | custom-call | bytes 65536 | tf_op jit(solution)/shard_map/pallas_call | solution.py:86
  43.7 2.5 %collective-permute-start.10 = (bf16[128,256]{1,0:T(8,128)(2,1)S(1)}, bf16[128,256]{1,0:T(8,128)(2,1)S(1)}, u32[]{:S(2)}, u32[]{:S(2)}) collective-permute-start(bf16[128,256]{1,0:T(8,128)(2,1)S(1)} %get-tuple-element.71), channel_id=1, source_target_pairs={{0,12},{4,8},{8,4},{12,0},{1,13},{5,9},{9,5},{13,1},{2,14},{6,10},... | collective-permute-start | bytes 196616 | tf_op jit(solution)/shard_map/ppermute | solution.py:21
  46.2 0.4 collective-permute-start.8
  46.6 1.6 %collective-permute-start.9 = (bf16[128,256]{1,0:T(8,128)(2,1)S(1)}, bf16[128,256]{1,0:T(8,128)(2,1)S(1)}, u32[]{:S(2)}, u32[]{:S(2)}) collective-permute-start(bf16[128,256]{1,0:T(8,128)(2,1)S(1)} %get-tuple-element.70), channel_id=1, source_target_pairs={{0,8},{4,12},{8,0},{12,4},{1,9},{5,13},{9,1},{13,5},{2,10},{6,14},... | collective-permute-start | bytes 196616 | tf_op jit(solution)/shard_map/ppermute | solution.py:21
  48.2 1.8 %shard_map.61 = (f32[128,256]{1,0:T(8,128)S(1)}, bf16[128,256]{1,0:T(8,128)(2,1)S(1)}, bf16[128,256]{1,0:T(8,128)(2,1)S(1)}, bf16[128,256]{1,0:T(8,128)(2,1)S(1)...) custom-call(s32[3]{0:T(128)S(1)} %pad_add_fusion.ids_ref, bf16[2,512,512]{2,1,0:T(8,128)(2,1)S(1)} %get-tuple-element.65.left_ref, ...), custom_call_target="tpu_custom_call" | custom-call | bytes 65536 | tf_op jit(solution)/shard_map/pallas_call | solution.py:86
  50.0 1.2 %collective-permute-start.15 = (bf16[256,512]{1,0:T(8,128)(2,1)S(1)}, bf16[256,512]{1,0:T(8,128)(2,1)S(1)}, u32[]{:S(2)}, u32[]{:S(2)}) collective-permute-start(bf16[256,512]{1,0:T(8,128)(2,1)S(1)} %get-tuple-element.83), channel_id=1, source_target_pairs={{0,2},{1,3},{2,0},{3,1},{4,6},{5,7},{6,4},{7,5},{8,10},{9,11},{10,... | collective-permute-start | bytes 786440 | tf_op jit(solution)/shard_map/ppermute | solution.py:21
  51.2 0.3 collective-permute-start.12
  51.5 0.0 collective-permute-done.10
  51.5 2.7 %collective-permute-start.13 = (bf16[128,256]{1,0:T(8,128)(2,1)S(1)}, bf16[128,256]{1,0:T(8,128)(2,1)S(1)}, u32[]{:S(2)}, u32[]{:S(2)}) collective-permute-start(bf16[128,256]{1,0:T(8,128)(2,1)S(1)} %get-tuple-element.80), channel_id=1, source_target_pairs={{0,8},{4,12},{8,0},{12,4},{1,9},{5,13},{9,1},{13,5},{2,10},{6,14},... | collective-permute-start | bytes 196616 | tf_op jit(solution)/shard_map/ppermute | solution.py:21
  54.2 0.0 collective-permute-done.8
  54.2 1.4 %collective-permute-start.14 = (bf16[128,256]{1,0:T(8,128)(2,1)S(1)}, bf16[128,256]{1,0:T(8,128)(2,1)S(1)}, u32[]{:S(2)}, u32[]{:S(2)}) collective-permute-start(bf16[128,256]{1,0:T(8,128)(2,1)S(1)} %get-tuple-element.81), channel_id=1, source_target_pairs={{0,12},{4,8},{8,4},{12,0},{1,13},{5,9},{9,5},{13,1},{2,14},{6,10},... | collective-permute-start | bytes 196616 | tf_op jit(solution)/shard_map/ppermute | solution.py:21
  55.6 0.0 collective-permute-done.9
  55.6 0.0 collective-permute-done.12
  55.6 2.5 %collective-permute-done.13 = bf16[128,256]{1,0:T(8,128)(2,1)S(1)} collective-permute-done((bf16[128,256]{1,0:T(8,128)(2,1)S(1)}, bf16[128,256]{1,0:T(8,128)(2,1)S(1)}, u32[]{:S(2)}, u32[]{:S(2)}) %collective-permute-start.13) | collective-permute-done | bytes 65568 | tf_op jit(solution)/shard_map/ppermute | solution.py:21
  58.1 2.2 %collective-permute-done.14 = bf16[128,256]{1,0:T(8,128)(2,1)S(1)} collective-permute-done((bf16[128,256]{1,0:T(8,128)(2,1)S(1)}, bf16[128,256]{1,0:T(8,128)(2,1)S(1)}, u32[]{:S(2)}, u32[]{:S(2)}) %collective-permute-start.14) | collective-permute-done | bytes 65568 | tf_op jit(solution)/shard_map/ppermute | solution.py:21
  60.4 0.1 collective-permute-start.19
  60.5 2.0 %collective-permute-start.16 = (bf16[128,512]{1,0:T(8,128)(2,1)S(1)}, bf16[128,512]{1,0:T(8,128)(2,1)S(1)}, u32[]{:S(2)}, u32[]{:S(2)}) collective-permute-start(bf16[128,512]{1,0:T(8,128)(2,1)S(1)} %pad_maximum_fusion.1), channel_id=1, source_target_pairs={{0,8},{4,12},{8,0},{12,4},{1,9},{5,13},{9,1},{13,5},{2,10},{6,14},... | collective-permute-start | bytes 393224 | tf_op jit(solution)/shard_map/ppermute | solution.py:21
  62.5 2.4 %collective-permute-start.17 = (bf16[128,512]{1,0:T(8,128)(2,1)S(1)}, bf16[128,512]{1,0:T(8,128)(2,1)S(1)}, u32[]{:S(2)}, u32[]{:S(2)}) collective-permute-start(bf16[128,512]{1,0:T(8,128)(2,1)S(1)} %pad_maximum_fusion.1), channel_id=1, source_target_pairs={{0,12},{4,8},{8,4},{12,0},{1,13},{5,9},{9,5},{13,1},{2,14},{6,10},... | collective-permute-start | bytes 393224 | tf_op jit(solution)/shard_map/ppermute | solution.py:21
  64.9 0.9 %collective-permute-start.18 = (bf16[128,512]{1,0:T(8,128)(2,1)S(1)}, bf16[128,512]{1,0:T(8,128)(2,1)S(1)}, u32[]{:S(2)}, u32[]{:S(2)}) collective-permute-start(bf16[128,512]{1,0:T(8,128)(2,1)S(1)} %pad_maximum_fusion.1), channel_id=1, source_target_pairs={{0,2},{1,3},{2,0},{3,1},{4,6},{5,7},{6,4},{7,5},{8,10},{9,11},{10,... | collective-permute-start | bytes 393224 | tf_op jit(solution)/shard_map/ppermute | solution.py:21
  65.8 1.4 %collective-permute-done.19 = bf16[128,512]{1,0:T(8,128)(2,1)S(1)} collective-permute-done((bf16[128,512]{1,0:T(8,128)(2,1)S(1)}, bf16[128,512]{1,0:T(8,128)(2,1)S(1)}, u32[]{:S(2)}, u32[]{:S(2)}) %collective-permute-start.19) | collective-permute-done | bytes 131104 | tf_op jit(solution)/shard_map/ppermute | solution.py:21
  67.1 0.9 %collective-permute-start.20 = (bf16[128,512]{1,0:T(8,128)(2,1)S(1)}, bf16[128,512]{1,0:T(8,128)(2,1)S(1)}, u32[]{:S(2)}, u32[]{:S(2)}) collective-permute-start(bf16[128,512]{1,0:T(8,128)(2,1)S(1)} %collective-permute-done.19), channel_id=1, source_target_pairs={{0,2},{1,3},{2,0},{3,1},{4,6},{5,7},{6,4},{7,5},{8,10},{9,11},{10,... | collective-permute-start | bytes 393224 | tf_op jit(solution)/shard_map/ppermute | solution.py:21
  68.0 0.1 collective-permute-start.23
  68.1 2.7 %collective-permute-done.16 = bf16[128,512]{1,0:T(8,128)(2,1)S(1)} collective-permute-done((bf16[128,512]{1,0:T(8,128)(2,1)S(1)}, bf16[128,512]{1,0:T(8,128)(2,1)S(1)}, u32[]{:S(2)}, u32[]{:S(2)}) %collective-permute-start.16) | collective-permute-done | bytes 131104 | tf_op jit(solution)/shard_map/ppermute | solution.py:21
  70.8 1.3 %collective-permute-done.20 = bf16[128,512]{1,0:T(8,128)(2,1)S(1)} collective-permute-done((bf16[128,512]{1,0:T(8,128)(2,1)S(1)}, bf16[128,512]{1,0:T(8,128)(2,1)S(1)}, u32[]{:S(2)}, u32[]{:S(2)}) %collective-permute-start.20) | collective-permute-done | bytes 131104 | tf_op jit(solution)/shard_map/ppermute | solution.py:21
  72.1 0.6 collective-permute-start.24
  72.7 0.1 collective-permute-start.22
  72.8 0.5 collective-permute-start.26
  73.3 0.0 collective-permute-done.23.refs_1_
  73.3 0.9 %collective-permute-start.21 = (bf16[256,512]{1,0:T(8,128)(2,1)S(1)}, bf16[256,512]{1,0:T(8,128)(2,1)S(1)}, u32[]{:S(2)}, u32[]{:S(2)}) collective-permute-start(bf16[256,512]{1,0:T(8,128)(2,1)S(1)} %constant_dynamic-update-slice_fusion.refs_0_), channel_id=1, source_target_pairs={{0,2},{1,3},{2,0},{3,1},{4,6},{5,7},{6,4},{7,5},{8,10},{9,11},{10,... | collective-permute-start | bytes 786440 | tf_op jit(solution)/shard_map/ppermute | solution.py:21
  74.2 0.2 collective-permute-done.24.refs_3_
  74.4 2.5 %shard_map.62.refs_2_ = f32[2,2,512,512]{3,2,1,0:T(8,128)} custom-call(s32[3]{0:T(128)S(1)} %pad_add_fusion.ids_ref, f32[2,2,512,512]{3,2,1,0:T(8,128)S(1)} %copy-done.1, bf16[256,512]{1,0:T(8,128)(2,1)S(1)} %pad_maximum_fusion.refs_0_, bf16[256,512]{1,0:T(8,128)(2,1)S(1)} %collective-permute-done.23.refs_1_, ...), custom_call_target="tpu_custom_call" | custom-call | bytes 65536 | tf_op jit(solution)/shard_map/pallas_call | solution.py:69
  76.9 0.0 collective-permute-done.22.refs_1_
  76.9 1.6 %shard_map.63.refs_2_ = f32[2,2,512,512]{3,2,1,0:T(8,128)} custom-call(s32[3]{0:T(128)S(1)} %pad_add_fusion.ids_ref, f32[2,2,512,512]{3,2,1,0:T(8,128)S(1)} %copy-done.1, bf16[256,512]{1,0:T(8,128)(2,1)S(1)} %constant_dynamic-update-slice_fusion.refs_0_, bf16[256,512]{1,0:T(8,128)(2,1)S(1)} %collective-permute-done.22.refs_1_, ...), custom_call_target="tpu_custom_call", output_to_operand_aliasing={{}: (4, {})} | custom-call | bytes 65536 | tf_op jit(solution)/shard_map/pallas_call | solution.py:69
  78.5 2.2 %shard_map.64 = f32[128,2,1024]{2,1,0:T(2,128)} custom-call(s32[3]{0:T(128)S(1)} %pad_add_fusion.ids_ref, f32[256,512]{1,0:T(8,128)S(1)} %get-tuple-element.99.refs_0_, bf16[256,512]{1,0:T(8,128)(2,1)S(1)} %collective-permute-done.15.refs_1_, f32[256,512]{1,0:T(8,128)S(1)} %collective-permute-done.25.refs_2_, ...), custom_call_target="tpu_custom_call" | custom-call | bytes 65536 | tf_op jit(solution)/shard_map/pallas_call | solution.py:86
  80.7 0.9 %collective-permute-done.21.refs_0_ = bf16[256,512]{1,0:T(8,128)(2,1)S(1)} collective-permute-done((bf16[256,512]{1,0:T(8,128)(2,1)S(1)}, bf16[256,512]{1,0:T(8,128)(2,1)S(1)}, u32[]{:S(2)}, u32[]{:S(2)}) %collective-permute-start.21) | collective-permute-done | bytes 262176 | tf_op jit(solution)/shard_map/ppermute | solution.py:21
  81.6 1.5 %collective-permute-done.27.refs_1_ = bf16[256,512]{1,0:T(8,128)(2,1)S(1)} collective-permute-done((bf16[256,512]{1,0:T(8,128)(2,1)S(1)}, bf16[256,512]{1,0:T(8,128)(2,1)S(1)}, u32[]{:S(2)}, u32[]{:S(2)}) %collective-permute-start.27) | collective-permute-done | bytes 262176 | tf_op jit(solution)/shard_map/ppermute | solution.py:21
  83.1 1.6 %shard_map.65 = f32[2,2,512,512]{3,2,1,0:T(8,128)} custom-call(s32[3]{0:T(128)S(1)} %pad_add_fusion.ids_ref, f32[2,2,512,512]{3,2,1,0:T(8,128)S(1)} %copy-done.1, bf16[256,512]{1,0:T(8,128)(2,1)S(1)} %collective-permute-done.21.refs_0_, bf16[256,512]{1,0:T(8,128)(2,1)S(1)} %collective-permute-done.27.refs_1_, ...), custom_call_target="tpu_custom_call", output_to_operand_aliasing={{}: (4, {})} | custom-call | bytes 65536 | tf_op jit(solution)/shard_map/pallas_call | solution.py:69
  (26 shorter events, 0.2 us)
Async XLA Ops:
  0.6 3.7 %copy-start = (bf16[512,2,1024]{2,1,0:T(2,128)(2,1)S(1)}, bf16[512,2,1024]{2,1,0:T(2,128)(2,1)}, u32[]{:S(2)}) copy-start(bf16[512,2,1024]{2,1,0:T(2,128)(2,1)} %param.5) | copy-start | bytes 6291460
  0.6 31.6 %collective-permute-start.5 = (bf16[2,512,512]{2,1,0:T(8,128)(2,1)}, bf16[2,512,512]{2,1,0:T(8,128)(2,1)}, u32[]{:S(2)}, u32[]{:S(2)}) collective-permute-start(bf16[2,512,512]{2,1,0:T(8,128)(2,1)} %refs_0_.1), channel_id=1, source_target_pairs={{0,2},{1,3},{2,0},{3,1},{4,6},{5,7},{6,4},{7,5},{8,10},{9,11},{10,... | collective-permute-start | bytes 3145736 | tf_op jit(solution)/shard_map/ppermute | solution.py:21
  6.1 15.9 %collective-permute-start.2 = (bf16[512,256]{1,0:T(8,128)(2,1)}, bf16[512,256]{1,0:T(8,128)(2,1)}, u32[]{:S(2)}, u32[]{:S(2)}) collective-permute-start(bf16[512,256]{1,0:T(8,128)(2,1)} %get-tuple-element.59.refs_4_), channel_id=1, source_target_pairs={{0,8},{4,12},{8,0},{12,4},{1,9},{5,13},{9,1},{13,5},{2,10},{6,14},... | collective-permute-start | bytes 786440 | tf_op jit(solution)/shard_map/ppermute | solution.py:21
  8.7 19.7 %collective-permute-start.1 = (bf16[512,256]{1,0:T(8,128)(2,1)}, bf16[512,256]{1,0:T(8,128)(2,1)}, u32[]{:S(2)}, u32[]{:S(2)}) collective-permute-start(bf16[512,256]{1,0:T(8,128)(2,1)} %get-tuple-element.59.refs_4_), channel_id=1, source_target_pairs={{0,4},{4,0},{8,12},{12,8},{1,5},{5,1},{9,13},{13,9},{2,6},{6,2},{1... | collective-permute-start | bytes 786440 | tf_op jit(solution)/shard_map/ppermute | solution.py:21
  10.2 22.0 %collective-permute-start.3 = (bf16[512,256]{1,0:T(8,128)(2,1)S(1)}, bf16[512,256]{1,0:T(8,128)(2,1)}, u32[]{:S(2)}, u32[]{:S(2)}) collective-permute-start(bf16[512,256]{1,0:T(8,128)(2,1)S(1)} %get-tuple-element.62.refs_7_), channel_id=1, source_target_pairs={{0,4},{4,0},{8,12},{12,8},{1,5},{5,1},{9,13},{13,9},{2,6},{6,2},{1... | collective-permute-start | bytes 786440 | tf_op jit(solution)/shard_map/ppermute | solution.py:21
  10.7 21.5 %collective-permute-start.4 = (bf16[512,256]{1,0:T(8,128)(2,1)S(1)}, bf16[512,256]{1,0:T(8,128)(2,1)}, u32[]{:S(2)}, u32[]{:S(2)}) collective-permute-start(bf16[512,256]{1,0:T(8,128)(2,1)S(1)} %get-tuple-element.62.refs_7_), channel_id=1, source_target_pairs={{0,8},{4,12},{8,0},{12,4},{1,9},{5,13},{9,1},{13,5},{2,10},{6,14},... | collective-permute-start | bytes 786440 | tf_op jit(solution)/shard_map/ppermute | solution.py:21
  21.9 12.5 %collective-permute-start = (bf16[2,512,512]{2,1,0:T(8,128)(2,1)}, bf16[2,512,512]{2,1,0:T(8,128)(2,1)}, u32[]{:S(2)}, u32[]{:S(2)}) collective-permute-start(bf16[2,512,512]{2,1,0:T(8,128)(2,1)} %refs_0_.1), channel_id=1, source_target_pairs={{0,1},{1,0},{2,3},{3,2},{4,5},{5,4},{6,7},{7,6},{8,9},{9,8},{10,11... | collective-permute-start | bytes 3145736 | tf_op jit(solution)/shard_map/ppermute | solution.py:21
  32.2 3.0 %collective-permute-start.6 = (bf16[2,512,512]{2,1,0:T(8,128)(2,1)}, bf16[2,512,512]{2,1,0:T(8,128)(2,1)}, u32[]{:S(2)}, u32[]{:S(2)}) collective-permute-start(bf16[2,512,512]{2,1,0:T(8,128)(2,1)} %collective-permute-done.5.refs_2_), channel_id=1, source_target_pairs={{0,1},{1,0},{2,3},{3,2},{4,5},{5,4},{6,7},{7,6},{8,9},{9,8},{10,11... | collective-permute-start | bytes 3145736 | tf_op jit(solution)/shard_map/ppermute | solution.py:21
  32.2 9.5 %collective-permute-start.7 = (bf16[512,256]{1,0:T(8,128)(2,1)}, bf16[512,256]{1,0:T(8,128)(2,1)}, u32[]{:S(2)}, u32[]{:S(2)}) collective-permute-start(bf16[512,256]{1,0:T(8,128)(2,1)} %collective-permute-done.2.refs_6_), channel_id=1, source_target_pairs={{0,4},{4,0},{8,12},{12,8},{1,5},{5,1},{9,13},{13,9},{2,6},{6,2},{1... | collective-permute-start | bytes 786440 | tf_op jit(solution)/shard_map/ppermute | solution.py:21
  33.5 14.6 %collective-permute-start.11 = (bf16[512,256]{1,0:T(8,128)(2,1)}, bf16[512,256]{1,0:T(8,128)(2,1)}, u32[]{:S(2)}, u32[]{:S(2)}) collective-permute-start(bf16[512,256]{1,0:T(8,128)(2,1)} %collective-permute-done.4.refs_9_), channel_id=1, source_target_pairs={{0,4},{4,0},{8,12},{12,8},{1,5},{5,1},{9,13},{13,9},{2,6},{6,2},{1... | collective-permute-start | bytes 786440 | tf_op jit(solution)/shard_map/ppermute | solution.py:21
  35.2 1.2 %copy-start.2 = (bf16[2,512,512]{2,1,0:T(8,128)(2,1)S(1)}, bf16[2,512,512]{2,1,0:T(8,128)(2,1)}, u32[]{:S(2)}) copy-start(bf16[2,512,512]{2,1,0:T(8,128)(2,1)} %refs_0_.1) | copy-start | bytes 3145732
  41.7 32.7 %copy-start.1 = (f32[2,2,512,512]{3,2,1,0:T(8,128)S(1)}, f32[2,2,512,512]{3,2,1,0:T(8,128)}, u32[]{:S(2)}) copy-start(f32[2,2,512,512]{3,2,1,0:T(8,128)} %pivot_ref.5) | copy-start | bytes 12582916
  43.7 7.8 %collective-permute-start.10 = (bf16[128,256]{1,0:T(8,128)(2,1)S(1)}, bf16[128,256]{1,0:T(8,128)(2,1)S(1)}, u32[]{:S(2)}, u32[]{:S(2)}) collective-permute-start(bf16[128,256]{1,0:T(8,128)(2,1)S(1)} %get-tuple-element.71), channel_id=1, source_target_pairs={{0,12},{4,8},{8,4},{12,0},{1,13},{5,9},{9,5},{13,1},{2,14},{6,10},... | collective-permute-start | bytes 196616 | tf_op jit(solution)/shard_map/ppermute | solution.py:21
  46.2 8.0 %collective-permute-start.8 = (bf16[128,256]{1,0:T(8,128)(2,1)S(1)}, bf16[128,256]{1,0:T(8,128)(2,1)S(1)}, u32[]{:S(2)}, u32[]{:S(2)}) collective-permute-start(bf16[128,256]{1,0:T(8,128)(2,1)S(1)} %get-tuple-element.69), channel_id=1, source_target_pairs={{0,4},{4,0},{8,12},{12,8},{1,5},{5,1},{9,13},{13,9},{2,6},{6,2},{1... | collective-permute-start | bytes 196616 | tf_op jit(solution)/shard_map/ppermute | solution.py:21
  46.6 9.0 %collective-permute-start.9 = (bf16[128,256]{1,0:T(8,128)(2,1)S(1)}, bf16[128,256]{1,0:T(8,128)(2,1)S(1)}, u32[]{:S(2)}, u32[]{:S(2)}) collective-permute-start(bf16[128,256]{1,0:T(8,128)(2,1)S(1)} %get-tuple-element.70), channel_id=1, source_target_pairs={{0,8},{4,12},{8,0},{12,4},{1,9},{5,13},{9,1},{13,5},{2,10},{6,14},... | collective-permute-start | bytes 196616 | tf_op jit(solution)/shard_map/ppermute | solution.py:21
  50.0 10.3 %collective-permute-start.15 = (bf16[256,512]{1,0:T(8,128)(2,1)S(1)}, bf16[256,512]{1,0:T(8,128)(2,1)S(1)}, u32[]{:S(2)}, u32[]{:S(2)}) collective-permute-start(bf16[256,512]{1,0:T(8,128)(2,1)S(1)} %get-tuple-element.83), channel_id=1, source_target_pairs={{0,2},{1,3},{2,0},{3,1},{4,6},{5,7},{6,4},{7,5},{8,10},{9,11},{10,... | collective-permute-start | bytes 786440 | tf_op jit(solution)/shard_map/ppermute | solution.py:21
  51.2 4.4 %collective-permute-start.12 = (bf16[128,256]{1,0:T(8,128)(2,1)S(1)}, bf16[128,256]{1,0:T(8,128)(2,1)S(1)}, u32[]{:S(2)}, u32[]{:S(2)}) collective-permute-start(bf16[128,256]{1,0:T(8,128)(2,1)S(1)} %get-tuple-element.79), channel_id=1, source_target_pairs={{0,4},{4,0},{8,12},{12,8},{1,5},{5,1},{9,13},{13,9},{2,6},{6,2},{1... | collective-permute-start | bytes 196616 | tf_op jit(solution)/shard_map/ppermute | solution.py:21
  51.5 6.6 %collective-permute-start.13 = (bf16[128,256]{1,0:T(8,128)(2,1)S(1)}, bf16[128,256]{1,0:T(8,128)(2,1)S(1)}, u32[]{:S(2)}, u32[]{:S(2)}) collective-permute-start(bf16[128,256]{1,0:T(8,128)(2,1)S(1)} %get-tuple-element.80), channel_id=1, source_target_pairs={{0,8},{4,12},{8,0},{12,4},{1,9},{5,13},{9,1},{13,5},{2,10},{6,14},... | collective-permute-start | bytes 196616 | tf_op jit(solution)/shard_map/ppermute | solution.py:21
  54.2 6.1 %collective-permute-start.14 = (bf16[128,256]{1,0:T(8,128)(2,1)S(1)}, bf16[128,256]{1,0:T(8,128)(2,1)S(1)}, u32[]{:S(2)}, u32[]{:S(2)}) collective-permute-start(bf16[128,256]{1,0:T(8,128)(2,1)S(1)} %get-tuple-element.81), channel_id=1, source_target_pairs={{0,12},{4,8},{8,4},{12,0},{1,13},{5,9},{9,5},{13,1},{2,14},{6,10},... | collective-permute-start | bytes 196616 | tf_op jit(solution)/shard_map/ppermute | solution.py:21
  60.4 6.7 %collective-permute-start.19 = (bf16[128,512]{1,0:T(8,128)(2,1)S(1)}, bf16[128,512]{1,0:T(8,128)(2,1)S(1)}, u32[]{:S(2)}, u32[]{:S(2)}) collective-permute-start(bf16[128,512]{1,0:T(8,128)(2,1)S(1)} %pad_maximum_fusion.1), channel_id=1, source_target_pairs={{0,4},{4,0},{8,12},{12,8},{1,5},{5,1},{9,13},{13,9},{2,6},{6,2},{1... | collective-permute-start | bytes 393224 | tf_op jit(solution)/shard_map/ppermute | solution.py:21
  60.5 10.3 %collective-permute-start.16 = (bf16[128,512]{1,0:T(8,128)(2,1)S(1)}, bf16[128,512]{1,0:T(8,128)(2,1)S(1)}, u32[]{:S(2)}, u32[]{:S(2)}) collective-permute-start(bf16[128,512]{1,0:T(8,128)(2,1)S(1)} %pad_maximum_fusion.1), channel_id=1, source_target_pairs={{0,8},{4,12},{8,0},{12,4},{1,9},{5,13},{9,1},{13,5},{2,10},{6,14},... | collective-permute-start | bytes 393224 | tf_op jit(solution)/shard_map/ppermute | solution.py:21
  62.5 8.3 %collective-permute-start.17 = (bf16[128,512]{1,0:T(8,128)(2,1)S(1)}, bf16[128,512]{1,0:T(8,128)(2,1)S(1)}, u32[]{:S(2)}, u32[]{:S(2)}) collective-permute-start(bf16[128,512]{1,0:T(8,128)(2,1)S(1)} %pad_maximum_fusion.1), channel_id=1, source_target_pairs={{0,12},{4,8},{8,4},{12,0},{1,13},{5,9},{9,5},{13,1},{2,14},{6,10},... | collective-permute-start | bytes 393224 | tf_op jit(solution)/shard_map/ppermute | solution.py:21
  64.9 5.9 %collective-permute-start.18 = (bf16[128,512]{1,0:T(8,128)(2,1)S(1)}, bf16[128,512]{1,0:T(8,128)(2,1)S(1)}, u32[]{:S(2)}, u32[]{:S(2)}) collective-permute-start(bf16[128,512]{1,0:T(8,128)(2,1)S(1)} %pad_maximum_fusion.1), channel_id=1, source_target_pairs={{0,2},{1,3},{2,0},{3,1},{4,6},{5,7},{6,4},{7,5},{8,10},{9,11},{10,... | collective-permute-start | bytes 393224 | tf_op jit(solution)/shard_map/ppermute | solution.py:21
  67.1 5.0 %collective-permute-start.20 = (bf16[128,512]{1,0:T(8,128)(2,1)S(1)}, bf16[128,512]{1,0:T(8,128)(2,1)S(1)}, u32[]{:S(2)}, u32[]{:S(2)}) collective-permute-start(bf16[128,512]{1,0:T(8,128)(2,1)S(1)} %collective-permute-done.19), channel_id=1, source_target_pairs={{0,2},{1,3},{2,0},{3,1},{4,6},{5,7},{6,4},{7,5},{8,10},{9,11},{10,... | collective-permute-start | bytes 393224 | tf_op jit(solution)/shard_map/ppermute | solution.py:21
  68.0 5.3 %collective-permute-start.23 = (bf16[256,512]{1,0:T(8,128)(2,1)S(1)}, bf16[256,512]{1,0:T(8,128)(2,1)S(1)}, u32[]{:S(2)}, u32[]{:S(2)}) collective-permute-start(bf16[256,512]{1,0:T(8,128)(2,1)S(1)} %pad_maximum_fusion.refs_0_), channel_id=1, source_target_pairs={{0,1},{1,0},{2,3},{3,2},{4,5},{5,4},{6,7},{7,6},{8,9},{9,8},{10,11... | collective-permute-start | bytes 786440 | tf_op jit(solution)/shard_map/ppermute | solution.py:21
  72.1 6.4 %collective-permute-start.25 = (f32[256,512]{1,0:T(8,128)S(1)}, f32[256,512]{1,0:T(8,128)S(1)}, u32[]{:S(2)}, u32[]{:S(2)}) collective-permute-start(f32[256,512]{1,0:T(8,128)S(1)} %get-tuple-element.99.refs_0_), channel_id=1, source_target_pairs={{0,1},{1,0},{2,3},{3,2},{4,5},{5,4},{6,7},{7,6},{8,9},{9,8},{10,11... | collective-permute-start | bytes 1572872 | tf_op jit(solution)/shard_map/ppermute | solution.py:21
  72.1 2.2 %collective-permute-start.24 = (bf16[256,512]{1,0:T(8,128)(2,1)S(1)}, bf16[256,512]{1,0:T(8,128)(2,1)S(1)}, u32[]{:S(2)}, u32[]{:S(2)}) collective-permute-start(bf16[256,512]{1,0:T(8,128)(2,1)S(1)} %constant_dynamic-update-slice_fusion.2.refs_2_), channel_id=1, source_target_pairs={{0,1},{1,0},{2,3},{3,2},{4,5},{5,4},{6,7},{7,6},{8,9},{9,8},{10,11... | collective-permute-start | bytes 786440 | tf_op jit(solution)/shard_map/ppermute | solution.py:21
  72.7 4.2 %collective-permute-start.22 = (bf16[256,512]{1,0:T(8,128)(2,1)S(1)}, bf16[256,512]{1,0:T(8,128)(2,1)S(1)}, u32[]{:S(2)}, u32[]{:S(2)}) collective-permute-start(bf16[256,512]{1,0:T(8,128)(2,1)S(1)} %constant_dynamic-update-slice_fusion.refs_0_), channel_id=1, source_target_pairs={{0,1},{1,0},{2,3},{3,2},{4,5},{5,4},{6,7},{7,6},{8,9},{9,8},{10,11... | collective-permute-start | bytes 786440 | tf_op jit(solution)/shard_map/ppermute | solution.py:21
  72.8 5.7 %collective-permute-start.26 = (bf16[256,512]{1,0:T(8,128)(2,1)S(1)}, bf16[256,512]{1,0:T(8,128)(2,1)S(1)}, u32[]{:S(2)}, u32[]{:S(2)}) collective-permute-start(bf16[256,512]{1,0:T(8,128)(2,1)S(1)} %collective-permute-done.15.refs_1_), channel_id=1, source_target_pairs={{0,1},{1,0},{2,3},{3,2},{4,5},{5,4},{6,7},{7,6},{8,9},{9,8},{10,11... | collective-permute-start | bytes 786440 | tf_op jit(solution)/shard_map/ppermute | solution.py:21
  73.3 8.3 %collective-permute-start.21 = (bf16[256,512]{1,0:T(8,128)(2,1)S(1)}, bf16[256,512]{1,0:T(8,128)(2,1)S(1)}, u32[]{:S(2)}, u32[]{:S(2)}) collective-permute-start(bf16[256,512]{1,0:T(8,128)(2,1)S(1)} %constant_dynamic-update-slice_fusion.refs_0_), channel_id=1, source_target_pairs={{0,2},{1,3},{2,0},{3,1},{4,6},{5,7},{6,4},{7,5},{8,10},{9,11},{10,... | collective-permute-start | bytes 786440 | tf_op jit(solution)/shard_map/ppermute | solution.py:21
  81.6 1.5 %collective-permute-start.27 = (bf16[256,512]{1,0:T(8,128)(2,1)S(1)}, bf16[256,512]{1,0:T(8,128)(2,1)S(1)}, u32[]{:S(2)}, u32[]{:S(2)}) collective-permute-start(bf16[256,512]{1,0:T(8,128)(2,1)S(1)} %collective-permute-done.21.refs_0_), channel_id=1, source_target_pairs={{0,1},{1,0},{2,3},{3,2},{4,5},{5,4},{6,7},{7,6},{8,9},{9,8},{10,11... | collective-permute-start | bytes 786440 | tf_op jit(solution)/shard_map/ppermute | solution.py:21
